TPU v7x, 256 devices: a whole 4x4x8 slice. The times are simulated.
256 devices in a mesh: half: 2 (over x_lo), row: 16 (over z, core), col: 8 (over y, x_hi).
Axes of the slice: x: 4 (x_hi: 2, x_lo: 2; x = x_hi * 2 + x_lo), y: 4, z: 8, core: 2. Of those that a mesh axis runs over, the one named last changes fastest.
Arguments:
- child_update: float32 [2, 16384, 1024], P('half', ('row', 'col')), may hold values from -4 to 4
- parent_front: float32 [32768, 4096], P(('row', 'col'), 'half'), may hold values from -4 to 192, as said below
- row_map: int32 [2, 128], P(None, ('row', 'col')), may hold values from 0 to 255, as said below
- col_map: int32 [2, 8], replicated, may hold values from 0 to 31, as said below
Outputs:
- factored: float32 [32768, 4096], P('row', ('half', 'col'))
Inputs may be any that keep to these rules, and one draw needn't show every extreme that they name: parent_front's diagonal entries lie between 96 and 192. `row_map`: the blocks of the k-th run of 1024 update matrix rows name distinct parent blocks of the k-th run of 2048 parent rows, in no fixed order. `col_map`: each row holds distinct increasing block numbers.
All inputs are finite; a program needn't handle non-finite values.
Results may differ from a plain program's by a relative error of at most 0.000075.
Values sent between devices are 32-bit elements; how exact they have to be, the bound alone decides.
No kernel may reach another device: no remote copies, remote signals or barrier semaphores. Data moves between devices by JAX's collectives and lax.ppermute only.
A program may use at most 128 MiB of HBM per device.

v0:
```python
import jax
import jax.numpy as jnp
from jax import lax
from jax.sharding import PartitionSpec as P

BLK = 128
NB = 1024
W = 4096


HIGHEST = lax.Precision.HIGHEST


def place_rows(child_rows, block_list, column_blocks, shard_index, prow, block_count):
    parent_per = prow // BLK
    local_blocks = block_list - shard_index * parent_per
    row_select = (jnp.arange(parent_per, dtype=jnp.int32)[:, None] == local_blocks[None, :]).astype(
        jnp.float32
    )
    targets = jnp.arange(block_count, dtype=jnp.int32)
    col_select = (column_blocks[:, None] == targets[None, :]).astype(jnp.float32)
    child_blocks = child_rows.reshape(block_list.shape[0], BLK, column_blocks.shape[0], BLK)
    placed = jnp.einsum("pk,kbjl,jw->pbwl", row_select, child_blocks, col_select, precision=HIGHEST)
    return placed.reshape(prow, block_count * BLK)


def body(child_update, parent_front, row_map, col_map):
    half_index = lax.axis_index("half")
    shard_index = lax.axis_index("row") * lax.axis_size("col") + lax.axis_index("col")
    prow, half_width = parent_front.shape
    wblocks = W // BLK
    own_columns = lax.dynamic_index_in_dim(col_map, half_index, 0, keepdims=False)
    own_blocks = lax.dynamic_index_in_dim(row_map, half_index, 0, keepdims=False)
    contribution = place_rows(
        lax.all_gather(child_update[0], "col", axis=0, tiled=True),
        lax.all_gather(own_blocks, "col", axis=0, tiled=True),
        own_columns,
        shard_index,
        prow,
        wblocks,
    )
    summed = lax.psum_scatter(contribution, "half", scatter_dimension=1, tiled=True)
    front_slab = parent_front + summed
    first_row = shard_index * prow
    panel_source = front_slab[:, :NB] * (half_index == 0).astype(jnp.float32)
    diag_buffer = jnp.zeros((NB + prow, NB), jnp.float32)
    diag_buffer = lax.dynamic_update_slice(
        diag_buffer, panel_source, (jnp.minimum(first_row, NB), 0)
    )
    diag_block = lax.psum(diag_buffer[:NB], ("row", "col"))
    lower_factor = jnp.linalg.cholesky(diag_block)
    solved = lax.linalg.triangular_solve(
        lower_factor, front_slab[:, :NB], left_side=False, lower=True, transpose_a=True
    )
    padded_factor = jnp.concatenate([lower_factor, jnp.zeros((prow, NB), jnp.float32)], 0)
    top_rows = lax.dynamic_slice_in_dim(padded_factor, jnp.minimum(first_row, NB), prow, 0)
    row_global = first_row + jnp.arange(prow, dtype=jnp.int32)
    own_panel = jnp.where(row_global[:, None] < NB, top_rows, solved)
    panel_term = jnp.where(half_index == 0, own_panel, 0.0)
    panel_rows = lax.psum(panel_term, "half")
    replaced = jnp.concatenate([panel_rows, front_slab[:, NB:]], 1)
    front_slab = jnp.where(half_index == 0, replaced, front_slab)
    grid_block = lax.all_to_all(front_slab, "col", split_axis=1, concat_axis=0, tiled=True)
    group_panel = lax.all_gather(panel_rows, "col", axis=0, tiled=True)
    group_rows = group_panel.shape[0]
    col_width = grid_block.shape[1]
    col_block = half_index * lax.axis_size("col") + lax.axis_index("col")
    offset_rows = col_block * col_width - lax.axis_index("row") * group_rows
    padded_panel = jnp.concatenate(
        [
            jnp.zeros((col_width, NB), jnp.float32),
            group_panel,
            jnp.zeros((col_width, NB), jnp.float32),
        ],
        0,
    )
    start_row = jnp.clip(offset_rows + col_width, 0, group_rows + col_width)
    column_piece = lax.dynamic_slice_in_dim(padded_panel, start_row, col_width, 0)
    wanted = offset_rows + jnp.arange(col_width, dtype=jnp.int32)
    inside = (wanted >= 0) & (wanted < group_rows)
    column_piece = jnp.where(inside[:, None], column_piece, 0.0)
    column_rows = lax.psum(column_piece, "row")
    product = jnp.dot(group_panel, column_rows.T, precision=HIGHEST)
    col_global = col_block * col_width + jnp.arange(col_width, dtype=jnp.int32)
    return jnp.where(col_global[None, :] >= NB, grid_block - product, grid_block)


def solution(mesh):
    return jax.shard_map(
        body,
        mesh=mesh,
        in_specs=(
            P("half", ("row", "col"), None),
            P(("row", "col"), "half"),
            P(None, ("row", "col")),
            P(),
        ),
        out_specs=P("row", ("half", "col")),
        check_vma=False,
    )
```

profile of v0, /device:TPU:2, one launch (start us, length us, event | category | flops | bytes accessed | tf_op | source)
XLA Modules:
  0.0 2141.8 jit_solution(2375566628960902986)
XLA Ops:
  10.0 13.4 all-reduce.2
  23.5 65.0 %all-gather.7.cloned.1.call-done = f32[1,1024,1024]{2,1,0:T(8,128)} async-done(((f32[1,128,1024]{2,1,0:T(8,128)}), f32[1,1024,1024]{2,1,0:T(8,128)}) %all-gather.7.cloned.1.call-update) | async-done | bytes 4194320 | tf_op jit(solution)/shard_map/all_gather | solution.py:35
  88.5 3.2 copy.36
  91.7 4.3 fusion.1
  96.0 3.9 convolution_bitcast_fusion
  99.9 5.3 copy.5
  105.2 4.4 copy.45
  113.1 53.8 %reduce-scatter.2.cloned.1.call-done = f32[256,2048]{0,1:T(8,128)} async-done(((f32[256,4096]{0,1:T(8,128)}), f32[256,2048]{0,1:T(8,128)}) %reduce-scatter.2.cloned.1.call-update) | async-done | bytes 2097168 | tf_op jit(solution)/shard_map/reduce_scatter | solution.py:42
  166.9 2.5 add.146
  170.5 2.7 broadcast_in_dim.42
  173.1 5.9 dynamic_update_slice.3
  179.0 4.8 slice.256
  183.9 1287.5 %all-reduce.7.cloned.1.call-done = f32[1024,1024]{0,1:T(8,128)} async-done(((f32[1024,1024]{0,1:T(8,128)}), f32[1024,1024]{0,1:T(8,128)}) %all-reduce.7.cloned.1.call-update) | async-done | bytes 4194320 | tf_op jit(solution)/shard_map/psum | solution.py:50
  1471.5 5.8 copy.7
  1477.2 4.4 fusion
  1483.6 11.7 cholesky.223
  1495.5 9.8 custom-call.62
  1508.6 11.7 cholesky.244
  1520.6 2.5 cholesky.255
  1523.1 9.8 custom-call.63
  1535.8 2.7 convolution_subtract_fusion.1
  1538.5 11.7 cholesky.468
  1551.0 9.8 custom-call.64
  1562.0 3.3 convolution_subtract_fusion.2
  1565.4 11.7 cholesky.487
  1577.8 9.8 custom-call.65
  1588.8 3.2 convolution_subtract_fusion.3
  1592.0 12.1 cholesky.506
  1604.8 9.8 custom-call.66
  1615.8 3.2 convolution_subtract_fusion.4
  1619.0 11.7 cholesky.526
  1631.5 9.8 custom-call.67
  1642.3 2.9 convolution_subtract_fusion.11
  1645.2 11.7 cholesky.546
  1657.7 9.8 custom-call.68
  1668.4 2.2 convolution_subtract_fusion.13
  1670.7 11.7 cholesky.564
  1692.9 4.4 fusion.3
  1697.3 28.3 %while.1 = (s32[]{:T(128)}, f32[1024,1024]{0,1:T(8,128)}, s32[8,2]{0,1:T(2,128)S(1)}, f32[8,128,128]{2,1,0:T(8,128)}, s32[]{:T(128)}) while((s32[]{:T(128)}, f32[1024,1024]{0,1:T(8,128)}, s32[8,2]{0,1:T(2,128)S(1)}, f32[8,128,128]{2,1,0:T(8,128)}, s32[]{:T(128)}) %tuple.52), condition=%wide.while_cond, body=%wide.while_body.sunk | while | flops 2 | bytes 393329 | solution.py:52
  1698.1 2.2 dynamic-slice.8
  1712.1 2.2 dynamic-slice.8
  1725.6 79.4 %custom-call.69 = f32[8,128,128]{1,2,0:T(8,128)S(1)} custom-call(f32[8,128,128]{2,1,0:T(8,128)} %get-tuple-element.12), custom_call_target="InvertDiagBlocksLowerTriangular" | custom-call | tf_op jit(solution)/shard_map/triangular_solve | solution.py:52
  1820.2 48.4 %all-reduce.9.cloned.1.call-done = f32[256,1024]{0,1:T(8,128)} async-done(((f32[256,1024]{0,1:T(8,128)}), f32[256,1024]{0,1:T(8,128)}) %all-reduce.9.cloned.1.call-update) | async-done | bytes 1048592 | tf_op jit(solution)/shard_map/psum | solution.py:60
  1868.6 2.8 maximum_select_fusion
  1871.4 6.3 all-to-all-start
  1877.9 126.1 %all-gather.5.cloned.1.call-done = f32[2048,1024]{0,1:T(8,128)} async-done(((f32[256,1024]{0,1:T(8,128)}), f32[2048,1024]{0,1:T(8,128)}) %all-gather.5.cloned.1.call-update) | async-done | bytes 8388624 | tf_op jit(solution)/shard_map/all_gather | solution.py:64
  2008.1 109.3 %all-reduce.11.cloned.1.call-done = f32[256,1024]{0,1:T(8,128)} async-done(((f32[256,1024]{0,1:T(8,128)}), f32[256,1024]{0,1:T(8,128)}) %all-reduce.11.cloned.1.call-update) | async-done | bytes 1048592 | tf_op jit(solution)/shard_map/psum | solution.py:82
  2117.4 17.1 subtract_select_fusion
  (142 shorter events, 74.1 us)
Async XLA Ops:
  6.5 16.9 copy-start
  6.5 82.0 %all-gather.7.cloned.1.call-start = ((), (), s32[]{:S(2)}) async-start(), calls=%async_computation.7 | async-start | bytes 4718592 | tf_op jit(solution)/shard_map/all_gather | solution.py:35
  7.3 159.6 %reduce-scatter.2.cloned.1.call-start = ((), (), s32[]{:S(2)}) async-start(), calls=%async_computation.2 | async-start | bytes 6291456 | tf_op jit(solution)/shard_map/reduce_scatter | solution.py:42
  109.7 1.6 copy-start.5
  109.7 1361.8 %all-reduce.7.cloned.1.call-start = ((), (), s32[]{:S(2)}) async-start(), calls=%async_computation.3 | async-start | bytes 8388608 | tf_op jit(solution)/shard_map/psum | solution.py:50
  183.8 1684.8 %all-reduce.9.cloned.1.call-start = ((), (), s32[]{:S(2)}) async-start(), calls=%async_computation.4 | async-start | bytes 2097152 | tf_op jit(solution)/shard_map/psum | solution.py:60
  1481.7 1.9 copy-start.3
  1809.9 8.9 copy-start.2
  1818.8 49.9 %copy-start.4 = (f32[256,1024]{0,1:T(8,128)S(1)}, f32[256,1024]{0,1:T(8,128)}, u32[]{:S(2)}) copy-start(f32[256,1024]{0,1:T(8,128)} %get-tuple-element.30) | copy-start | bytes 3145732
  1820.2 183.8 %all-gather.5.cloned.1.call-start = ((), (), s32[]{:S(2)}) async-start(), calls=%async_computation.5 | async-start | bytes 9437184 | tf_op jit(solution)/shard_map/all_gather | solution.py:64
  1871.4 134.6 %all-to-all-start = ((f32[256,8,256]{0,2,1:T(8,128)}), f32[256,8,256]{0,2,1:T(8,128)S(1)}, u32[]{:S(2)}, u32[]{:S(2)}) async-start(f32[256,8,256]{0,2,1:T(8,128)} %bitcast.139), calls=%async_computation.1 | async-start | bytes 4194304 | tf_op jit(solution)/shard_map/all_to_all | solution.py:63
  1877.8 239.6 %all-reduce.11.cloned.1.call-start = ((), (), s32[]{:S(2)}) async-start(), calls=%async_computation.6 | async-start | bytes 2097152 | tf_op jit(solution)/shard_map/psum | solution.py:82
  2117.4 17.2 copy-start.1
Sparse Core Ops, SparseCore 0:
  10.0 78.4 all-gather.6
  109.8 57.0 reduce-scatter.1
  184.0 1287.4 all-reduce.6
  1820.3 48.2 all-reduce.8
  1871.2 132.7 all-gather.4
  2006.3 111.0 all-reduce.10
where the time goes:
time: 2150 us; the launch traced here: 2140 us
  waiting for transfers between devices  1690 us (79%)
  other arithmetic  266 us (12%)
  local copies, waits for them, and re-layouts  79.1 us (4%)
  matrix products  66.3 us (3%)
    psum x1, waiting for transfers between devices, body(): diag_block = lax.psum(diag_buffer[:NB], ('row', 'col'))  1290 us
    another operation x30, other arithmetic, body(): lower_factor = jnp.linalg.cholesky(diag_block)  168 us
    all_gather x1, waiting for transfers between devices, body(): group_panel = lax.all_gather(panel_rows, 'col', axis=0, tiled=True)  126 us
    psum x1, waiting for transfers between devices, body(): column_rows = lax.psum(column_piece, 'row')  109 us
    another operation x3, other arithmetic, body(): lax.linalg.triangular_solve(lower_factor, front_slab[:, :NB], left_side=F...  83.8 us
    all_gather x1, waiting for transfers between devices, body(): lax.all_gather(child_update[0], 'col', axis=0, tiled=True)  65 us
    reduce_scatter x1, waiting for transfers between devices, body(): lax.psum_scatter(contribution, 'half', scatter_dimension=1, tiled=True)  53.8 us
    psum x1, waiting for transfers between devices, body(): panel_rows = lax.psum(panel_term, 'half')  48.4 us
  transfers between devices with their start and end apart: 7, of which 6 were waited for; matrix products, arithmetic and copies ran while one was open for 1% of the time, Pallas kernels for 0%

commit v1 on v0

v1 whole, which is shorter than its diff:
```python
import jax
import jax.numpy as jnp
from jax import lax
from jax.experimental import pallas as pl
from jax.experimental.pallas import tpu as pltpu
from jax.sharding import PartitionSpec as P

BLK = 128
NB = 1024
W = 4096
STRIP = 64
PLANE = ("col", "half")
HIGHEST = lax.Precision.HIGHEST
VMEM_LIMIT = 48 * 1024 * 1024


def prep_kernel(src_ref, hit_ref, child_ref, parent_ref, rows_ref, strips_ref, wide_ref):
    is_first_half = rows_ref[2]
    for w in range(W // BLK):
        start = pl.multiple_of(src_ref[w] * BLK, BLK)
        block = jnp.where(hit_ref[w] > 0, child_ref[:, pl.ds(start, BLK)], 0.0)
        j = w // 2
        q = (j % 8) * 2 + j // 8
        wide_ref[q, :, (w % 2) * BLK : (w % 2 + 1) * BLK] = block
        if w < NB // BLK:
            turned = block.T
            strips_ref[2 * w, :, 0:BLK] = turned[0:STRIP]
            strips_ref[2 * w + 1, :, 0:BLK] = turned[STRIP:BLK]

    @pl.when(is_first_half == 1)
    def _():
        for w in range(NB // BLK):
            turned = parent_ref[:, w * BLK : (w + 1) * BLK].T
            strips_ref[2 * w, :, BLK : 3 * BLK] = turned[0:STRIP]
            strips_ref[2 * w + 1, :, BLK : 3 * BLK] = turned[STRIP:BLK]

    @pl.when(is_first_half != 1)
    def _():
        for s in range(2):
            value = jnp.full((STRIP, BLK), rows_ref[s], jnp.int32).astype(jnp.float32)
            for d in range(16):
                strips_ref[d, :, (1 + s) * BLK : (2 + s) * BLK] = value


def prep(child, parent, source, hit, rows):
    smem = pl.BlockSpec(memory_space=pltpu.SMEM)
    return pl.pallas_call(
        prep_kernel,
        grid=(1,),
        in_specs=[
            smem,
            smem,
            pl.BlockSpec((BLK, NB), lambda i: (0, 0)),
            pl.BlockSpec((2 * BLK, NB), lambda i: (0, 0)),
            smem,
        ],
        out_specs=[
            pl.BlockSpec((16, STRIP, 3 * BLK), lambda i: (0, 0, 0)),
            pl.BlockSpec((16, BLK, 2 * BLK), lambda i: (0, 0, 0)),
        ],
        out_shape=[
            jax.ShapeDtypeStruct((16, STRIP, 3 * BLK), jnp.float32),
            jax.ShapeDtypeStruct((16, BLK, 2 * BLK), jnp.float32),
        ],
        compiler_params=pltpu.CompilerParams(vmem_limit_bytes=VMEM_LIMIT),
        name="prep",
    )(source, hit, child, parent, rows)


def strip_kernel(where_ref, pieces_ref, out_ref):
    for c in range(8):
        out_ref[:, 256 * c : 256 * (c + 1)] = pieces_ref[2 * c, :, BLK : 3 * BLK]
    for c in range(8):
        for s in range(2):
            at = pl.multiple_of(where_ref[s, c] * BLK, BLK)
            out_ref[:, pl.ds(at, BLK)] += pieces_ref[2 * c + s, :, 0:BLK]


def assemble_strip(pieces, where):
    return pl.pallas_call(
        strip_kernel,
        in_specs=[pl.BlockSpec(memory_space=pltpu.SMEM), pl.BlockSpec(memory_space=pltpu.VMEM)],
        out_specs=pl.BlockSpec(memory_space=pltpu.VMEM),
        out_shape=jax.ShapeDtypeStruct((STRIP, 2048), jnp.float32),
        compiler_params=pltpu.CompilerParams(vmem_limit_bytes=VMEM_LIMIT),
        name="strip",
    )(where, pieces)


def split_bf16(x):
    high = x.astype(jnp.bfloat16)
    return high, (x - high.astype(jnp.float32)).astype(jnp.bfloat16)


def product_kernel(inv_ref, flags_ref, wt_ref, rows_ref, sym_ref, front_ref, child_ref, out_ref, wh, wl):
    t = pl.program_id(0)

    @pl.when(t == 0)
    def _():
        high, low = split_bf16(wt_ref[...])
        wh[...] = high
        wl[...] = low

    use_sym = jnp.logical_and(flags_ref[0] == 1, t < 4)
    a = jnp.where(use_sym, sym_ref[...], rows_ref[...])
    ah, al = split_bf16(a)
    dims = (((1,), (0,)), ((), ()))

    def dot(x, y):
        return lax.dot_general(x, y, dims, preferred_element_type=jnp.float32)

    turned = dot(wh[...], ah) + (dot(wh[...], al) + dot(wl[...], ah))
    term = turned.T
    keep = flags_ref[1] == 0
    for b in range(2):
        base = front_ref[b * BLK : (b + 1) * BLK, :]
        for s in range(2):
            k = inv_ref[s, 2 * t + b]
            part = child_ref[jnp.maximum(k, 0) * 2 + s]
            base = base + jnp.where(k >= 0, part, 0.0)
        base = jnp.where(keep, base, 0.0)
        out_ref[b * BLK : (b + 1) * BLK, :] = base - term[b * BLK : (b + 1) * BLK, :]


def product(inv, flags, wt, rows, sym, front, child):
    smem = pl.BlockSpec(memory_space=pltpu.SMEM)
    return pl.pallas_call(
        product_kernel,
        grid=(8,),
        in_specs=[
            smem,
            smem,
            pl.BlockSpec((256, NB), lambda t: (0, 0)),
            pl.BlockSpec((NB, 256), lambda t: (0, t)),
            pl.BlockSpec((NB, 256), lambda t: (0, jnp.minimum(t, 3))),
            pl.BlockSpec((256, 256), lambda t: (t, 0)),
            pl.BlockSpec((16, BLK, 256), lambda t: (0, 0, 0)),
        ],
        out_specs=pl.BlockSpec((256, 256), lambda t: (t, 0)),
        out_shape=jax.ShapeDtypeStruct((2048, 256), jnp.float32),
        scratch_shapes=[pltpu.VMEM((256, NB), jnp.bfloat16), pltpu.VMEM((256, NB), jnp.bfloat16)],
        compiler_params=pltpu.CompilerParams(vmem_limit_bytes=VMEM_LIMIT),
        cost_estimate=pl.CostEstimate(flops=3 * 2 * 2048 * 1024 * 256, bytes_accessed=16 << 20, transcendentals=0),
        name="product",
    )(inv, flags, wt, rows, sym, front, child)


def body(child_update, parent_front, row_map, col_map):
    half = lax.axis_index("half")
    row = lax.axis_index("row")
    col = lax.axis_index("col")
    strip = half * 8 + col
    targets = jnp.arange(W // BLK, dtype=jnp.int32)
    own_columns = lax.dynamic_index_in_dim(col_map, half, 0, keepdims=False)
    match = (own_columns[:, None] == targets[None, :]).astype(jnp.int32)
    source = jnp.sum(match * jnp.arange(8, dtype=jnp.int32)[:, None], 0)
    hit = jnp.sum(match, 0)
    rows = jnp.concatenate([row_map[:, 0] - row * 16, jnp.where(half == 0, 1, 0)[None]]).astype(jnp.int32)
    strips, wide = prep(child_update[0], parent_front, source, hit, rows)

    pieces = lax.all_to_all(strips, PLANE, 0, 0, tiled=True)
    where = pieces[1::2, 0, BLK : 3 * BLK : BLK].T.astype(jnp.int32)
    a_strip = assemble_strip(pieces, where)

    diag_strip = a_strip[:, :NB]
    core0 = [lax.ppermute(diag_strip, "row", [(0, 2 * z)]) for z in range(1, 8)]
    spread = jnp.where(row == 0, diag_strip, sum(core0[1:], core0[0]))
    is_core0 = row % 2 == 0
    to_core1 = lax.ppermute(spread[STRIP // 2 :], "row", [(2 * z, 2 * z + 1) for z in range(8)])
    mine = jnp.where(is_core0, spread[: STRIP // 2], to_core1)
    gathered = lax.all_to_all(
        jnp.broadcast_to(mine[None], (16, STRIP // 2, NB)), PLANE, 0, 0, tiled=True
    )
    other = lax.ppermute(gathered, "row", [(i, i ^ 1) for i in range(16)])
    first = jnp.where(is_core0, gathered, other)
    second = jnp.where(is_core0, other, gathered)
    diag = jnp.concatenate([first, second], 1).reshape(NB, NB)

    wanted = jnp.broadcast_to(
        a_strip.reshape(STRIP, 8, 1, 256).transpose(1, 2, 0, 3), (8, 2, STRIP, 256)
    ).reshape(16, STRIP, 256)
    matching = lax.all_to_all(wanted, PLANE, 0, 0, tiled=True).reshape(NB, 256)
    sent = [
        lax.ppermute(matching, ("half", "row"), [(0, 2 * z), (16 + 1, 16 + 2 * z + 1)]) for z in range(1, 8)
    ]
    spread_c = jnp.where(row < 2, matching, sum(sent[1:], sent[0]))
    swapped = lax.ppermute(
        spread_c,
        ("half", "row"),
        [(2 * z, 2 * z + 1) for z in range(8)] + [(16 + 2 * z + 1, 16 + 2 * z) for z in range(8)],
    )
    c_turned = jnp.where(row % 2 == half, spread_c, swapped)

    a_turned = lax.all_gather(a_strip, PLANE, axis=0, tiled=True)
    front = lax.all_to_all(parent_front, "col", split_axis=1, concat_axis=0, tiled=True)
    child = lax.all_to_all(wide, PLANE, 0, 0, tiled=True)

    sym = (diag + diag.T) * 0.5
    lower = lax.linalg.cholesky(sym, symmetrize_input=False)
    solved = lax.linalg.triangular_solve(lower, c_turned, left_side=True, lower=True)
    unit = (
        jnp.arange(NB, dtype=jnp.int32)[:, None] == strip * 256 + jnp.arange(256, dtype=jnp.int32)[None, :]
    ).astype(jnp.float32)
    is_panel = strip < 4
    middle = jnp.where(is_panel, -unit, solved)
    wt = lax.linalg.triangular_solve(lower, middle, left_side=True, lower=True, transpose_a=True).T

    blocks = jnp.arange(16, dtype=jnp.int32)
    order = jnp.arange(8, dtype=jnp.int32)
    inv = jnp.max(jnp.where(where[:, :, None] == blocks[None, None, :], order[None, :, None], -1), axis=1)
    flags = jnp.stack([(row == 0).astype(jnp.int32), is_panel.astype(jnp.int32)])
    return product(inv, flags, wt, a_turned, sym, front, child)


def solution(mesh):
    return jax.shard_map(
        body,
        mesh=mesh,
        in_specs=(
            P("half", ("row", "col"), None),
            P(("row", "col"), "half"),
            P(None, ("row", "col")),
            P(),
        ),
        out_specs=P("row", ("half", "col")),
        check_vma=False,
    )
```

time: 2150 us -> 605 us (0.28)
  waiting for transfers between devices: 1690 us -> 50.7 us
  starting transfers between devices: 6.54 us -> 69.3 us
    psum x3 -> x0, waiting for transfers between devices: 1450 us -> none  [the longest x1 1290 us: body(): diag_block = lax.psum(diag_buffer[:NB], ('row', 'col'))]
    all_gather x2 -> x1, waiting for transfers between devices: 191 us -> 0.01 us  [body(): a_turned = lax.all_gather(a_strip, PLANE, axis=0, tiled=True)]
    reduce_scatter x1 -> x0, waiting for transfers between devices: 53.8 us -> none  [body(): lax.psum_scatter(contribution, 'half', scatter_dimension=1, tiled=True)]
    ppermute x0 -> x17, starting transfers between devices: none -> 34.3 us  [the longest x7 15.6 us: body(): core0 = [lax.ppermute(diag_strip, 'row', [(0, 2 * z)]) for z in range(1, 8)]]
    all_to_all x1 -> x4, waiting for transfers between devices: 0.01 us -> 31.5 us  [the longest x1 19.2 us: body(): lax.all_to_all(jnp.broadcast_to(mine[None], (16, STRIP // 2, NB)), PLANE,...]
    all_to_all x0 -> x1, blocking collectives: none -> 28.9 us  [body(): pieces = lax.all_to_all(strips, PLANE, 0, 0, tiled=True)]
    all_to_all x1 -> x4, starting transfers between devices: 6.34 us -> 35 us  [the longest x1 17.1 us: body(): child = lax.all_to_all(wide, PLANE, 0, 0, tiled=True)]
    dot_general x3 -> x0, matrix products: 25.3 us -> none  [the longest x1 17.1 us: body(): product = jnp.dot(group_panel, column_rows.T, precision=HIGHEST)]
  transfers between devices with their start and end apart: 7 -> 22, of which waited for: 6 -> 7; matrix products, arithmetic and copies ran while one was open for 1% -> 67% of each run, Pallas kernels for 0% -> 0%
where the time goes in v1:
time: 605 us; the launch traced here: 593 us
  other arithmetic  285 us (47%)
  local copies, waits for them, and re-layouts  74 us (12%)
  starting transfers between devices  69.3 us (11%)
  matrix products  51.4 us (8%)
  waiting for transfers between devices  50.7 us (8%)
  blocking collectives  28.9 us (5%)
  between operations  19.8 us (3%)
  Pallas kernels  14.6 us (2%)
    another operation x30, other arithmetic, body(): lower = lax.linalg.cholesky(sym, symmetrize_input=False)  180 us
    another operation x3, other arithmetic, body(): lax.linalg.triangular_solve(lower, middle, left_side=True, lower=True, tr...  85.6 us
    all_to_all x1, blocking collectives, body(): pieces = lax.all_to_all(strips, PLANE, 0, 0, tiled=True)  28.9 us
    another operation x24, local copies, waits for them, and re-layouts  28.6 us
    another operation x14, matrix products, body(): lower = lax.linalg.cholesky(sym, symmetrize_input=False)  24.9 us
    unnamed x59, local copies, waits for them, and re-layouts  19.8 us
    all_to_all x1, waiting for transfers between devices, body(): lax.all_to_all(jnp.broadcast_to(mine[None], (16, STRIP // 2, NB)), PLANE,...  19.2 us
    all_to_all x1, starting transfers between devices, body(): child = lax.all_to_all(wide, PLANE, 0, 0, tiled=True)  17.1 us
  transfers between devices with their start and end apart: 22, of which 7 were waited for; matrix products, arithmetic and copies ran while one was open for 67% of the time, Pallas kernels for 0%

profile of v1, /device:TPU:2, one launch (start us, length us, event | category | flops | bytes accessed | tf_op | source)
XLA Modules:
  0.0 593.3 jit_solution(4498007193187663579)
XLA Ops:
  12.1 28.9 %all_to_all.39.pieces_ref = f32[16,64,384]{2,1,0:T(8,128)S(1)} all-to-all(f32[16,64,384]{2,1,0:T(8,128)S(1)} %get-tuple-element.7), channel_id=1, replica_groups=mesh['half'=2,'row'=16,'col'=8] {'col','half'}, dimensions={0} | all-to-all | bytes 3145728 | tf_op jit(solution)/shard_map/all_to_all | solution.py:161
  44.3 7.8 %collective-permute-start.6 = (f32[64,1024]{1,0:T(8,128)S(1)}, f32[64,1024]{1,0:T(8,128)S(1)}, u32[]{:S(2)}, u32[]{:S(2)}) collective-permute-start(f32[64,1024]{1,0:T(8,128)S(1)} %slice.245), channel_id=1, source_target_pairs={{0,112},{1,113},{2,114},{3,115},{4,116},{5,117},{6,118},{7,119},{1... | collective-permute-start | bytes 786440 | tf_op jit(solution)/shard_map/ppermute | solution.py:166
  55.8 4.9 all-to-all-start.2
  67.3 2.7 collective-permute-done.2
  70.0 2.8 collective-permute-done
  72.8 2.8 collective-permute-done.1
  80.6 7.3 %all-to-all-start.1 = ((f32[16,32,1024]{2,1,0:T(8,128)}), f32[16,32,1024]{2,1,0:T(8,128)}, u32[]{:S(2)}, u32[]{:S(2)}) async-start(f32[16,32,1024]{2,1,0:T(8,128)} %broadcast_in_dim.19), calls=%async_computation.1 | async-start | bytes 4194304 | tf_op jit(solution)/shard_map/all_to_all | solution.py:171
  97.6 19.2 %all-to-all-done.1 = f32[16,32,1024]{2,1,0:T(8,128)} async-done(((f32[16,32,1024]{2,1,0:T(8,128)}), f32[16,32,1024]{2,1,0:T(8,128)}, u32[]{:S(2)}, u32[]{:S(2)}) %all-to-all-start.1) | async-done | bytes 2097184 | tf_op jit(solution)/shard_map/all_to_all | solution.py:171
  116.8 6.4 %collective-permute-start.8 = (f32[16,32,1024]{2,1,0:T(8,128)}, f32[16,32,1024]{2,1,0:T(8,128)}, u32[]{:S(2)}, u32[]{:S(2)}) collective-permute-start(f32[16,32,1024]{2,1,0:T(8,128)} %all-to-all-done.1), channel_id=1, source_target_pairs={{0,8},{8,0},{16,24},{24,16},{32,40},{40,32},{48,56},{56,48},{64,72... | collective-permute-start | bytes 6291464 | tf_op jit(solution)/shard_map/ppermute | solution.py:174
  123.2 4.8 add_select_fusion
  130.8 5.8 all-to-all-start.3
  137.9 9.9 %collective-permute-done.16 = f32[1024,256]{1,0:T(8,128)} collective-permute-done((f32[1024,256]{1,0:T(8,128)}, f32[1024,256]{1,0:T(8,128)}, u32[]{:S(2)}, u32[]{:S(2)}) %collective-permute-start.16) | collective-permute-done | bytes 1048608 | tf_op jit(solution)/shard_map/ppermute | solution.py:187
  149.2 2.7 broadcast_select_fusion.1
  151.9 2.5 pad_maximum_fusion
  154.4 5.5 copy.43
  159.9 4.4 fusion.sym_ref
  166.4 11.7 %cholesky.223 = f32[128,128]{1,0:T(8,128)S(1)} custom-call(f32[128,128]{1,0:T(8,128)S(1)} %cholesky.580), custom_call_target="Cholesky" | custom-call | tf_op jit(solution)/shard_map/cholesky | solution.py:199
  178.1 2.5 cholesky.255
  180.6 9.8 %custom-call.49 = f32[1,128,128]{1,2,0:T(8,128)S(1)} custom-call(f32[1,128,128]{2,1,0:T(8,128)S(1)} %get-tuple-element.77), custom_call_target="InvertDiagBlocksLowerTriangular" | custom-call | tf_op jit(solution)/shard_map/cholesky | solution.py:199
  190.4 2.3 constant_dynamic-update-slice_fusion.57
  195.1 11.9 %cholesky.244 = f32[128,128]{1,0:T(8,128)S(1)} custom-call(f32[128,128]{1,0:T(8,128)S(1)} %cholesky.584), custom_call_target="Cholesky" | custom-call | tf_op jit(solution)/shard_map/cholesky | solution.py:199
  207.6 9.8 %custom-call.50 = f32[1,128,128]{1,2,0:T(8,128)S(1)} custom-call(f32[1,128,128]{2,1,0:T(8,128)S(1)} %get-tuple-element.74), custom_call_target="InvertDiagBlocksLowerTriangular" | custom-call | tf_op jit(solution)/shard_map/cholesky | solution.py:199
  222.4 13.2 %cholesky.468 = f32[128,128]{1,0:T(8,128)} custom-call(f32[128,128]{1,0:T(8,128)} %cholesky.589), custom_call_target="Cholesky" | custom-call | tf_op jit(solution)/shard_map/cholesky | solution.py:199
  237.7 11.3 %custom-call.51 = f32[1,128,128]{1,2,0:T(8,128)} custom-call(f32[1,128,128]{2,1,0:T(8,128)} %get-tuple-element.71), custom_call_target="InvertDiagBlocksLowerTriangular" | custom-call | tf_op jit(solution)/shard_map/cholesky | solution.py:199
  250.9 2.4 slice_subtract_fusion.2
  253.9 12.9 %cholesky.487 = f32[128,128]{1,0:T(8,128)S(1)} custom-call(f32[128,128]{1,0:T(8,128)} %cholesky.594), custom_call_target="Cholesky" | custom-call | tf_op jit(solution)/shard_map/cholesky | solution.py:199
  268.1 10.6 %custom-call.52 = f32[1,128,128]{1,2,0:T(8,128)S(1)} custom-call(f32[1,128,128]{2,1,0:T(8,128)} %get-tuple-element.68), custom_call_target="InvertDiagBlocksLowerTriangular" | custom-call | tf_op jit(solution)/shard_map/cholesky | solution.py:199
  282.2 11.7 %cholesky.506 = f32[128,128]{1,0:T(8,128)S(1)} custom-call(f32[128,128]{1,0:T(8,128)S(1)} %cholesky.599), custom_call_target="Cholesky" | custom-call | tf_op jit(solution)/shard_map/cholesky | solution.py:199
  295.1 10.0 %custom-call.53 = f32[1,128,128]{1,2,0:T(8,128)S(1)} custom-call(f32[1,128,128]{2,1,0:T(8,128)S(1)} %get-tuple-element.65), custom_call_target="InvertDiagBlocksLowerTriangular" | custom-call | tf_op jit(solution)/shard_map/cholesky | solution.py:199
  308.4 11.7 %cholesky.526 = f32[128,128]{1,0:T(8,128)S(1)} custom-call(f32[128,128]{1,0:T(8,128)S(1)} %cholesky.604), custom_call_target="Cholesky" | custom-call | tf_op jit(solution)/shard_map/cholesky | solution.py:199
  320.7 9.8 %custom-call.54 = f32[1,128,128]{1,2,0:T(8,128)S(1)} custom-call(f32[1,128,128]{2,1,0:T(8,128)S(1)} %get-tuple-element.62), custom_call_target="InvertDiagBlocksLowerTriangular" | custom-call | tf_op jit(solution)/shard_map/cholesky | solution.py:199
  333.5 11.9 %cholesky.546 = f32[128,128]{1,0:T(8,128)S(1)} custom-call(f32[128,128]{1,0:T(8,128)S(1)} %cholesky.609), custom_call_target="Cholesky" | custom-call | tf_op jit(solution)/shard_map/cholesky | solution.py:199
  346.1 9.8 %custom-call.55 = f32[1,128,128]{1,2,0:T(8,128)S(1)} custom-call(f32[1,128,128]{2,1,0:T(8,128)S(1)} %get-tuple-element.59), custom_call_target="InvertDiagBlocksLowerTriangular" | custom-call | tf_op jit(solution)/shard_map/cholesky | solution.py:199
  358.5 11.7 %cholesky.564 = f32[128,128]{1,0:T(8,128)S(1)} custom-call(f32[128,128]{1,0:T(8,128)S(1)} %slice_subtract_fusion.20), custom_call_target="Cholesky" | custom-call | tf_op jit(solution)/shard_map/cholesky | solution.py:199
  381.5 4.8 select_select_fusion
  386.3 28.6 %while.1 = (s32[]{:T(128)}, f32[1024,1024]{1,0:T(8,128)}, s32[8,2]{0,1:T(2,128)S(1)}, f32[8,128,128]{2,1,0:T(8,128)}, s32[]{:T(128)}) while((s32[]{:T(128)}, f32[1024,1024]{1,0:T(8,128)}, s32[8,2]{0,1:T(2,128)S(1)}, f32[8,128,128]{2,1,0:T(8,128)}, s32[]{:T(128)}) %tuple.62), condition=%wide.while_cond, body=%wide.while_body.sunk | while | flops 2 | bytes 132205 | solution.py:206
  386.9 2.9 bitcast_dynamic-update-slice_fusion.2
  390.5 2.9 bitcast_dynamic-update-slice_fusion.2
  394.1 2.9 bitcast_dynamic-update-slice_fusion.2
  397.7 2.9 bitcast_dynamic-update-slice_fusion.2
  401.3 2.9 bitcast_dynamic-update-slice_fusion.2
  404.9 2.9 bitcast_dynamic-update-slice_fusion.2
  408.4 2.9 bitcast_dynamic-update-slice_fusion.2
  412.0 2.9 bitcast_dynamic-update-slice_fusion.2
  414.9 80.3 %custom-call.56 = f32[8,128,128]{1,2,0:T(8,128)} custom-call(f32[8,128,128]{2,1,0:T(8,128)} %get-tuple-element.16), custom_call_target="InvertDiagBlocksLowerTriangular" | custom-call | tf_op jit(solution)/shard_map/triangular_solve | solution.py:206
  532.0 17.1 %all-to-all-start.4 = ((f32[16,128,256]{2,1,0:T(8,128)}), f32[16,128,256]{2,1,0:T(8,128)}, u32[]{:S(2)}, u32[]{:S(2)}) async-start(f32[16,128,256]{2,1,0:T(8,128)} %copy-done.2), calls=%async_computation.4 | async-start | bytes 4194304 | tf_op jit(solution)/shard_map/all_to_all | solution.py:196
  562.2 12.4 %all-to-all-done.4.child_ref = f32[16,128,256]{2,1,0:T(8,128)} async-done(((f32[16,128,256]{2,1,0:T(8,128)}), f32[16,128,256]{2,1,0:T(8,128)}, u32[]{:S(2)}, u32[]{:S(2)}) %all-to-all-start.4) | async-done | bytes 2097184 | tf_op jit(solution)/shard_map/all_to_all | solution.py:196
  574.6 11.4 %product.1 = f32[2048,256]{1,0:T(8,128)} custom-call(s32[2,16]{1,0:T(2,128)S(1)} %select_reduce_fusion.8.inv_ref, s32[2]{0:T(128)S(1)} %add_convert_fusion.flags_ref, f32[256,1024]{1,0:T(8,128)S(1)} %bitcast.152, f32[1024,2048]{1,0:T(8,128)} %all-gather.2.cloned.1.call-done.rows_ref, f32[1024,1024]{1,0:T(8,128)} %copy-done.4, f32[2048,256]{1,0:T(8,128)S(1)} %bitcast.151, ...), custom_call_target="tpu_custom_call" | custom-call | flops 3221225472 | bytes 16777216 | tf_op jit(solution)/shard_map/product/pallas_call | solution.py:127
  (208 shorter events, 130.9 us)
Async XLA Ops:
  6.5 0.7 copy-start
  8.0 1.0 copy-start.3
  10.7 1.4 copy-start.2
  44.3 20.4 %collective-permute-start.6 = (f32[64,1024]{1,0:T(8,128)S(1)}, f32[64,1024]{1,0:T(8,128)S(1)}, u32[]{:S(2)}, u32[]{:S(2)}) collective-permute-start(f32[64,1024]{1,0:T(8,128)S(1)} %slice.245), channel_id=1, source_target_pairs={{0,112},{1,113},{2,114},{3,115},{4,116},{5,117},{6,118},{7,119},{1... | collective-permute-start | bytes 786440 | tf_op jit(solution)/shard_map/ppermute | solution.py:166
  52.0 13.9 %collective-permute-start.5 = (f32[64,1024]{1,0:T(8,128)S(1)}, f32[64,1024]{1,0:T(8,128)S(1)}, u32[]{:S(2)}, u32[]{:S(2)}) collective-permute-start(f32[64,1024]{1,0:T(8,128)S(1)} %slice.245), channel_id=1, source_target_pairs={{0,96},{1,97},{2,98},{3,99},{4,100},{5,101},{6,102},{7,103},{128,2... | collective-permute-start | bytes 786440 | tf_op jit(solution)/shard_map/ppermute | solution.py:166
  55.8 23.2 %all-to-all-start.2 = ((f32[16,64,256]{2,1,0:T(8,128)}), f32[16,64,256]{2,1,0:T(8,128)S(1)}, u32[]{:S(2)}, u32[]{:S(2)}) async-start(f32[16,64,256]{2,1,0:T(8,128)} %bitcast.28), calls=%async_computation.2 | async-start | bytes 2097152 | tf_op jit(solution)/shard_map/all_to_all | solution.py:182
  60.7 6.6 %collective-permute-start.4 = (f32[64,1024]{1,0:T(8,128)S(1)}, f32[64,1024]{1,0:T(8,128)S(1)}, u32[]{:S(2)}, u32[]{:S(2)}) collective-permute-start(f32[64,1024]{1,0:T(8,128)S(1)} %slice.245), channel_id=1, source_target_pairs={{0,80},{1,81},{2,82},{3,83},{4,84},{5,85},{6,86},{7,87},{128,208},... | collective-permute-start | bytes 786440 | tf_op jit(solution)/shard_map/ppermute | solution.py:166
  62.0 5.3 collective-permute-start.3
  63.3 6.7 %collective-permute-start.2 = (f32[64,1024]{1,0:T(8,128)S(1)}, f32[64,1024]{1,0:T(8,128)S(1)}, u32[]{:S(2)}, u32[]{:S(2)}) collective-permute-start(f32[64,1024]{1,0:T(8,128)S(1)} %slice.245), channel_id=1, source_target_pairs={{0,48},{1,49},{2,50},{3,51},{4,52},{5,53},{6,54},{7,55},{128,176},... | collective-permute-start | bytes 786440 | tf_op jit(solution)/shard_map/ppermute | solution.py:166
  64.7 8.2 %collective-permute-start = (f32[64,1024]{1,0:T(8,128)S(1)}, f32[64,1024]{1,0:T(8,128)S(1)}, u32[]{:S(2)}, u32[]{:S(2)}) collective-permute-start(f32[64,1024]{1,0:T(8,128)S(1)} %slice.245), channel_id=1, source_target_pairs={{0,16},{1,17},{2,18},{3,19},{4,20},{5,21},{6,22},{7,23},{128,144},... | collective-permute-start | bytes 786440 | tf_op jit(solution)/shard_map/ppermute | solution.py:166
  66.0 9.6 %collective-permute-start.1 = (f32[64,1024]{1,0:T(8,128)S(1)}, f32[64,1024]{1,0:T(8,128)S(1)}, u32[]{:S(2)}, u32[]{:S(2)}) collective-permute-start(f32[64,1024]{1,0:T(8,128)S(1)} %slice.245), channel_id=1, source_target_pairs={{0,32},{1,33},{2,34},{3,35},{4,36},{5,37},{6,38},{7,39},{128,160},... | collective-permute-start | bytes 786440 | tf_op jit(solution)/shard_map/ppermute | solution.py:166
  76.7 2.3 collective-permute-start.7
  80.6 36.2 %all-to-all-start.1 = ((f32[16,32,1024]{2,1,0:T(8,128)}), f32[16,32,1024]{2,1,0:T(8,128)}, u32[]{:S(2)}, u32[]{:S(2)}) async-start(f32[16,32,1024]{2,1,0:T(8,128)} %broadcast_in_dim.19), calls=%async_computation.1 | async-start | bytes 4194304 | tf_op jit(solution)/shard_map/all_to_all | solution.py:171
  87.9 6.4 %collective-permute-start.15 = (f32[1024,256]{1,0:T(8,128)S(1)}, f32[1024,256]{1,0:T(8,128)S(1)}, u32[]{:S(2)}, u32[]{:S(2)}) collective-permute-start(f32[1024,256]{1,0:T(8,128)S(1)} %bitcast.159), channel_id=1, source_target_pairs={{0,112},{136,248},{1,113},{137,249},{2,114},{138,250},{3,115},{139... | collective-permute-start | bytes 3145736 | tf_op jit(solution)/shard_map/ppermute | solution.py:184
  88.6 7.3 %collective-permute-start.14 = (f32[1024,256]{1,0:T(8,128)S(1)}, f32[1024,256]{1,0:T(8,128)S(1)}, u32[]{:S(2)}, u32[]{:S(2)}) collective-permute-start(f32[1024,256]{1,0:T(8,128)S(1)} %bitcast.160), channel_id=1, source_target_pairs={{0,96},{136,232},{1,97},{137,233},{2,98},{138,234},{3,99},{139,235... | collective-permute-start | bytes 3145736 | tf_op jit(solution)/shard_map/ppermute | solution.py:184
  89.4 8.3 %collective-permute-start.13 = (f32[1024,256]{1,0:T(8,128)S(1)}, f32[1024,256]{1,0:T(8,128)}, u32[]{:S(2)}, u32[]{:S(2)}) collective-permute-start(f32[1024,256]{1,0:T(8,128)S(1)} %bitcast.161), channel_id=1, source_target_pairs={{0,80},{136,216},{1,81},{137,217},{2,82},{138,218},{3,83},{139,219... | collective-permute-start | bytes 3145736 | tf_op jit(solution)/shard_map/ppermute | solution.py:184
  91.0 32.2 %collective-permute-start.12 = (f32[1024,256]{1,0:T(8,128)S(1)}, f32[1024,256]{1,0:T(8,128)}, u32[]{:S(2)}, u32[]{:S(2)}) collective-permute-start(f32[1024,256]{1,0:T(8,128)S(1)} %bitcast.162), channel_id=1, source_target_pairs={{0,64},{136,200},{1,65},{137,201},{2,66},{138,202},{3,67},{139,203... | collective-permute-start | bytes 3145736 | tf_op jit(solution)/shard_map/ppermute | solution.py:184
  92.7 30.5 %collective-permute-start.11 = (f32[1024,256]{1,0:T(8,128)S(1)}, f32[1024,256]{1,0:T(8,128)}, u32[]{:S(2)}, u32[]{:S(2)}) collective-permute-start(f32[1024,256]{1,0:T(8,128)S(1)} %bitcast.163), channel_id=1, source_target_pairs={{0,48},{136,184},{1,49},{137,185},{2,50},{138,186},{3,51},{139,187... | collective-permute-start | bytes 3145736 | tf_op jit(solution)/shard_map/ppermute | solution.py:184
  94.3 28.9 %copy-start.10 = (f32[1024,256]{1,0:T(8,128)}, f32[1024,256]{1,0:T(8,128)S(1)}, u32[]{:S(2)}) copy-start(f32[1024,256]{1,0:T(8,128)S(1)} %collective-permute-done.15) | copy-start | bytes 3145732
  94.3 28.9 %collective-permute-start.9 = (f32[1024,256]{1,0:T(8,128)S(1)}, f32[1024,256]{1,0:T(8,128)}, u32[]{:S(2)}, u32[]{:S(2)}) collective-permute-start(f32[1024,256]{1,0:T(8,128)S(1)} %bitcast.164), channel_id=1, source_target_pairs={{0,16},{136,152},{1,17},{137,153},{2,18},{138,154},{3,19},{139,155... | collective-permute-start | bytes 3145736 | tf_op jit(solution)/shard_map/ppermute | solution.py:184
  95.9 27.2 %copy-start.11 = (f32[1024,256]{1,0:T(8,128)}, f32[1024,256]{1,0:T(8,128)S(1)}, u32[]{:S(2)}) copy-start(f32[1024,256]{1,0:T(8,128)S(1)} %collective-permute-done.14) | copy-start | bytes 3145732
  95.9 27.3 %collective-permute-start.10 = (f32[1024,256]{1,0:T(8,128)S(1)}, f32[1024,256]{1,0:T(8,128)}, u32[]{:S(2)}, u32[]{:S(2)}) collective-permute-start(f32[1024,256]{1,0:T(8,128)S(1)} %bitcast.165), channel_id=1, source_target_pairs={{0,32},{136,168},{1,33},{137,169},{2,34},{138,170},{3,35},{139,171... | collective-permute-start | bytes 3145736 | tf_op jit(solution)/shard_map/ppermute | solution.py:184
  116.8 32.4 %collective-permute-start.8 = (f32[16,32,1024]{2,1,0:T(8,128)}, f32[16,32,1024]{2,1,0:T(8,128)}, u32[]{:S(2)}, u32[]{:S(2)}) collective-permute-start(f32[16,32,1024]{2,1,0:T(8,128)} %all-to-all-done.1), channel_id=1, source_target_pairs={{0,8},{8,0},{16,24},{24,16},{32,40},{40,32},{48,56},{56,48},{64,72... | collective-permute-start | bytes 6291464 | tf_op jit(solution)/shard_map/ppermute | solution.py:174
  123.2 6.1 %copy-start.6 = (f32[256,2048]{1,0:T(8,128)S(1)}, f32[256,2048]{1,0:T(8,128)}, u32[]{:S(2)}) copy-start(f32[256,2048]{1,0:T(8,128)} %parent_ref.1) | copy-start | bytes 6291460
  128.0 19.8 %collective-permute-start.16 = (f32[1024,256]{1,0:T(8,128)}, f32[1024,256]{1,0:T(8,128)}, u32[]{:S(2)}, u32[]{:S(2)}) collective-permute-start(f32[1024,256]{1,0:T(8,128)} %add_select_fusion), channel_id=1, source_target_pairs={{0,8},{16,24},{32,40},{48,56},{64,72},{80,88},{96,104},{112,120},{... | collective-permute-start | bytes 3145736 | tf_op jit(solution)/shard_map/ppermute | solution.py:187
  130.8 401.2 %all-to-all-start.3 = ((f32[256,8,256]{2,0,1:T(8,128)}), f32[256,8,256]{2,0,1:T(8,128)S(1)}, u32[]{:S(2)}, u32[]{:S(2)}) async-start(f32[256,8,256]{2,0,1:T(8,128)} %bitcast.158), calls=%async_computation.3 | async-start | bytes 4194304 | tf_op jit(solution)/shard_map/all_to_all | solution.py:195
  136.6 438.0 %all-gather.2.cloned.1.call-start = ((), (), s32[]{:S(2)}) async-start(), calls=%async_computation.5 | async-start | bytes 8912896 | tf_op jit(solution)/shard_map/all_gather | solution.py:194
  164.4 2.0 copy-start.4
  194.3 0.8 copy-start.9
  305.0 69.1 %copy-start.17 = (f32[128]{0:T(128)S(1)}, f32[128]{0:T(128)}, u32[]{:S(2)}) copy-start(f32[128]{0:T(128)} %get-tuple-element.67) | copy-start | bytes 1540
  305.0 70.4 %copy-start.18 = (f32[128]{0:T(128)S(1)}, f32[128]{0:T(128)}, u32[]{:S(2)}) copy-start(f32[128]{0:T(128)} %get-tuple-element.64) | copy-start | bytes 1540
  381.5 4.8 copy-start.19
  495.2 8.6 %copy-start.5 = (f32[1024,1024]{1,0:T(8,128)S(1)}, f32[1024,1024]{1,0:T(8,128)}, u32[]{:S(2)}) copy-start(f32[1024,1024]{1,0:T(8,128)} %get-tuple-element.140) | copy-start | bytes 12582916
  495.2 9.0 %copy-start.8 = (f32[8,128,128]{1,2,0:T(8,128)S(1)}, f32[8,128,128]{1,2,0:T(8,128)}, u32[]{:S(2)}) copy-start(f32[8,128,128]{1,2,0:T(8,128)} %custom-call.56) | copy-start | bytes 1572868
  502.6 4.6 copy-start.16
  509.6 1.6 copy-start.7
  532.0 42.6 %all-to-all-start.4 = ((f32[16,128,256]{2,1,0:T(8,128)}), f32[16,128,256]{2,1,0:T(8,128)}, u32[]{:S(2)}, u32[]{:S(2)}) async-start(f32[16,128,256]{2,1,0:T(8,128)} %copy-done.2), calls=%async_computation.4 | async-start | bytes 4194304 | tf_op jit(solution)/shard_map/all_to_all | solution.py:196
  549.0 13.1 %copy-start.15 = (f32[128,256]{0,1:T(8,128)S(1)}, f32[128,256]{0,1:T(8,128)}, u32[]{:S(2)}) copy-start(f32[128,256]{0,1:T(8,128)} %copy.49) | copy-start | bytes 393220
  549.0 13.1 %copy-start.14 = (f32[128,256]{0,1:T(8,128)S(1)}, f32[128,256]{0,1:T(8,128)}, u32[]{:S(2)}) copy-start(f32[128,256]{0,1:T(8,128)} %copy.50) | copy-start | bytes 393220
  549.0 13.1 %copy-start.13 = (f32[128,256]{0,1:T(8,128)S(1)}, f32[128,256]{0,1:T(8,128)}, u32[]{:S(2)}) copy-start(f32[128,256]{0,1:T(8,128)} %copy.51) | copy-start | bytes 393220
  549.1 13.1 %copy-start.12 = (f32[128,256]{0,1:T(8,128)S(1)}, f32[128,256]{0,1:T(8,128)}, u32[]{:S(2)}) copy-start(f32[128,256]{0,1:T(8,128)} %copy.52) | copy-start | bytes 393220
  574.6 11.4 %copy-start.1 = (s32[2,8]{1,0:T(2,128)S(1)}, s32[2,8]{1,0:T(2,128)}, u32[]{:S(2)}) copy-start(s32[2,8]{1,0:T(2,128)} %param.7) | copy-start | bytes 196
Sparse Core Ops, SparseCore 0:
  139.8 94.4 all-gather.1

commit v2 on v1

--- a/solution.py
+++ b/solution.py
@@ -10,8 +10,7 @@
 W = 4096
 STRIP = 64
 PLANE = ("col", "half")
-HIGHEST = lax.Precision.HIGHEST
-VMEM_LIMIT = 48 * 1024 * 1024
+VMEM_LIMIT = 56 * 1024 * 1024
 
 
 def prep_kernel(src_ref, hit_ref, child_ref, parent_ref, rows_ref, strips_ref, wide_ref):
@@ -90,6 +89,177 @@
 def split_bf16(x):
     high = x.astype(jnp.bfloat16)
     return high, (x - high.astype(jnp.float32)).astype(jnp.bfloat16)
+
+
+def dot3(xh, xl, yh, yl):
+    def dot(x, y):
+        return lax.dot_general(x, y, (((1,), (0,)), ((), ())), preferred_element_type=jnp.float32)
+
+    return dot(xh, yh) + (dot(xh, yl) + dot(xl, yh))
+
+
+def lane(x, i):
+    return jnp.broadcast_to(x[:, i : i + 1], (8, BLK))
+
+
+def sub(x, i):
+    return jnp.broadcast_to(x[i : i + 1, :], (8, x.shape[1]))
+
+
+def eliminate(d, e, base):
+    groups = len(d)
+    place = lax.broadcasted_iota(jnp.int32, (8, BLK), 0)
+    for g in range(groups):
+        first = base + 8 * g
+        columns = [lane(d[g], first + i) for i in range(8)]
+        below = [[lane(d[n], first + i) for i in range(8)] for n in range(g + 1, groups)]
+        scales = jnp.zeros((8, BLK), jnp.float32)
+        for i in range(8):
+            r = lax.rsqrt(sub(columns[i], i))
+            scales = jnp.where(place == i, r, scales)
+            l = columns[i] * r
+            low = [b[i] * r for b in below]
+            for m in range(i + 1, 8):
+                f = sub(l, m)
+                columns[m] = columns[m] - l * f
+                for n, b in enumerate(below):
+                    b[m] = b[m] - low[n] * f
+            dr = sub(d[g], i) * r
+            er = sub(e[g], i) * r
+            masked = jnp.where(place > i, l, 0.0)
+            d[g] = d[g] - masked * dr
+            e[g] = e[g] - masked * er
+            for n in range(len(below)):
+                d[g + 1 + n] = d[g + 1 + n] - low[n] * dr
+                e[g + 1 + n] = e[g + 1 + n] - low[n] * er
+        d[g] = d[g] * scales
+        e[g] = e[g] * scales
+    return d, e
+
+
+GROUP = 32
+
+
+def factor_block(de_ref):
+    for p in range(BLK // GROUP):
+        base = p * GROUP
+        rows = [slice(base + 8 * g, base + 8 * g + 8) for g in range(GROUP // 8)]
+        d = [de_ref[r, 0:BLK] for r in rows]
+        e = [de_ref[r, BLK : 2 * BLK] for r in rows]
+        d, e = eliminate(d, e, base)
+        for r, x, y in zip(rows, d, e):
+            de_ref[r, 0:BLK] = x
+            de_ref[r, BLK : 2 * BLK] = y
+        if base + GROUP < BLK:
+            done = de_ref[base : base + GROUP, :]
+            left = done[:, 0:BLK].T[base + GROUP :]
+            lh, ll = split_bf16(left)
+            rh, rl = split_bf16(done)
+            de_ref[base + GROUP :, :] -= dot3(lh, ll, rh, rl)
+
+
+def solve_kernel(flags_ref, own_ref, other_ref, c_ref, wt_ref, sym_ref, lh, ll, uh, ul, mh, ml, yh, yl, de, row):
+    core = flags_ref[0]
+    strip = flags_ref[1]
+    blocks = NB // BLK
+    for q in range(16):
+        at = pl.multiple_of(q * STRIP + core * 32, 32)
+        sym_ref[pl.ds(at, 32), :] = own_ref[q]
+        at = pl.multiple_of(q * STRIP + (1 - core) * 32, 32)
+        sym_ref[pl.ds(at, 32), :] = other_ref[q]
+    for i in range(blocks):
+        for j in range(i, blocks):
+            a = sym_ref[i * BLK : (i + 1) * BLK, j * BLK : (j + 1) * BLK]
+            b = sym_ref[j * BLK : (j + 1) * BLK, i * BLK : (i + 1) * BLK]
+            s = (a + b.T) * 0.5
+            sym_ref[i * BLK : (i + 1) * BLK, j * BLK : (j + 1) * BLK] = s
+            if j > i:
+                sym_ref[j * BLK : (j + 1) * BLK, i * BLK : (i + 1) * BLK] = s.T
+    mh[...] = jnp.zeros_like(mh)
+    ml[...] = jnp.zeros_like(ml)
+    eye = (
+        lax.broadcasted_iota(jnp.int32, (BLK, BLK), 0) == lax.broadcasted_iota(jnp.int32, (BLK, BLK), 1)
+    ).astype(jnp.float32)
+
+    def step(k, _):
+        for kk in range(blocks):
+
+            @pl.when(k == kk)
+            def _(kk=kk):
+                here = slice(kk * BLK, (kk + 1) * BLK)
+                done = kk * BLK
+                up = NB - done
+                if kk == 0:
+                    row[:, 0:NB] = sym_ref[here, :]
+                    row[:, NB:] = c_ref[here, :]
+                else:
+                    a, b = lh[here, 0:done], ll[here, 0:done]
+                    row[:, 0:up] = sym_ref[here, done:] - dot3(a, b, uh[0:done, done:], ul[0:done, done:])
+                    row[:, up:NB] = -dot3(a, b, mh[0:done, 0:done], ml[0:done, 0:done])
+                    row[:, NB:] = c_ref[here, :] - dot3(a, b, yh[0:done, :], yl[0:done, :])
+
+        de[:, 0:BLK] = row[:, 0:BLK]
+        de[:, BLK:] = eye
+        factor_block(de)
+        ih, il = split_bf16(de[:, BLK:])
+        rh, rl = split_bf16(row[:, BLK:])
+        scaled = dot3(ih, il, rh, rl)
+        sh, sl = split_bf16(scaled)
+        for kk in range(blocks):
+
+            @pl.when(k == kk)
+            def _(kk=kk):
+                here = slice(kk * BLK, (kk + 1) * BLK)
+                after = (kk + 1) * BLK
+                up = NB - after
+                if up:
+                    uh[here, after:] = sh[:, 0:up]
+                    ul[here, after:] = sl[:, 0:up]
+                    th, tl = split_bf16(scaled[:, 0:up].T)
+                    lh[after:, here] = th
+                    ll[after:, here] = tl
+                if kk:
+                    mh[here, 0 : kk * BLK] = sh[:, up : NB - BLK]
+                    ml[here, 0 : kk * BLK] = sl[:, up : NB - BLK]
+                mh[here, here] = ih
+                ml[here, here] = il
+                yh[here, :] = sh[:, NB - BLK :]
+                yl[here, :] = sl[:, NB - BLK :]
+
+        return 0
+
+    lax.fori_loop(0, blocks, step, 0)
+
+    @pl.when(strip < 4)
+    def _():
+        at = pl.multiple_of(jnp.minimum(strip, 3) * 256, 256)
+        wt_ref[...] = -(mh[pl.ds(at, 256), :].astype(jnp.float32) + ml[pl.ds(at, 256), :].astype(jnp.float32))
+
+    @pl.when(strip >= 4)
+    def _():
+        th, tl = yh[...].astype(jnp.float32).T.astype(jnp.bfloat16), yl[...].astype(jnp.float32).T.astype(jnp.bfloat16)
+        for n in range(4):
+            at = 256 * n
+            wt_ref[:, at : at + 256] = dot3(
+                th[:, at:], tl[:, at:], mh[at:, at : at + 256], ml[at:, at : at + 256]
+            )
+
+
+def solve(flags, own, other, c_turned):
+    vmem = pl.BlockSpec(memory_space=pltpu.VMEM)
+    half = pltpu.VMEM((NB, NB), jnp.bfloat16)
+    return pl.pallas_call(
+        solve_kernel,
+        in_specs=[pl.BlockSpec(memory_space=pltpu.SMEM), vmem, vmem, vmem],
+        out_specs=[vmem, vmem],
+        out_shape=[jax.ShapeDtypeStruct((256, NB), jnp.float32), jax.ShapeDtypeStruct((NB, NB), jnp.float32)],
+        scratch_shapes=[half] * 6
+        + [pltpu.VMEM((NB, 256), jnp.bfloat16)] * 2
+        + [pltpu.VMEM((BLK, 2 * BLK), jnp.float32), pltpu.VMEM((BLK, NB + 256), jnp.float32)],
+        compiler_params=pltpu.CompilerParams(vmem_limit_bytes=VMEM_LIMIT),
+        cost_estimate=pl.CostEstimate(flops=50_000_000_000, bytes_accessed=12 << 20, transcendentals=0),
+        name="solve",
+    )(flags, own, other, c_turned)
 
 
 def product_kernel(inv_ref, flags_ref, wt_ref, rows_ref, sym_ref, front_ref, child_ref, out_ref, wh, wl):
@@ -172,10 +342,6 @@
         jnp.broadcast_to(mine[None], (16, STRIP // 2, NB)), PLANE, 0, 0, tiled=True
     )
     other = lax.ppermute(gathered, "row", [(i, i ^ 1) for i in range(16)])
-    first = jnp.where(is_core0, gathered, other)
-    second = jnp.where(is_core0, other, gathered)
-    diag = jnp.concatenate([first, second], 1).reshape(NB, NB)
-
     wanted = jnp.broadcast_to(
         a_strip.reshape(STRIP, 8, 1, 256).transpose(1, 2, 0, 3), (8, 2, STRIP, 256)
     ).reshape(16, STRIP, 256)
@@ -195,20 +361,13 @@
     front = lax.all_to_all(parent_front, "col", split_axis=1, concat_axis=0, tiled=True)
     child = lax.all_to_all(wide, PLANE, 0, 0, tiled=True)
 
-    sym = (diag + diag.T) * 0.5
-    lower = lax.linalg.cholesky(sym, symmetrize_input=False)
-    solved = lax.linalg.triangular_solve(lower, c_turned, left_side=True, lower=True)
-    unit = (
-        jnp.arange(NB, dtype=jnp.int32)[:, None] == strip * 256 + jnp.arange(256, dtype=jnp.int32)[None, :]
-    ).astype(jnp.float32)
-    is_panel = strip < 4
-    middle = jnp.where(is_panel, -unit, solved)
-    wt = lax.linalg.triangular_solve(lower, middle, left_side=True, lower=True, transpose_a=True).T
+    place = jnp.stack([row % 2, strip]).astype(jnp.int32)
+    wt, sym = solve(place, gathered, other, c_turned)
 
     blocks = jnp.arange(16, dtype=jnp.int32)
     order = jnp.arange(8, dtype=jnp.int32)
     inv = jnp.max(jnp.where(where[:, :, None] == blocks[None, None, :], order[None, :, None], -1), axis=1)
-    flags = jnp.stack([(row == 0).astype(jnp.int32), is_panel.astype(jnp.int32)])
+    flags = jnp.stack([(row == 0).astype(jnp.int32), (strip < 4).astype(jnp.int32)])
     return product(inv, flags, wt, a_turned, sym, front, child)
 
 

time: 605 us -> 249 us (0.41); the launches traced: 593 us -> 248 us
  other arithmetic: 285 us -> 10.7 us
  local copies, waits for them, and re-layouts: 74 us -> 11.1 us
  Pallas kernels: 14.6 us -> 67 us
  matrix products: 51.4 us -> 0 us
  starting transfers between devices: 69.3 us -> 49 us
  waiting for transfers between devices: 50.7 us -> 67.6 us
  between operations: 19.8 us -> 13.6 us
    another operation x34 -> x2, other arithmetic: 266 us -> 1.23 us  [the longest x1 0.62 us: body(): jnp.stack([(row == 0).astype(jnp.int32), (strip < 4).astype(jnp.int32)])]
    another operation x44 -> x0, matrix products: 51.4 us -> none  [the longest x14 24.9 us: body(): lower = lax.linalg.cholesky(sym, symmetrize_input=False)]
    pallas_call x0 -> x1, Pallas kernels: none -> 48.7 us  [solve(): pl.pallas_call(solve_kernel, in_specs=[pl.BlockSpec(memory_space=pltpu.SM...]
    another operation x44 -> x0, local copies, waits for them, and re-layouts: 42.6 us -> none
    all_to_all x1, waiting for transfers between devices: 19.2 us -> 40.2 us  [body(): lax.all_to_all(jnp.broadcast_to(mine[None], (16, STRIP // 2, NB)), PLANE,...]
    all_to_all x1, waiting for transfers between devices: 0.01 us -> 18.8 us  [body(): lax.all_to_all(parent_front, 'col', split_axis=1, concat_axis=0, tiled=True)]
    unnamed x59 -> x21, local copies, waits for them, and re-layouts: 19.8 us -> 4.21 us
    all_to_all x1, waiting for transfers between devices: 12.4 us -> 0.01 us  [body(): child = lax.all_to_all(wide, PLANE, 0, 0, tiled=True)]
  transfers between devices with their start and end apart: 22 -> 22, of which waited for: 7 -> 7; matrix products, arithmetic and copies ran while one was open for 67% -> 6% of each run, Pallas kernels for 0% -> 20%
where the time goes in v2:
time: 249 us; the launch traced here: 248 us
  waiting for transfers between devices  67.6 us (27%)
  Pallas kernels  67 us (27%)
  starting transfers between devices  49 us (20%)
  blocking collectives  29.1 us (12%)
  between operations  13.6 us (5%)
  local copies, waits for them, and re-layouts  11.1 us (4%)
  other arithmetic  10.7 us (4%)
    pallas_call x1, Pallas kernels, solve(): pl.pallas_call(solve_kernel, in_specs=[pl.BlockSpec(memory_space=pltpu.SM...  48.7 us
    all_to_all x1, waiting for transfers between devices, body(): lax.all_to_all(jnp.broadcast_to(mine[None], (16, STRIP // 2, NB)), PLANE,...  40.2 us
    all_to_all x1, blocking collectives, body(): pieces = lax.all_to_all(strips, PLANE, 0, 0, tiled=True)  29.1 us
    all_to_all x1, waiting for transfers between devices, body(): lax.all_to_all(parent_front, 'col', split_axis=1, concat_axis=0, tiled=True)  18.8 us
    ppermute x7, starting transfers between devices, body(): core0 = [lax.ppermute(diag_strip, 'row', [(0, 2 * z)]) for z in range(1, 8)]  15.7 us
    pallas_call x1, Pallas kernels, product(): pl.pallas_call(product_kernel, grid=(8,), in_specs=[smem, smem, pl.BlockS...  12.3 us
    ppermute x7, starting transfers between devices, body(): lax.ppermute(matching, ('half', 'row'), [(0, 2 * z), (16 + 1, 16 + 2 * z...  9.68 us
    all_to_all x1, starting transfers between devices, body(): lax.all_to_all(jnp.broadcast_to(mine[None], (16, STRIP // 2, NB)), PLANE,...  7.56 us
  transfers between devices with their start and end apart: 22, of which 7 were waited for; matrix products, arithmetic and copies ran while one was open for 6% of the time, Pallas kernels for 20%

profile of v2, /device:TPU:2, one launch (start us, length us, event | category | flops | bytes accessed | tf_op | source)
XLA Modules:
  0.0 248.2 jit_solution(6286581682237122588)
XLA Ops:
  6.5 0.7 copy-done
  7.2 0.6 convert_reduce_fusion
  7.8 0.7 subtract_bitcast_fusion
  9.1 3.6 %prep.1 = (f32[16,64,384]{2,1,0:T(8,128)}, f32[16,128,256]{2,1,0:T(8,128)}) custom-call(s32[32]{0:T(128)} %get-tuple-element.14.src_ref, s32[32]{0:T(128)} %get-tuple-element.13.hit_ref, f32[128,1024]{1,0:T(8,128)} %bitcast.43, f32[256,2048]{1,0:T(8,128)} %parent_ref.1, s32[3]{0:T(128)} %pad_add_fusion.rows_ref), custom_call_target="tpu_custom_call" | custom-call | tf_op jit(solution)/shard_map/prep/pallas_call | solution.py:46
  12.7 29.1 %all_to_all.39.pieces_ref = f32[16,64,384]{2,1,0:T(8,128)S(1)} all-to-all(f32[16,64,384]{2,1,0:T(8,128)} %get-tuple-element.9), channel_id=1, replica_groups=mesh['half'=2,'row'=16,'col'=8] {'col','half'}, dimensions={0} | all-to-all | bytes 3145728 | tf_op jit(solution)/shard_map/all_to_all | solution.py:331
  41.8 0.7 slice.12
  42.5 0.7 copy.11
  43.2 2.4 strip.1
  45.6 1.0 slice.16
  46.6 3.8 %collective-permute-start = (f32[64,1024]{1,0:T(8,128)S(1)}, f32[64,1024]{1,0:T(8,128)S(1)}, u32[]{:S(2)}, u32[]{:S(2)}) collective-permute-start(f32[64,1024]{1,0:T(8,128)S(1)} %slice.16), channel_id=1, source_target_pairs={{0,16},{1,17},{2,18},{3,19},{4,20},{5,21},{6,22},{7,23},{128,144},... | collective-permute-start | bytes 786440 | tf_op jit(solution)/shard_map/ppermute | solution.py:336
  50.4 2.0 collective-permute-start.1
  52.4 1.2 copy.15
  53.8 1.1 broadcast_in_dim.39
  55.0 4.9 %all-to-all-start.2 = ((f32[16,64,256]{2,1,0:T(8,128)}), f32[16,64,256]{2,1,0:T(8,128)S(1)}, u32[]{:S(2)}, u32[]{:S(2)}) async-start(f32[16,64,256]{2,1,0:T(8,128)} %bitcast.13), calls=%async_computation.2 | async-start | bytes 2097152 | tf_op jit(solution)/shard_map/all_to_all | solution.py:348
  59.9 2.0 collective-permute-start.2
  61.9 3.2 %collective-permute-start.3 = (f32[64,1024]{1,0:T(8,128)S(1)}, f32[64,1024]{1,0:T(8,128)S(1)}, u32[]{:S(2)}, u32[]{:S(2)}) collective-permute-start(f32[64,1024]{1,0:T(8,128)S(1)} %slice.16), channel_id=1, source_target_pairs={{0,64},{1,65},{2,66},{3,67},{4,68},{5,69},{6,70},{7,71},{128,192},... | collective-permute-start | bytes 786440 | tf_op jit(solution)/shard_map/ppermute | solution.py:336
  65.2 1.3 collective-permute-start.4
  66.5 1.3 collective-permute-start.5
  67.8 2.0 collective-permute-start.6
  70.3 2.8 %collective-permute-done.5 = f32[64,1024]{1,0:T(8,128)S(1)} collective-permute-done((f32[64,1024]{1,0:T(8,128)S(1)}, f32[64,1024]{1,0:T(8,128)S(1)}, u32[]{:S(2)}, u32[]{:S(2)}) %collective-permute-start.5) | collective-permute-done | bytes 262176 | tf_op jit(solution)/shard_map/ppermute | solution.py:336
  73.1 2.8 %collective-permute-done.6 = f32[64,1024]{1,0:T(8,128)} collective-permute-done((f32[64,1024]{1,0:T(8,128)S(1)}, f32[64,1024]{1,0:T(8,128)}, u32[]{:S(2)}, u32[]{:S(2)}) %collective-permute-start.6) | collective-permute-done | bytes 262176 | tf_op jit(solution)/shard_map/ppermute | solution.py:336
  76.0 1.1 add_select_fusion.1
  77.1 1.3 collective-permute-start.7
  78.4 0.9 collective-permute-done.7
  79.4 1.0 copy-done.5
  80.4 1.6 broadcast_in_dim.37
  82.0 7.6 %all-to-all-start.1 = ((f32[16,32,1024]{2,1,0:T(8,128)}), f32[16,32,1024]{2,1,0:T(8,128)}, u32[]{:S(2)}, u32[]{:S(2)}) async-start(f32[16,32,1024]{2,1,0:T(8,128)} %broadcast_in_dim.37), calls=%async_computation.1 | async-start | bytes 4194304 | tf_op jit(solution)/shard_map/all_to_all | solution.py:341
  89.6 0.7 collective-permute-start.10
  90.3 0.7 collective-permute-start.11
  91.0 1.6 collective-permute-start.12
  92.7 1.6 collective-permute-start.13
  94.3 1.7 collective-permute-start.14
  96.0 1.6 collective-permute-start.15
  97.7 1.6 collective-permute-start.9
  99.3 40.2 %all-to-all-done.1.own_ref = f32[16,32,1024]{2,1,0:T(8,128)} async-done(((f32[16,32,1024]{2,1,0:T(8,128)}), f32[16,32,1024]{2,1,0:T(8,128)}, u32[]{:S(2)}, u32[]{:S(2)}) %all-to-all-start.1) | async-done | bytes 2097184 | tf_op jit(solution)/shard_map/all_to_all | solution.py:341
  139.5 1.6 copy.17
  141.0 3.6 %all-to-all-start.3 = ((f32[256,8,256]{2,0,1:T(8,128)}), f32[256,8,256]{2,0,1:T(8,128)S(1)}, u32[]{:S(2)}, u32[]{:S(2)}) async-start(f32[256,8,256]{2,0,1:T(8,128)} %bitcast.33), calls=%async_computation.3 | async-start | bytes 4194304 | tf_op jit(solution)/shard_map/all_to_all | solution.py:361
  144.7 4.6 %add_select_fusion = f32[1024,256]{1,0:T(8,128)} fusion(f32[1024,256]{1,0:T(8,128)} %collective-permute-done.15, f32[1024,256]{1,0:T(8,128)} %collective-permute-done.14, f32[1024,256]{1,0:T(8,128)} %collective-permute-done.13, f32[1024,256]{1,0:T(8,128)} %collective-permute-done.12, f32[1024,256]{1,0:T(8,128)} %copy-done.8, ...), kind=kLoop, calls=%fused_computation.1 | loop fusion | flops 1835008 | bytes 9437185 | tf_op jit(solution)/shard_map/jit(_where)/select_n | solution.py:352
  149.3 1.3 collective-permute-start.16
  151.2 0.6 add_convert_fusion.flags_ref
  151.8 0.7 select_reduce_fusion.inv_ref
  152.5 1.5 collective-permute-done.16
  154.1 1.2 broadcast_select_fusion.c_ref
  155.2 18.8 %all-to-all-done.3 = f32[256,8,256]{2,0,1:T(8,128)S(1)} async-done(((f32[256,8,256]{2,0,1:T(8,128)}), f32[256,8,256]{2,0,1:T(8,128)S(1)}, u32[]{:S(2)}, u32[]{:S(2)}) %all-to-all-start.3) | async-done | bytes 2097184 | tf_op jit(solution)/shard_map/all_to_all | solution.py:361
  174.0 1.3 copy-done.1
  175.3 4.9 %all-to-all-start.4 = ((f32[16,128,256]{2,1,0:T(8,128)}), f32[16,128,256]{2,1,0:T(8,128)}, u32[]{:S(2)}, u32[]{:S(2)}) async-start(f32[16,128,256]{2,1,0:T(8,128)} %get-tuple-element.12), calls=%async_computation.4 | async-start | bytes 4194304 | tf_op jit(solution)/shard_map/all_to_all | solution.py:362
  180.3 48.7 %solve.1 = (f32[256,1024]{1,0:T(8,128)}, f32[1024,1024]{1,0:T(8,128)}) custom-call(s32[2]{0:T(128)} %pad_add_fusion.1.flags_ref, f32[16,32,1024]{2,1,0:T(8,128)} %all-to-all-done.1.own_ref, f32[16,32,1024]{2,1,0:T(8,128)} %collective-permute-done.8.other_ref, f32[1024,256]{1,0:T(8,128)} %broadcast_select_fusion.c_ref), custom_call_target="tpu_custom_call" | custom-call | flops 49999998976 | bytes 12582912 | tf_op jit(solution)/shard_map/solve/pallas_call | solution.py:251
  229.0 12.3 %product.1 = f32[2048,256]{1,0:T(8,128)} custom-call(s32[2,16]{1,0:T(2,128)} %select_reduce_fusion.inv_ref, s32[2]{0:T(128)} %add_convert_fusion.flags_ref, f32[256,1024]{1,0:T(8,128)} %get-tuple-element.10.wt_ref, f32[1024,2048]{1,0:T(8,128)} %all-gather.2.cloned.1.call-done.rows_ref, f32[1024,1024]{1,0:T(8,128)} %get-tuple-element.11.sym_ref, ...), custom_call_target="tpu_custom_call" | custom-call | flops 3221225472 | bytes 16777216 | tf_op jit(solution)/shard_map/product/pallas_call | solution.py:297
  (43 shorter events, 2.0 us)
Async XLA Ops:
  6.5 0.7 copy-start
  6.5 222.4 %all-gather.2.cloned.1.call-start = ((), (), s32[]{:S(2)}) async-start(), calls=%async_computation.5 | async-start | bytes 8912896 | tf_op jit(solution)/shard_map/all_gather | solution.py:360
  41.8 1.4 copy-start.4
  46.6 19.9 %collective-permute-start = (f32[64,1024]{1,0:T(8,128)S(1)}, f32[64,1024]{1,0:T(8,128)S(1)}, u32[]{:S(2)}, u32[]{:S(2)}) collective-permute-start(f32[64,1024]{1,0:T(8,128)S(1)} %slice.16), channel_id=1, source_target_pairs={{0,16},{1,17},{2,18},{3,19},{4,20},{5,21},{6,22},{7,23},{128,144},... | collective-permute-start | bytes 786440 | tf_op jit(solution)/shard_map/ppermute | solution.py:336
  50.4 17.4 %collective-permute-start.1 = (f32[64,1024]{1,0:T(8,128)S(1)}, f32[64,1024]{1,0:T(8,128)S(1)}, u32[]{:S(2)}, u32[]{:S(2)}) collective-permute-start(f32[64,1024]{1,0:T(8,128)S(1)} %slice.16), channel_id=1, source_target_pairs={{0,32},{1,33},{2,34},{3,35},{4,36},{5,37},{6,38},{7,39},{128,160},... | collective-permute-start | bytes 786440 | tf_op jit(solution)/shard_map/ppermute | solution.py:336
  53.8 22.1 %copy-start.3 = (f32[64,2048]{1,0:T(8,128)S(1)}, f32[64,2048]{1,0:T(8,128)}, u32[]{:S(2)}) copy-start(f32[64,2048]{1,0:T(8,128)} %strip.1) | copy-start | bytes 1572868
  55.0 24.4 %all-to-all-start.2 = ((f32[16,64,256]{2,1,0:T(8,128)}), f32[16,64,256]{2,1,0:T(8,128)S(1)}, u32[]{:S(2)}, u32[]{:S(2)}) async-start(f32[16,64,256]{2,1,0:T(8,128)} %bitcast.13), calls=%async_computation.2 | async-start | bytes 2097152 | tf_op jit(solution)/shard_map/all_to_all | solution.py:348
  59.9 9.9 %collective-permute-start.2 = (f32[64,1024]{1,0:T(8,128)S(1)}, f32[64,1024]{1,0:T(8,128)S(1)}, u32[]{:S(2)}, u32[]{:S(2)}) collective-permute-start(f32[64,1024]{1,0:T(8,128)S(1)} %slice.16), channel_id=1, source_target_pairs={{0,48},{1,49},{2,50},{3,51},{4,52},{5,53},{6,54},{7,55},{128,176},... | collective-permute-start | bytes 786440 | tf_op jit(solution)/shard_map/ppermute | solution.py:336
  61.9 7.9 %collective-permute-start.3 = (f32[64,1024]{1,0:T(8,128)S(1)}, f32[64,1024]{1,0:T(8,128)S(1)}, u32[]{:S(2)}, u32[]{:S(2)}) collective-permute-start(f32[64,1024]{1,0:T(8,128)S(1)} %slice.16), channel_id=1, source_target_pairs={{0,64},{1,65},{2,66},{3,67},{4,68},{5,69},{6,70},{7,71},{128,192},... | collective-permute-start | bytes 786440 | tf_op jit(solution)/shard_map/ppermute | solution.py:336
  65.2 5.2 %collective-permute-start.4 = (f32[64,1024]{1,0:T(8,128)S(1)}, f32[64,1024]{1,0:T(8,128)S(1)}, u32[]{:S(2)}, u32[]{:S(2)}) collective-permute-start(f32[64,1024]{1,0:T(8,128)S(1)} %slice.16), channel_id=1, source_target_pairs={{0,80},{1,81},{2,82},{3,83},{4,84},{5,85},{6,86},{7,87},{128,208},... | collective-permute-start | bytes 786440 | tf_op jit(solution)/shard_map/ppermute | solution.py:336
  66.5 6.7 %collective-permute-start.5 = (f32[64,1024]{1,0:T(8,128)S(1)}, f32[64,1024]{1,0:T(8,128)S(1)}, u32[]{:S(2)}, u32[]{:S(2)}) collective-permute-start(f32[64,1024]{1,0:T(8,128)S(1)} %slice.16), channel_id=1, source_target_pairs={{0,96},{1,97},{2,98},{3,99},{4,100},{5,101},{6,102},{7,103},{128,2... | collective-permute-start | bytes 786440 | tf_op jit(solution)/shard_map/ppermute | solution.py:336
  67.8 8.1 %collective-permute-start.6 = (f32[64,1024]{1,0:T(8,128)S(1)}, f32[64,1024]{1,0:T(8,128)}, u32[]{:S(2)}, u32[]{:S(2)}) collective-permute-start(f32[64,1024]{1,0:T(8,128)S(1)} %slice.16), channel_id=1, source_target_pairs={{0,112},{1,113},{2,114},{3,115},{4,116},{5,117},{6,118},{7,119},{1... | collective-permute-start | bytes 786440 | tf_op jit(solution)/shard_map/ppermute | solution.py:336
  77.1 2.3 collective-permute-start.7
  79.4 1.0 copy-start.5
  82.0 7.6 %copy-start.6 = (f32[16,64,256]{2,1,0:T(8,128)S(1)}, f32[16,64,256]{2,1,0:T(8,128)}, u32[]{:S(2)}) copy-start(f32[16,64,256]{2,1,0:T(8,128)} %copy-done.5) | copy-start | bytes 3145732
  82.0 57.4 %copy-start.2 = (f32[256,2048]{1,0:T(8,128)S(1)}, f32[256,2048]{1,0:T(8,128)}, u32[]{:S(2)}) copy-start(f32[256,2048]{1,0:T(8,128)} %parent_ref.1) | copy-start | bytes 6291460
  82.0 57.4 %all-to-all-start.1 = ((f32[16,32,1024]{2,1,0:T(8,128)}), f32[16,32,1024]{2,1,0:T(8,128)}, u32[]{:S(2)}, u32[]{:S(2)}) async-start(f32[16,32,1024]{2,1,0:T(8,128)} %broadcast_in_dim.37), calls=%async_computation.1 | async-start | bytes 4194304 | tf_op jit(solution)/shard_map/all_to_all | solution.py:341
  89.6 6.4 %collective-permute-start.10 = (f32[1024,256]{1,0:T(8,128)S(1)}, f32[1024,256]{1,0:T(8,128)S(1)}, u32[]{:S(2)}, u32[]{:S(2)}) collective-permute-start(f32[1024,256]{1,0:T(8,128)S(1)} %bitcast.35), channel_id=1, source_target_pairs={{0,32},{136,168},{1,33},{137,169},{2,34},{138,170},{3,35},{139,171... | collective-permute-start | bytes 3145736 | tf_op jit(solution)/shard_map/ppermute | solution.py:350
  90.3 7.3 %collective-permute-start.11 = (f32[1024,256]{1,0:T(8,128)S(1)}, f32[1024,256]{1,0:T(8,128)S(1)}, u32[]{:S(2)}, u32[]{:S(2)}) collective-permute-start(f32[1024,256]{1,0:T(8,128)S(1)} %bitcast.36), channel_id=1, source_target_pairs={{0,48},{136,184},{1,49},{137,185},{2,50},{138,186},{3,51},{139,187... | collective-permute-start | bytes 3145736 | tf_op jit(solution)/shard_map/ppermute | solution.py:350
  91.0 8.2 %collective-permute-start.12 = (f32[1024,256]{1,0:T(8,128)S(1)}, f32[1024,256]{1,0:T(8,128)}, u32[]{:S(2)}, u32[]{:S(2)}) collective-permute-start(f32[1024,256]{1,0:T(8,128)S(1)} %bitcast.37), channel_id=1, source_target_pairs={{0,64},{136,200},{1,65},{137,201},{2,66},{138,202},{3,67},{139,203... | collective-permute-start | bytes 3145736 | tf_op jit(solution)/shard_map/ppermute | solution.py:350
  92.7 52.0 %collective-permute-start.13 = (f32[1024,256]{1,0:T(8,128)S(1)}, f32[1024,256]{1,0:T(8,128)}, u32[]{:S(2)}, u32[]{:S(2)}) collective-permute-start(f32[1024,256]{1,0:T(8,128)S(1)} %bitcast.38), channel_id=1, source_target_pairs={{0,80},{136,216},{1,81},{137,217},{2,82},{138,218},{3,83},{139,219... | collective-permute-start | bytes 3145736 | tf_op jit(solution)/shard_map/ppermute | solution.py:350
  94.3 50.3 %collective-permute-start.14 = (f32[1024,256]{1,0:T(8,128)S(1)}, f32[1024,256]{1,0:T(8,128)}, u32[]{:S(2)}, u32[]{:S(2)}) collective-permute-start(f32[1024,256]{1,0:T(8,128)S(1)} %bitcast.39), channel_id=1, source_target_pairs={{0,96},{136,232},{1,97},{137,233},{2,98},{138,234},{3,99},{139,235... | collective-permute-start | bytes 3145736 | tf_op jit(solution)/shard_map/ppermute | solution.py:350
  96.0 1.7 copy-start.7
  96.0 48.7 %collective-permute-start.15 = (f32[1024,256]{1,0:T(8,128)S(1)}, f32[1024,256]{1,0:T(8,128)}, u32[]{:S(2)}, u32[]{:S(2)}) collective-permute-start(f32[1024,256]{1,0:T(8,128)S(1)} %bitcast.40), channel_id=1, source_target_pairs={{0,112},{136,248},{1,113},{137,249},{2,114},{138,250},{3,115},{139... | collective-permute-start | bytes 3145736 | tf_op jit(solution)/shard_map/ppermute | solution.py:350
  97.7 1.6 copy-start.8
  97.7 47.0 %collective-permute-start.9 = (f32[1024,256]{1,0:T(8,128)S(1)}, f32[1024,256]{1,0:T(8,128)}, u32[]{:S(2)}, u32[]{:S(2)}) collective-permute-start(f32[1024,256]{1,0:T(8,128)S(1)} %bitcast.41), channel_id=1, source_target_pairs={{0,16},{136,152},{1,17},{137,153},{2,18},{138,154},{3,19},{139,155... | collective-permute-start | bytes 3145736 | tf_op jit(solution)/shard_map/ppermute | solution.py:350
  139.5 40.8 %collective-permute-start.8 = (f32[16,32,1024]{2,1,0:T(8,128)}, f32[16,32,1024]{2,1,0:T(8,128)}, u32[]{:S(2)}, u32[]{:S(2)}) collective-permute-start(f32[16,32,1024]{2,1,0:T(8,128)} %all-to-all-done.1.own_ref), channel_id=1, source_target_pairs={{0,8},{8,0},{16,24},{24,16},{32,40},{40,32},{48,56},{56,48},{64,72... | collective-permute-start | bytes 6291464 | tf_op jit(solution)/shard_map/ppermute | solution.py:344
  141.0 33.0 %all-to-all-start.3 = ((f32[256,8,256]{2,0,1:T(8,128)}), f32[256,8,256]{2,0,1:T(8,128)S(1)}, u32[]{:S(2)}, u32[]{:S(2)}) async-start(f32[256,8,256]{2,0,1:T(8,128)} %bitcast.33), calls=%async_computation.3 | async-start | bytes 4194304 | tf_op jit(solution)/shard_map/all_to_all | solution.py:361
  144.6 7.2 %copy-start.9 = (s32[8,1,2]{0,2,1:T(2,128)S(1)}, s32[8,1,2]{0,2,1:T(2,128)}, u32[]{:S(2)}) copy-start(s32[8,1,2]{0,2,1:T(2,128)} %copy.11) | copy-start | bytes 196
  149.3 4.8 %collective-permute-start.16 = (f32[1024,256]{1,0:T(8,128)}, f32[1024,256]{1,0:T(8,128)S(1)}, u32[]{:S(2)}, u32[]{:S(2)}) collective-permute-start(f32[1024,256]{1,0:T(8,128)} %add_select_fusion), channel_id=1, source_target_pairs={{0,8},{16,24},{32,40},{48,56},{64,72},{80,88},{96,104},{112,120},{... | collective-permute-start | bytes 3145736 | tf_op jit(solution)/shard_map/ppermute | solution.py:353
  174.0 1.3 copy-start.1
  175.3 53.6 %all-to-all-start.4 = ((f32[16,128,256]{2,1,0:T(8,128)}), f32[16,128,256]{2,1,0:T(8,128)}, u32[]{:S(2)}, u32[]{:S(2)}) async-start(f32[16,128,256]{2,1,0:T(8,128)} %get-tuple-element.12), calls=%async_computation.4 | async-start | bytes 4194304 | tf_op jit(solution)/shard_map/all_to_all | solution.py:362
Sparse Core Ops, SparseCore 0:
  45.7 104.1 all-gather.1

commit v3 on v2

v3 whole, which is shorter than its diff:
```python
import jax
import jax.numpy as jnp
from jax import lax
from jax.experimental import pallas as pl
from jax.experimental.pallas import tpu as pltpu
from jax.sharding import PartitionSpec as P

BLK = 128
NB = 1024
W = 4096
STRIP = 64
RUN = 32
HALF = NB // 2
TILE = 256
PLANE = ("col", "half")
VMEM_LIMIT = 24 * 1024 * 1024


def prep_kernel(src_ref, hit_ref, child_ref, parent_ref, rows_ref, strips_ref, wide_ref):
    is_first_half = rows_ref[2]
    for w in range(W // BLK):
        start = pl.multiple_of(src_ref[w] * BLK, BLK)
        block = jnp.where(hit_ref[w] > 0, child_ref[:, pl.ds(start, BLK)], 0.0)
        j = w // 2
        q = (j % 8) * 2 + j // 8
        wide_ref[q, :, (w % 2) * BLK : (w % 2 + 1) * BLK] = block
        if w < NB // BLK:
            turned = block.T
            strips_ref[2 * w, :, 0:BLK] = turned[0:STRIP]
            strips_ref[2 * w + 1, :, 0:BLK] = turned[STRIP:BLK]

    @pl.when(is_first_half == 1)
    def _():
        for w in range(NB // BLK):
            turned = parent_ref[:, w * BLK : (w + 1) * BLK].T
            strips_ref[2 * w, :, BLK : 3 * BLK] = turned[0:STRIP]
            strips_ref[2 * w + 1, :, BLK : 3 * BLK] = turned[STRIP:BLK]

    @pl.when(is_first_half != 1)
    def _():
        for s in range(2):
            value = jnp.full((STRIP, BLK), rows_ref[s], jnp.int32).astype(jnp.float32)
            for d in range(16):
                strips_ref[d, :, (1 + s) * BLK : (2 + s) * BLK] = value


def prep(child, parent, source, hit, rows):
    smem = pl.BlockSpec(memory_space=pltpu.SMEM)
    return pl.pallas_call(
        prep_kernel,
        grid=(1,),
        in_specs=[
            smem,
            smem,
            pl.BlockSpec((BLK, NB), lambda i: (0, 0)),
            pl.BlockSpec((2 * BLK, NB), lambda i: (0, 0)),
            smem,
        ],
        out_specs=[
            pl.BlockSpec((16, STRIP, 3 * BLK), lambda i: (0, 0, 0)),
            pl.BlockSpec((16, BLK, 2 * BLK), lambda i: (0, 0, 0)),
        ],
        out_shape=[
            jax.ShapeDtypeStruct((16, STRIP, 3 * BLK), jnp.float32),
            jax.ShapeDtypeStruct((16, BLK, 2 * BLK), jnp.float32),
        ],
        compiler_params=pltpu.CompilerParams(vmem_limit_bytes=VMEM_LIMIT),
        name="prep",
    )(source, hit, child, parent, rows)


def strip_kernel(where_ref, place_ref, pieces_ref, out_ref, keep_ref, give_ref):
    core = place_ref[0]
    for c in range(8):
        out_ref[:, 256 * c : 256 * (c + 1)] = pieces_ref[2 * c, :, BLK : 3 * BLK]
    for c in range(8):
        for s in range(2):
            at = pl.multiple_of(where_ref[s, c] * BLK, BLK)
            out_ref[:, pl.ds(at, BLK)] += pieces_ref[2 * c + s, :, 0:BLK]
    keep_ref[...] = out_ref[pl.ds(pl.multiple_of(core * RUN, RUN), RUN), :]
    give_ref[...] = out_ref[pl.ds(pl.multiple_of((1 - core) * RUN, RUN), RUN), :]


def assemble_strip(pieces, where, place):
    smem = pl.BlockSpec(memory_space=pltpu.SMEM)
    vmem = pl.BlockSpec(memory_space=pltpu.VMEM)
    half = jax.ShapeDtypeStruct((RUN, 2048), jnp.float32)
    return pl.pallas_call(
        strip_kernel,
        in_specs=[smem, smem, vmem],
        out_specs=[vmem] * 3,
        out_shape=[jax.ShapeDtypeStruct((STRIP, 2048), jnp.float32), half, half],
        compiler_params=pltpu.CompilerParams(vmem_limit_bytes=24 * 1024 * 1024),
        name="strip",
    )(where, place, pieces)


def share_kernel(place_ref, keep_ref, got_ref, start_ref, wanted_ref):
    core = place_ref[0]
    start_ref[...] = jnp.where(core == 0, keep_ref[:, 0:NB], got_ref[:, 0:NB])
    for c in range(8):
        a = keep_ref[:, 256 * c : 256 * (c + 1)]
        b = got_ref[:, 256 * c : 256 * (c + 1)]
        wanted_ref[2 * c] = jnp.where(core == 0, a, b)
        wanted_ref[2 * c + 1] = jnp.where(core == 0, b, a)


def share(place, keep, got):
    vmem = pl.BlockSpec(memory_space=pltpu.VMEM)
    return pl.pallas_call(
        share_kernel,
        in_specs=[pl.BlockSpec(memory_space=pltpu.SMEM), vmem, vmem],
        out_specs=[vmem] * 2,
        out_shape=[
            jax.ShapeDtypeStruct((RUN, NB), jnp.float32),
            jax.ShapeDtypeStruct((16, RUN, 256), jnp.float32),
        ],
        compiler_params=pltpu.CompilerParams(vmem_limit_bytes=16 * 1024 * 1024),
        name="share",
    )(place, keep, got)


def turn_kernel(parent_ref, out_ref):
    for n in range(8):
        out_ref[n] = parent_ref[:, 256 * n : 256 * (n + 1)]


def turn(parent):
    vmem = pl.BlockSpec(memory_space=pltpu.VMEM)
    return pl.pallas_call(
        turn_kernel,
        in_specs=[vmem],
        out_specs=vmem,
        out_shape=jax.ShapeDtypeStruct((8, 256, 256), jnp.float32),
        compiler_params=pltpu.CompilerParams(vmem_limit_bytes=16 * 1024 * 1024),
        cost_estimate=pl.CostEstimate(flops=60_000_000_000, bytes_accessed=4 << 20, transcendentals=0),
        name="turn",
    )(parent)


def pick_kernel(copies, index_ref, *refs):
    out_ref = refs[-1]
    for i in range(len(refs) - 1):

        @pl.when(index_ref[0] == i)
        def _(i=i):
            if copies:
                for n in range(copies):
                    out_ref[n] = refs[i][...]
            else:
                out_ref[...] = refs[i][...]


def pick(index, arrays, copies=0):
    shape = arrays[0].shape
    vmem = pl.BlockSpec(memory_space=pltpu.VMEM)
    return pl.pallas_call(
        lambda *refs: pick_kernel(copies, *refs),
        in_specs=[pl.BlockSpec(memory_space=pltpu.SMEM)] + [vmem] * len(arrays),
        out_specs=vmem,
        out_shape=jax.ShapeDtypeStruct((copies,) + shape if copies else shape, arrays[0].dtype),
        compiler_params=pltpu.CompilerParams(vmem_limit_bytes=16 * 1024 * 1024),
        name="pick",
    )(index, *arrays)


def split_bf16(x):
    high = x.astype(jnp.bfloat16)
    return high, (x - high.astype(jnp.float32)).astype(jnp.bfloat16)


def dot3(xh, xl, yh, yl):
    def dot(x, y):
        return lax.dot_general(x, y, (((1,), (0,)), ((), ())), preferred_element_type=jnp.float32)

    return dot(xh, yh) + (dot(xh, yl) + dot(xl, yh))


def lane(x, i):
    return jnp.broadcast_to(x[:, i : i + 1], (8, BLK))


def sub(x, i):
    return jnp.broadcast_to(x[i : i + 1, :], (8, x.shape[1]))


def eliminate(d, e, base):
    groups = len(d)
    place = lax.broadcasted_iota(jnp.int32, (8, BLK), 0)
    for g in range(groups):
        first = base + 8 * g
        columns = [lane(d[g], first + i) for i in range(8)]
        below = [[lane(d[n], first + i) for i in range(8)] for n in range(g + 1, groups)]
        scales = jnp.zeros((8, BLK), jnp.float32)
        for i in range(8):
            r = lax.rsqrt(sub(columns[i], i))
            scales = jnp.where(place == i, r, scales)
            l = columns[i] * r
            low = [b[i] * r for b in below]
            for m in range(i + 1, 8):
                f = sub(l, m)
                columns[m] = columns[m] - l * f
                for n, b in enumerate(below):
                    b[m] = b[m] - low[n] * f
            dr = sub(d[g], i) * r
            er = sub(e[g], i) * r
            masked = jnp.where(place > i, l, 0.0)
            d[g] = d[g] - masked * dr
            e[g] = e[g] - masked * er
            for n in range(len(below)):
                d[g + 1 + n] = d[g + 1 + n] - low[n] * dr
                e[g + 1 + n] = e[g + 1 + n] - low[n] * er
        d[g] = d[g] * scales
        e[g] = e[g] * scales
    return d, e


GROUP = 32


def factor_block(de_ref):
    for p in range(BLK // GROUP):
        base = p * GROUP
        rows = [slice(base + 8 * g, base + 8 * g + 8) for g in range(GROUP // 8)]
        d = [de_ref[r, 0:BLK] for r in rows]
        e = [de_ref[r, BLK : 2 * BLK] for r in rows]
        d, e = eliminate(d, e, base)
        for r, x, y in zip(rows, d, e):
            de_ref[r, 0:BLK] = x
            de_ref[r, BLK : 2 * BLK] = y
        if base + GROUP < BLK:
            done = de_ref[base : base + GROUP, :]
            left = done[:, 0:BLK].T[base + GROUP :]
            lh, ll = split_bf16(left)
            rh, rl = split_bf16(done)
            de_ref[base + GROUP :, :] -= dot3(lh, ll, rh, rl)


def factor_half(a_ref, r_ref, lh, ll, uh, ul, mh, ml, zh, zl, de, row):
    blocks = HALF // BLK
    mh[...] = jnp.zeros_like(mh)
    ml[...] = jnp.zeros_like(ml)
    eye = (
        lax.broadcasted_iota(jnp.int32, (BLK, BLK), 0) == lax.broadcasted_iota(jnp.int32, (BLK, BLK), 1)
    ).astype(jnp.float32)

    def step(k, _):
        for kk in range(blocks):

            @pl.when(k == kk)
            def _(kk=kk):
                here = slice(kk * BLK, (kk + 1) * BLK)
                done = kk * BLK
                up = HALF - done
                if kk == 0:
                    row[:, 0:HALF] = a_ref[here, 0:HALF]
                    row[:, HALF:] = r_ref[here, :]
                else:
                    x, y = lh[here, 0:done], ll[here, 0:done]
                    row[:, 0:up] = a_ref[here, done:HALF] - dot3(x, y, uh[0:done, done:], ul[0:done, done:])
                    row[:, up:HALF] = -dot3(x, y, mh[0:done, 0:done], ml[0:done, 0:done])
                    row[:, HALF:] = r_ref[here, :] - dot3(x, y, zh[0:done, :], zl[0:done, :])

        de[:, 0:BLK] = row[:, 0:BLK]
        de[:, BLK:] = eye
        factor_block(de)
        ih, il = split_bf16(de[:, BLK:])
        rh, rl = split_bf16(row[:, BLK:])
        scaled = dot3(ih, il, rh, rl)
        sh, sl = split_bf16(scaled)
        for kk in range(blocks):

            @pl.when(k == kk)
            def _(kk=kk):
                here = slice(kk * BLK, (kk + 1) * BLK)
                after = (kk + 1) * BLK
                up = HALF - after
                if up:
                    uh[here, after:] = sh[:, 0:up]
                    ul[here, after:] = sl[:, 0:up]
                    th, tl = split_bf16(scaled[:, 0:up].T)
                    lh[after:, here] = th
                    ll[after:, here] = tl
                if kk:
                    mh[here, 0 : kk * BLK] = sh[:, up : HALF - BLK]
                    ml[here, 0 : kk * BLK] = sl[:, up : HALF - BLK]
                mh[here, here] = ih
                ml[here, here] = il
                zh[here, :] = sh[:, HALF - BLK :]
                zl[here, :] = sl[:, HALF - BLK :]

        return 0

    lax.fori_loop(0, blocks, step, 0)


def first_kernel(
    place_ref, own_ref, other_ref, out_ref, mh_out, ml_out, rest_out, cross_out,
    lh, ll, uh, ul, zh, zl, de, row, sym_ref, mh_ref, ml_ref, rest_ref, cross_ref, sem
):
    core = place_ref[0]
    for q in range(16):
        at = pl.multiple_of(q * STRIP + core * 32, 32)
        sym_ref[pl.ds(at, 32), :] = own_ref[q]
        at = pl.multiple_of(q * STRIP + (1 - core) * 32, 32)
        sym_ref[pl.ds(at, 32), :] = other_ref[q]
    blocks = NB // BLK
    for i in range(blocks):
        for j in range(i, blocks):
            a = sym_ref[i * BLK : (i + 1) * BLK, j * BLK : (j + 1) * BLK]
            b = sym_ref[j * BLK : (j + 1) * BLK, i * BLK : (i + 1) * BLK]
            s = (a + b.T) * 0.5
            sym_ref[i * BLK : (i + 1) * BLK, j * BLK : (j + 1) * BLK] = s
            if j > i:
                sym_ref[j * BLK : (j + 1) * BLK, i * BLK : (i + 1) * BLK] = s.T
    moves = [pltpu.make_async_copy(sym_ref, out_ref, sem.at[0])]
    moves[0].start()
    factor_half(
        sym_ref.at[0:HALF, 0:HALF], sym_ref.at[0:HALF, HALF:], lh, ll, uh, ul, mh_ref, ml_ref, zh, zl, de, row
    )
    for n, (x, y) in enumerate([(mh_ref, mh_out), (ml_ref, ml_out)]):
        moves.append(pltpu.make_async_copy(x, y, sem.at[1 + n]))
        moves[-1].start()
    th = zh[...].astype(jnp.float32).T.astype(jnp.bfloat16)
    tl = zl[...].astype(jnp.float32).T.astype(jnp.bfloat16)
    rest_ref[...] = sym_ref[HALF:, HALF:] - dot3(th, tl, zh[...], zl[...])
    moves.append(pltpu.make_async_copy(rest_ref, rest_out, sem.at[3]))
    moves[-1].start()
    cross_ref[...] = -dot3(th, tl, mh_ref[...], ml_ref[...])
    moves.append(pltpu.make_async_copy(cross_ref, cross_out, sem.at[4]))
    moves[-1].start()
    for move in moves:
        move.wait()


def second_kernel(
    place_ref, rest_in, cross_in, mh_in, ml_in, c_in, d_in, wt_ref,
    lh, ll, uh, ul, nh, nl, zh, zl, de, row, rest_ref, cross_ref, mh_ref, ml_ref, c_ref, d_ref, c_all, sem
):
    strip = place_ref[1]
    pairs = [(rest_in, rest_ref), (cross_in, cross_ref), (mh_in, mh_ref), (ml_in, ml_ref), (c_in, c_ref), (d_in, d_ref)]
    moves = [pltpu.make_async_copy(x, y, sem.at[n]) for n, (x, y) in enumerate(pairs)]
    for move in moves:
        move.start()
    for move in moves[:2]:
        move.wait()
    factor_half(rest_ref, cross_ref, lh, ll, uh, ul, nh, nl, zh, zl, de, row)
    for move in moves[2:]:
        move.wait()

    def joined(x, y):
        return x.astype(jnp.float32) + y.astype(jnp.float32)

    for s in range(2):

        @pl.when(strip == s)
        def _(s=s):
            at = slice(256 * s, 256 * s + 256)
            wt_ref[:, 0:HALF] = -joined(mh_ref[at, :], ml_ref[at, :])
            wt_ref[:, HALF:] = jnp.zeros((256, HALF), jnp.float32)

        @pl.when(strip == s + 2)
        def _(s=s):
            at = slice(256 * s, 256 * s + 256)
            wt_ref[:, 0:HALF] = -joined(zh[at, :], zl[at, :])
            wt_ref[:, HALF:] = -joined(nh[at, :], nl[at, :])

    @pl.when(strip >= 4)
    def _():
        core = place_ref[0]
        for q in range(16):
            at = pl.multiple_of(q * STRIP + core * RUN, RUN)
            c_all[pl.ds(at, RUN), :] = c_ref[q]
            at = pl.multiple_of(q * STRIP + (1 - core) * RUN, RUN)
            c_all[pl.ds(at, RUN), :] = d_ref[q]
        ch, cl = split_bf16(c_all[0:HALF, :])
        dh, dl = split_bf16(c_all[HALF:, :])
        low = dot3(zh[...], zl[...], ch, cl) + dot3(nh[...], nl[...], dh, dl)
        th, tl = split_bf16(low.T)
        high = dot3(mh_ref[...], ml_ref[...], ch, cl)
        sh, sl = split_bf16(high.T)
        wt_ref[:, 0:HALF] = dot3(sh, sl, mh_ref[...], ml_ref[...]) + dot3(th, tl, zh[...], zl[...])
        wt_ref[:, HALF:] = dot3(th, tl, nh[...], nl[...])


SQUARE = (HALF, HALF)


def factor_scratch(count):
    return [pltpu.VMEM(SQUARE, jnp.bfloat16)] * count + [
        pltpu.VMEM((BLK, 2 * BLK), jnp.float32),
        pltpu.VMEM((BLK, NB), jnp.float32),
    ]


def first_half(place, own, other):
    vmem = pl.BlockSpec(memory_space=pltpu.VMEM)
    hbm = pl.BlockSpec(memory_space=pltpu.HBM)
    shapes = [((NB, NB), jnp.float32)] + [(SQUARE, jnp.bfloat16)] * 2 + [(SQUARE, jnp.float32)] * 2
    return pl.pallas_call(
        first_kernel,
        in_specs=[pl.BlockSpec(memory_space=pltpu.SMEM), vmem, vmem],
        out_specs=[hbm] * 5,
        out_shape=[jax.ShapeDtypeStruct(*shape) for shape in shapes],
        scratch_shapes=factor_scratch(6) + [pltpu.VMEM(*shape) for shape in shapes] + [pltpu.SemaphoreType.DMA((5,))],
        compiler_params=pltpu.CompilerParams(vmem_limit_bytes=60 * 1024 * 1024),
        cost_estimate=pl.CostEstimate(flops=30_000_000_000, bytes_accessed=12 << 20, transcendentals=0),
        name="first_half",
    )(place, own, other)


def second_half(place, rest, cross, mh, ml, c_turned, d_turned):
    hbm = pl.BlockSpec(memory_space=pltpu.HBM)
    arrays = (rest, cross, mh, ml, c_turned, d_turned)
    return pl.pallas_call(
        second_kernel,
        in_specs=[pl.BlockSpec(memory_space=pltpu.SMEM)] + [hbm] * 6,
        out_specs=pl.BlockSpec(memory_space=pltpu.VMEM),
        out_shape=jax.ShapeDtypeStruct((256, NB), jnp.float32),
        scratch_shapes=factor_scratch(8)
        + [pltpu.VMEM(x.shape, x.dtype) for x in arrays]
        + [pltpu.VMEM((NB, 256), jnp.float32), pltpu.SemaphoreType.DMA((6,))],
        compiler_params=pltpu.CompilerParams(vmem_limit_bytes=60 * 1024 * 1024),
        cost_estimate=pl.CostEstimate(flops=1_000_000_000, bytes_accessed=6 << 20, transcendentals=0),
        name="second_half",
    )(place, *arrays)


def product_kernel(inv_ref, flags_ref, wt_ref, rows_ref, sym_ref, front_ref, child_ref, out_ref, wh, wl):
    t = pl.program_id(0)

    @pl.when(t == 0)
    def _():
        high, low = split_bf16(wt_ref[...])
        wh[...] = high
        wl[...] = low

    use_sym = jnp.logical_and(flags_ref[0] == 1, t < NB // TILE)
    a = jnp.where(use_sym, sym_ref[...], rows_ref[...])
    ah, al = split_bf16(a)
    term = dot3(wh[...], wl[...], ah, al).T
    keep = flags_ref[1] == 0
    for b in range(TILE // BLK):
        part = front_ref[0, b * BLK : (b + 1) * BLK, :]
        for s in range(2):
            n = inv_ref[s, (TILE // BLK) * t + b]
            part = part + jnp.where(n >= 0, child_ref[jnp.maximum(n, 0) * 2 + s], 0.0)
        part = jnp.where(keep, part, 0.0)
        out_ref[b * BLK : (b + 1) * BLK, :] = part - term[b * BLK : (b + 1) * BLK, :]


def product(inv, flags, wt, rows, sym, front, child):
    def sym_tile(t, flags):
        return jnp.where(flags[0] == 1, jnp.minimum(t, NB // TILE - 1), 0)

    return pl.pallas_call(
        product_kernel,
        grid_spec=pltpu.PrefetchScalarGridSpec(
            num_scalar_prefetch=2,
            grid=(2048 // TILE,),
            in_specs=[
                pl.BlockSpec((256, NB), lambda t, i, f: (0, 0)),
                pl.BlockSpec((NB, TILE), lambda t, i, f: (0, t)),
                pl.BlockSpec((NB, TILE), lambda t, i, f: (0, sym_tile(t, f))),
                pl.BlockSpec((1, TILE, 256), lambda t, i, f: (t, 0, 0)),
                pl.BlockSpec((16, BLK, 256), lambda t, i, f: (0, 0, 0)),
            ],
            out_specs=pl.BlockSpec((TILE, 256), lambda t, i, f: (t, 0)),
            scratch_shapes=[pltpu.VMEM((256, NB), jnp.bfloat16), pltpu.VMEM((256, NB), jnp.bfloat16)],
        ),
        out_shape=jax.ShapeDtypeStruct((2048, 256), jnp.float32),
        compiler_params=pltpu.CompilerParams(vmem_limit_bytes=60 * 1024 * 1024),
        cost_estimate=pl.CostEstimate(flops=3 * 2 * 2048 * 1024 * 256, bytes_accessed=16 << 20, transcendentals=0),
        name="product",
    )(inv, flags, wt, rows, sym, front, child)


def body(child_update, parent_front, row_map, col_map):
    half = lax.axis_index("half")
    row = lax.axis_index("row")
    col = lax.axis_index("col")
    strip = half * 8 + col
    targets = jnp.arange(W // BLK, dtype=jnp.int32)
    own_columns = lax.dynamic_index_in_dim(col_map, half, 0, keepdims=False)
    match = (own_columns[:, None] == targets[None, :]).astype(jnp.int32)
    source = jnp.sum(match * jnp.arange(8, dtype=jnp.int32)[:, None], 0)
    hit = jnp.sum(match, 0)
    rows = jnp.concatenate([row_map[:, 0] - row * 16, jnp.where(half == 0, 1, 0)[None]]).astype(jnp.int32)
    strips, wide = prep(child_update[0], parent_front, source, hit, rows)

    pieces = lax.all_to_all(strips, PLANE, 0, 0, tiled=True)
    where = pieces[1::2, 0, BLK : 3 * BLK : BLK].T.astype(jnp.int32)
    core = row % 2
    chip = (row // 2)[None]
    place = jnp.stack([core, strip]).astype(jnp.int32)
    swap = [(i, i ^ 1) for i in range(16)]
    a_strip, keep, give = assemble_strip(pieces, where, place)

    start, wanted = share(place, keep, lax.ppermute(give, "row", swap))
    halves = [lax.ppermute(start, "row", [(0, 2 * z), (1, 2 * z + 1)]) for z in range(1, 8)]
    spread = pick(chip, [start] + halves, copies=16)

    matching = lax.all_to_all(wanted, PLANE, 0, 0, tiled=True)
    child = lax.all_to_all(wide, PLANE, 0, 0, tiled=True)
    late_strip, spread = lax.optimization_barrier((a_strip, spread))
    a_turned = lax.all_gather(late_strip, PLANE, axis=0, tiled=True)
    spread, matching, child = lax.optimization_barrier((spread, matching, child))
    gathered = lax.all_to_all(spread, PLANE, 0, 0, tiled=True)
    other = lax.ppermute(gathered, "row", swap)
    parent_then, _ = lax.optimization_barrier((parent_front, spread))
    turned_parent = turn(parent_then)

    def along(x, pairs):
        return lax.ppermute(x, "row", [(2 * i + n, 2 * j + n) for i, j in pairs for n in range(2)])

    mine = jnp.where(row < 2, matching, 0.0)
    to_3, to_6 = along(matching, [(0, 3)]), along(matching, [(0, 6)])
    to_3, to_6, turned_parent = lax.optimization_barrier((to_3, to_6, turned_parent))
    relay = mine + (to_3 + to_6)
    gathered, relay, turned_parent = lax.optimization_barrier((gathered, relay, turned_parent))
    front = lax.all_to_all(turned_parent, "col", 0, 0, tiled=True)
    last = [along(relay, [(0, 1), (3, 4), (6, 7)]), along(relay, [(3, 2), (6, 5)])]
    sym, mh, ml, rest, cross = first_half(place, gathered, other)

    rest, relay, *last = lax.optimization_barrier((rest, relay, *last))
    c_turned = relay + (last[0] + last[1])
    d_turned = lax.ppermute(c_turned, "row", swap)
    wt = second_half(place, rest, cross, mh, ml, c_turned, d_turned)

    blocks = jnp.arange(16, dtype=jnp.int32)
    order = jnp.arange(8, dtype=jnp.int32)
    inv = jnp.max(jnp.where(where[:, :, None] == blocks[None, None, :], order[None, :, None], -1), axis=1)
    flags = jnp.stack([(row == 0).astype(jnp.int32), (strip < 4).astype(jnp.int32)])
    return product(inv, flags, wt, a_turned, sym, front, child)


def solution(mesh):
    return jax.shard_map(
        body,
        mesh=mesh,
        in_specs=(
            P("half", ("row", "col"), None),
            P(("row", "col"), "half"),
            P(None, ("row", "col")),
            P(),
        ),
        out_specs=P("row", ("half", "col")),
        check_vma=False,
    )
```

time: 249 us -> 269 us (1.080)
  blocking collectives: 29.1 us -> 57.3 us
  starting transfers between devices: 49 us -> 39.9 us
  other arithmetic: 10.7 us -> 5.12 us
  waiting for transfers between devices: 67.6 us -> 73 us
  local copies, waits for them, and re-layouts: 11.1 us -> 8.34 us
    all_to_all x1 -> x2, blocking collectives: 29.1 us -> 57.3 us  [the longest x1 41.5 us: body(): child = lax.all_to_all(wide, PLANE, 0, 0, tiled=True)]
    select_n x4 -> x0, other arithmetic: 6.93 us -> none  [the longest x1 4.61 us: body(): spread_c = jnp.where(row < 2, matching, sum(sent[1:], sent[0]))]
    all_to_all x4 -> x3, waiting for transfers between devices: 58.9 us -> 65.8 us  [the longest x1 44.4 us: body(): gathered = lax.all_to_all(spread, PLANE, 0, 0, tiled=True)]
    ppermute x17 -> x14, starting transfers between devices: 28 us -> 22.6 us  [the longest x7 15.8 us: body(): lax.ppermute(start, 'row', [(0, 2 * z), (1, 2 * z + 1)])]
    pallas_call x3 -> x7, Pallas kernels: 63.4 us -> 67.2 us  [the longest x1 25 us: first_half(): pl.pallas_call(first_kernel, in_specs=[pl.BlockSpec(memory_space=pltpu.SM...]
    all_to_all x4 -> x3, starting transfers between devices: 21 us -> 17.3 us  [the longest x1 7.71 us: body(): pieces = lax.all_to_all(strips, PLANE, 0, 0, tiled=True)]
    unnamed x21 -> x24, local copies, waits for them, and re-layouts: 4.21 us -> 7.57 us
    add x0 -> x2, other arithmetic: none -> 2.97 us  [the longest x1 1.6 us: body(): relay = mine + (to_3 + to_6)]
  transfers between devices with their start and end apart: 22 -> 18, of which waited for: 7 -> 7; matrix products, arithmetic and copies ran while one was open for 6% -> 2% of each run, Pallas kernels for 20% -> 19%
where the time goes in v3:
time: 269 us; the launch traced here: 267 us
  waiting for transfers between devices  73 us (27%)
  Pallas kernels  69.3 us (26%)
  blocking collectives  57.3 us (21%)
  starting transfers between devices  39.9 us (15%)
  between operations  13.7 us (5%)
  local copies, waits for them, and re-layouts  8.34 us (3%)
  other arithmetic  5.12 us (2%)
    all_to_all x1, waiting for transfers between devices, body(): gathered = lax.all_to_all(spread, PLANE, 0, 0, tiled=True)  44.4 us
    all_to_all x1, blocking collectives, body(): child = lax.all_to_all(wide, PLANE, 0, 0, tiled=True)  41.5 us
    pallas_call x1, Pallas kernels, first_half(): pl.pallas_call(first_kernel, in_specs=[pl.BlockSpec(memory_space=pltpu.SM...  25 us
    pallas_call x1, Pallas kernels, second_half(): pl.pallas_call(second_kernel, in_specs=[pl.BlockSpec(memory_space=pltpu.S...  24.5 us
    all_to_all x1, waiting for transfers between devices, body(): pieces = lax.all_to_all(strips, PLANE, 0, 0, tiled=True)  21.4 us
    all_to_all x1, blocking collectives, body(): matching = lax.all_to_all(wanted, PLANE, 0, 0, tiled=True)  15.8 us
    ppermute x7, starting transfers between devices, body(): lax.ppermute(start, 'row', [(0, 2 * z), (1, 2 * z + 1)])  15.8 us
    pallas_call x1, Pallas kernels, product(): pl.pallas_call(product_kernel, grid_spec=pltpu.PrefetchScalarGridSpec(num...  13 us
  transfers between devices with their start and end apart: 18, of which 7 were waited for; matrix products, arithmetic and copies ran while one was open for 2% of the time, Pallas kernels for 19%

profile of v3, /device:TPU:2, one launch (start us, length us, event | category | flops | bytes accessed | tf_op | source)
XLA Modules:
  0.0 266.7 jit_solution(2410282951107496800)
XLA Ops:
  6.5 0.7 copy-done
  7.2 0.1 convert_reduce_fusion
  7.3 0.7 subtract_bitcast_fusion
  8.0 0.1 pad_add_fusion.rows_ref
  8.0 1.6 copy-done.1
  9.6 1.0 copy-done.6
  10.7 2.1 prep.1
  12.8 1.4 copy-done.3
  14.2 7.7 %all-to-all-start = ((f32[16,64,384]{2,1,0:T(8,128)}), f32[16,64,384]{2,1,0:T(8,128)S(1)}, u32[]{:S(2)}, u32[]{:S(2)}) async-start(f32[16,64,384]{2,1,0:T(8,128)} %get-tuple-element.33), calls=%async_computation | async-start | bytes 3145728 | tf_op jit(solution)/shard_map/all_to_all | solution.py:491
  22.0 21.4 %all-to-all-done.pieces_ref = f32[16,64,384]{2,1,0:T(8,128)S(1)} async-done(((f32[16,64,384]{2,1,0:T(8,128)}), f32[16,64,384]{2,1,0:T(8,128)S(1)}, u32[]{:S(2)}, u32[]{:S(2)}) %all-to-all-start) | async-done | bytes 1572896 | tf_op jit(solution)/shard_map/all_to_all | solution.py:491
  43.4 0.7 slice.3
  44.1 0.1 copy.7
  44.2 1.5 strip.1
  45.7 1.5 collective-permute-done.got_ref
  47.2 0.6 share.1
  47.8 4.0 %collective-permute-start.1 = (f32[32,1024]{1,0:T(8,128)S(1)}, f32[32,1024]{1,0:T(8,128)S(1)}, u32[]{:S(2)}, u32[]{:S(2)}) collective-permute-start(f32[32,1024]{1,0:T(8,128)S(1)} %get-tuple-element.37.refs_1_), channel_id=1, source_target_pairs={{0,16},{8,24},{1,17},{9,25},{2,18},{10,26},{3,19},{11,27},{4,20},{... | collective-permute-start | bytes 393224 | tf_op jit(solution)/shard_map/ppermute | solution.py:500
  51.8 2.0 collective-permute-start.2
  53.8 2.0 collective-permute-start.3
  55.9 3.2 %collective-permute-start.4 = (f32[32,1024]{1,0:T(8,128)S(1)}, f32[32,1024]{1,0:T(8,128)S(1)}, u32[]{:S(2)}, u32[]{:S(2)}) collective-permute-start(f32[32,1024]{1,0:T(8,128)S(1)} %get-tuple-element.37.refs_1_), channel_id=1, source_target_pairs={{0,64},{8,72},{1,65},{9,73},{2,66},{10,74},{3,67},{11,75},{4,68},{... | collective-permute-start | bytes 393224 | tf_op jit(solution)/shard_map/ppermute | solution.py:500
  59.1 1.3 collective-permute-start.5
  60.4 1.3 collective-permute-start.6
  61.7 1.9 collective-permute-start.7
  63.7 0.6 collective-permute-done.5.refs_6_
  64.2 2.8 %collective-permute-done.6.refs_7_ = f32[32,1024]{1,0:T(8,128)S(1)} collective-permute-done((f32[32,1024]{1,0:T(8,128)S(1)}, f32[32,1024]{1,0:T(8,128)S(1)}, u32[]{:S(2)}, u32[]{:S(2)}) %collective-permute-start.6) | collective-permute-done | bytes 131104 | tf_op jit(solution)/shard_map/ppermute | solution.py:500
  67.1 2.0 collective-permute-done.7.refs_8_
  69.1 2.4 pick.1
  71.5 41.5 %all_to_all.25.child_ref = f32[16,128,256]{2,1,0:T(8,128)} all-to-all(f32[16,128,256]{2,1,0:T(8,128)S(1)} %copy-done.4), channel_id=1, replica_groups=mesh['half'=2,'row'=16,'col'=8] {'col','half'}, dimensions={0} | all-to-all | bytes 4194304 | tf_op jit(solution)/shard_map/all_to_all | solution.py:504
  113.0 15.8 %all_to_all.26 = f32[16,32,256]{2,1,0:T(8,128)S(1)} all-to-all(f32[16,32,256]{2,1,0:T(8,128)S(1)} %get-tuple-element.39), channel_id=1, replica_groups=mesh['half'=2,'row'=16,'col'=8] {'col','half'}, dimensions={0} | all-to-all | bytes 1048576 | tf_op jit(solution)/shard_map/all_to_all | solution.py:503
  128.8 5.8 %all-to-all-start.3 = ((f32[16,32,1024]{2,1,0:T(8,128)}), f32[16,32,1024]{2,1,0:T(8,128)}, u32[]{:S(2)}, u32[]{:S(2)}) async-start(f32[16,32,1024]{2,1,0:T(8,128)} %pick.1), calls=%async_computation.3 | async-start | bytes 4194304 | tf_op jit(solution)/shard_map/all_to_all | solution.py:508
  134.6 1.3 collective-permute-start.8
  135.9 2.1 collective-permute-start.9
  138.0 44.4 %all-to-all-done.3.own_ref = f32[16,32,1024]{2,1,0:T(8,128)} async-done(((f32[16,32,1024]{2,1,0:T(8,128)}), f32[16,32,1024]{2,1,0:T(8,128)}, u32[]{:S(2)}, u32[]{:S(2)}) %all-to-all-start.3) | async-done | bytes 2097184 | tf_op jit(solution)/shard_map/all_to_all | solution.py:508
  182.4 0.1 turn.1
  182.6 1.6 add_add_fusion.1
  184.2 1.3 collective-permute-start.11
  185.6 1.5 collective-permute-start.12
  187.0 3.8 %all-to-all-start.4 = ((f32[8,256,256]{2,1,0:T(8,128)}), f32[8,256,256]{2,1,0:T(8,128)S(1)}, u32[]{:S(2)}, u32[]{:S(2)}) async-start(f32[8,256,256]{2,1,0:T(8,128)} %copy-done.5), calls=%async_computation.4 | async-start | bytes 4194304 | tf_op jit(solution)/shard_map/all_to_all | solution.py:521
  190.8 25.0 %first_half.1 = (f32[1024,1024]{1,0:T(8,128)}, bf16[512,512]{1,0:T(8,128)(2,1)}, bf16[512,512]{1,0:T(8,128)(2,1)}, f32[512,512]{1,0:T(8,128)}, f32[512,512]{1,0:T(8,128)}) custom-call(s32[2]{0:T(128)} %copy-done.7, f32[16,32,1024]{2,1,0:T(8,128)} %all-to-all-done.3.own_ref, f32[16,32,1024]{2,1,0:T(8,128)} %collective-permute-done.10.other_ref), custom_call_target="tpu_custom_call" | custom-call | flops 30000001024 | bytes 12582912 | tf_op jit(solution)/shard_map/first_half/pallas_call | solution.py:400
  215.9 0.8 copy-done.10
  216.7 1.4 add_add_fusion.c_in
  218.1 0.6 collective-permute-start.13
  218.7 0.6 add_convert_fusion.flags_ref
  219.3 0.7 select_reduce_fusion.inv_ref
  219.9 0.3 collective-permute-done.13.d_in
  220.2 0.8 copy-done.11
  221.0 24.5 %second_half.1.wt_ref = f32[256,1024]{1,0:T(8,128)} custom-call(s32[2]{0:T(128)} %copy-done.7, f32[512,512]{1,0:T(8,128)} %get-tuple-element.50.rest_in, f32[512,512]{1,0:T(8,128)} %get-tuple-element.51.cross_in, bf16[512,512]{1,0:T(8,128)(2,1)} %get-tuple-element.52.mh_in, bf16[512,512]{1,0:T(8,128)(2,1)} %get-tuple-element.53.ml_in, ...), custom_call_target="tpu_custom_call" | custom-call | flops 1000000000 | bytes 6291456 | tf_op jit(solution)/shard_map/second_half/pallas_call | solution.py:415
  245.5 1.3 copy-done.8
  246.8 13.0 %product.1 = f32[2048,256]{1,0:T(8,128)} custom-call(s32[2,16]{1,0:T(2,128)} %select_reduce_fusion.inv_ref, s32[2]{0:T(128)} %add_convert_fusion.flags_ref, f32[256,1024]{1,0:T(8,128)} %second_half.1.wt_ref, f32[1024,2048]{1,0:T(8,128)} %all-gather.2.cloned.1.call-done.rows_ref, f32[1024,1024]{1,0:T(8,128)} %get-tuple-element.58.sym_ref, ...), custom_call_target="tpu_custom_call" | custom-call | flops 3221225472 | bytes 16777216 | tf_op jit(solution)/shard_map/product/pallas_call | solution.py:456
  (35 shorter events, 0.2 us)
Async XLA Ops:
  6.5 0.7 copy-start
  8.0 1.6 copy-start.1
  9.6 1.0 copy-start.6
  12.8 1.4 copy-start.3
  14.2 29.2 %all-to-all-start = ((f32[16,64,384]{2,1,0:T(8,128)}), f32[16,64,384]{2,1,0:T(8,128)S(1)}, u32[]{:S(2)}, u32[]{:S(2)}) async-start(f32[16,64,384]{2,1,0:T(8,128)} %get-tuple-element.33), calls=%async_computation | async-start | bytes 3145728 | tf_op jit(solution)/shard_map/all_to_all | solution.py:491
  21.9 223.7 %all-gather.2.cloned.1.call-start = ((), (), s32[]{:S(2)}) async-start(), calls=%async_computation.5 | async-start | bytes 8912896 | tf_op jit(solution)/shard_map/all_gather | solution.py:506
  22.0 49.5 %copy-start.7 = (s32[2]{0:T(128)}, s32[2]{0:T(128)S(1)}, u32[]{:S(2)}) copy-start(s32[2]{0:T(128)S(1)} %pad_add_fusion.1.place_ref) | copy-start | bytes 28
  45.7 1.5 collective-permute-start
  47.2 24.3 %copy-start.4 = (f32[16,128,256]{2,1,0:T(8,128)S(1)}, f32[16,128,256]{2,1,0:T(8,128)}, u32[]{:S(2)}) copy-start(f32[16,128,256]{2,1,0:T(8,128)} %copy-done.3) | copy-start | bytes 6291460
  47.8 12.6 %collective-permute-start.1 = (f32[32,1024]{1,0:T(8,128)S(1)}, f32[32,1024]{1,0:T(8,128)S(1)}, u32[]{:S(2)}, u32[]{:S(2)}) collective-permute-start(f32[32,1024]{1,0:T(8,128)S(1)} %get-tuple-element.37.refs_1_), channel_id=1, source_target_pairs={{0,16},{8,24},{1,17},{9,25},{2,18},{10,26},{3,19},{11,27},{4,20},{... | collective-permute-start | bytes 393224 | tf_op jit(solution)/shard_map/ppermute | solution.py:500
  51.8 9.9 %collective-permute-start.2 = (f32[32,1024]{1,0:T(8,128)S(1)}, f32[32,1024]{1,0:T(8,128)S(1)}, u32[]{:S(2)}, u32[]{:S(2)}) collective-permute-start(f32[32,1024]{1,0:T(8,128)S(1)} %get-tuple-element.37.refs_1_), channel_id=1, source_target_pairs={{0,32},{8,40},{1,33},{9,41},{2,34},{10,42},{3,35},{11,43},{4,36},{... | collective-permute-start | bytes 393224 | tf_op jit(solution)/shard_map/ppermute | solution.py:500
  53.8 9.9 %collective-permute-start.3 = (f32[32,1024]{1,0:T(8,128)S(1)}, f32[32,1024]{1,0:T(8,128)S(1)}, u32[]{:S(2)}, u32[]{:S(2)}) collective-permute-start(f32[32,1024]{1,0:T(8,128)S(1)} %get-tuple-element.37.refs_1_), channel_id=1, source_target_pairs={{0,48},{8,56},{1,49},{9,57},{2,50},{10,58},{3,51},{11,59},{4,52},{... | collective-permute-start | bytes 393224 | tf_op jit(solution)/shard_map/ppermute | solution.py:500
  55.9 7.8 %collective-permute-start.4 = (f32[32,1024]{1,0:T(8,128)S(1)}, f32[32,1024]{1,0:T(8,128)S(1)}, u32[]{:S(2)}, u32[]{:S(2)}) collective-permute-start(f32[32,1024]{1,0:T(8,128)S(1)} %get-tuple-element.37.refs_1_), channel_id=1, source_target_pairs={{0,64},{8,72},{1,65},{9,73},{2,66},{10,74},{3,67},{11,75},{4,68},{... | collective-permute-start | bytes 393224 | tf_op jit(solution)/shard_map/ppermute | solution.py:500
  59.1 5.1 %collective-permute-start.5 = (f32[32,1024]{1,0:T(8,128)S(1)}, f32[32,1024]{1,0:T(8,128)S(1)}, u32[]{:S(2)}, u32[]{:S(2)}) collective-permute-start(f32[32,1024]{1,0:T(8,128)S(1)} %get-tuple-element.37.refs_1_), channel_id=1, source_target_pairs={{0,80},{8,88},{1,81},{9,89},{2,82},{10,90},{3,83},{11,91},{4,84},{... | collective-permute-start | bytes 393224 | tf_op jit(solution)/shard_map/ppermute | solution.py:500
  60.4 6.6 %collective-permute-start.6 = (f32[32,1024]{1,0:T(8,128)S(1)}, f32[32,1024]{1,0:T(8,128)S(1)}, u32[]{:S(2)}, u32[]{:S(2)}) collective-permute-start(f32[32,1024]{1,0:T(8,128)S(1)} %get-tuple-element.37.refs_1_), channel_id=1, source_target_pairs={{0,96},{8,104},{1,97},{9,105},{2,98},{10,106},{3,99},{11,107},{4,1... | collective-permute-start | bytes 393224 | tf_op jit(solution)/shard_map/ppermute | solution.py:500
  61.7 7.3 %collective-permute-start.7 = (f32[32,1024]{1,0:T(8,128)S(1)}, f32[32,1024]{1,0:T(8,128)}, u32[]{:S(2)}, u32[]{:S(2)}) collective-permute-start(f32[32,1024]{1,0:T(8,128)S(1)} %get-tuple-element.37.refs_1_), channel_id=1, source_target_pairs={{0,112},{8,120},{1,113},{9,121},{2,114},{10,122},{3,115},{11,123},... | collective-permute-start | bytes 393224 | tf_op jit(solution)/shard_map/ppermute | solution.py:500
  128.8 53.6 %copy-start.2 = (f32[256,2048]{1,0:T(8,128)S(1)}, f32[256,2048]{1,0:T(8,128)}, u32[]{:S(2)}) copy-start(f32[256,2048]{1,0:T(8,128)} %parent_ref.2) | copy-start | bytes 6291460
  128.8 53.6 %all-to-all-start.3 = ((f32[16,32,1024]{2,1,0:T(8,128)}), f32[16,32,1024]{2,1,0:T(8,128)}, u32[]{:S(2)}, u32[]{:S(2)}) async-start(f32[16,32,1024]{2,1,0:T(8,128)} %pick.1), calls=%async_computation.3 | async-start | bytes 4194304 | tf_op jit(solution)/shard_map/all_to_all | solution.py:508
  134.6 48.0 %collective-permute-start.8 = (f32[16,32,256]{2,1,0:T(8,128)S(1)}, f32[16,32,256]{2,1,0:T(8,128)S(1)}, u32[]{:S(2)}, u32[]{:S(2)}) collective-permute-start(f32[16,32,256]{2,1,0:T(8,128)S(1)} %all_to_all.26), channel_id=1, source_target_pairs={{0,48},{8,56},{1,49},{9,57},{2,50},{10,58},{3,51},{11,59},{4,52},{... | collective-permute-start | bytes 1572872 | tf_op jit(solution)/shard_map/ppermute | solution.py:514
  135.9 46.7 %collective-permute-start.9 = (f32[16,32,256]{2,1,0:T(8,128)S(1)}, f32[16,32,256]{2,1,0:T(8,128)}, u32[]{:S(2)}, u32[]{:S(2)}) collective-permute-start(f32[16,32,256]{2,1,0:T(8,128)S(1)} %all_to_all.26), channel_id=1, source_target_pairs={{0,96},{8,104},{1,97},{9,105},{2,98},{10,106},{3,99},{11,107},{4,1... | collective-permute-start | bytes 1572872 | tf_op jit(solution)/shard_map/ppermute | solution.py:514
  182.4 8.4 %collective-permute-start.10 = (f32[16,32,1024]{2,1,0:T(8,128)}, f32[16,32,1024]{2,1,0:T(8,128)}, u32[]{:S(2)}, u32[]{:S(2)}) collective-permute-start(f32[16,32,1024]{2,1,0:T(8,128)} %all-to-all-done.3.own_ref), channel_id=1, source_target_pairs={{0,8},{8,0},{16,24},{24,16},{32,40},{40,32},{48,56},{56,48},{64,72... | collective-permute-start | bytes 6291464 | tf_op jit(solution)/shard_map/ppermute | solution.py:509
  182.6 3.0 %copy-start.5 = (f32[8,256,256]{2,1,0:T(8,128)}, f32[8,256,256]{2,1,0:T(8,128)S(1)}, u32[]{:S(2)}) copy-start(f32[8,256,256]{2,1,0:T(8,128)S(1)} %turn.1) | copy-start | bytes 6291460
  184.2 31.7 %collective-permute-start.11 = (f32[16,32,256]{2,1,0:T(8,128)S(1)}, f32[16,32,256]{2,1,0:T(8,128)S(1)}, u32[]{:S(2)}, u32[]{:S(2)}) collective-permute-start(f32[16,32,256]{2,1,0:T(8,128)S(1)} %add_add_fusion.1), channel_id=1, source_target_pairs={{0,16},{8,24},{48,64},{56,72},{96,112},{104,120},{1,17},{9,25},{49... | collective-permute-start | bytes 1572872 | tf_op jit(solution)/shard_map/ppermute | solution.py:514
  185.6 30.3 %collective-permute-start.12 = (f32[16,32,256]{2,1,0:T(8,128)S(1)}, f32[16,32,256]{2,1,0:T(8,128)}, u32[]{:S(2)}, u32[]{:S(2)}) collective-permute-start(f32[16,32,256]{2,1,0:T(8,128)S(1)} %add_add_fusion.1), channel_id=1, source_target_pairs={{48,32},{56,40},{96,80},{104,88},{49,33},{57,41},{97,81},{105,89},... | collective-permute-start | bytes 1572872 | tf_op jit(solution)/shard_map/ppermute | solution.py:514
  187.0 58.5 %all-to-all-start.4 = ((f32[8,256,256]{2,1,0:T(8,128)}), f32[8,256,256]{2,1,0:T(8,128)S(1)}, u32[]{:S(2)}, u32[]{:S(2)}) async-start(f32[8,256,256]{2,1,0:T(8,128)} %copy-done.5), calls=%async_computation.4 | async-start | bytes 4194304 | tf_op jit(solution)/shard_map/all_to_all | solution.py:521
  215.9 0.8 copy-start.10
  218.1 2.2 copy-start.9
  218.1 2.1 collective-permute-start.13
  220.2 0.8 copy-start.11
  245.5 1.3 copy-start.8
Sparse Core Ops, SparseCore 0:
  71.6 109.1 all-gather.1

commit v4 on v3

--- a/solution.py
+++ b/solution.py
@@ -421,7 +421,7 @@
         + [pltpu.VMEM(x.shape, x.dtype) for x in arrays]
         + [pltpu.VMEM((NB, 256), jnp.float32), pltpu.SemaphoreType.DMA((6,))],
         compiler_params=pltpu.CompilerParams(vmem_limit_bytes=60 * 1024 * 1024),
-        cost_estimate=pl.CostEstimate(flops=1_000_000_000, bytes_accessed=6 << 20, transcendentals=0),
+        cost_estimate=pl.CostEstimate(flops=30_000_000_000, bytes_accessed=6 << 20, transcendentals=0),
         name="second_half",
     )(place, *arrays)
 

time: 269 us -> 217 us (0.81)
  waiting for transfers between devices: 73 us -> 30.4 us
  blocking collectives: 57.3 us -> 45.7 us
  starting transfers between devices: 39.9 us -> 48 us
    all_to_all x1, waiting for transfers between devices: 44.4 us -> 19.3 us  [body(): gathered = lax.all_to_all(spread, PLANE, 0, 0, tiled=True)]
    all_to_all x1, waiting for transfers between devices: 21.4 us -> 0.01 us  [body(): child = lax.all_to_all(wide, PLANE, 0, 0, tiled=True)]
    all_to_all x1, blocking collectives: 41.5 us -> 28.9 us  [body(): pieces = lax.all_to_all(strips, PLANE, 0, 0, tiled=True)]
    ppermute x4, starting transfers between devices: 6.23 us -> 12.9 us  [along(): lax.ppermute(x, 'row', [(2 * i + n, 2 * j + n) for i, j in pairs for n in...]
    all_to_all x1, starting transfers between devices: 3.79 us -> 8.36 us  [body(): front = lax.all_to_all(turned_parent, 'col', 0, 0, tiled=True)]
    all_to_all x1, waiting for transfers between devices: 0.01 us -> 3.47 us  [body(): front = lax.all_to_all(turned_parent, 'col', 0, 0, tiled=True)]
    unnamed x24 -> x18, local copies, waits for them, and re-layouts: 7.57 us -> 5.44 us
  transfers between devices with their start and end apart: 18 -> 18, of which waited for: 7 -> 7; matrix products, arithmetic and copies ran while one was open for 2% -> 2% of each run, Pallas kernels for 19% -> 25%
where the time goes in v4:
time: 217 us; the launch traced here: 216 us
  Pallas kernels  68.6 us (32%)
  starting transfers between devices  48 us (22%)
  blocking collectives  45.7 us (21%)
  waiting for transfers between devices  30.4 us (14%)
  between operations  13.7 us (6%)
  local copies, waits for them, and re-layouts  6.24 us (3%)
  other arithmetic  3.46 us (2%)
    all_to_all x1, blocking collectives, body(): pieces = lax.all_to_all(strips, PLANE, 0, 0, tiled=True)  28.9 us
    pallas_call x1, Pallas kernels, first_half(): pl.pallas_call(first_kernel, in_specs=[pl.BlockSpec(memory_space=pltpu.SM...  25.1 us
    pallas_call x1, Pallas kernels, second_half(): pl.pallas_call(second_kernel, in_specs=[pl.BlockSpec(memory_space=pltpu.S...  24.5 us
    all_to_all x1, waiting for transfers between devices, body(): gathered = lax.all_to_all(spread, PLANE, 0, 0, tiled=True)  19.3 us
    all_to_all x1, blocking collectives, body(): matching = lax.all_to_all(wanted, PLANE, 0, 0, tiled=True)  16.8 us
    ppermute x7, starting transfers between devices, body(): lax.ppermute(start, 'row', [(0, 2 * z), (1, 2 * z + 1)])  15 us
    pallas_call x1, Pallas kernels, product(): pl.pallas_call(product_kernel, grid_spec=pltpu.PrefetchScalarGridSpec(num...  13 us
    ppermute x4, starting transfers between devices, along(): lax.ppermute(x, 'row', [(2 * i + n, 2 * j + n) for i, j in pairs for n in...  12.9 us
  transfers between devices with their start and end apart: 18, of which 7 were waited for; matrix products, arithmetic and copies ran while one was open for 2% of the time, Pallas kernels for 25%

profile of v4, /device:TPU:2, one launch (start us, length us, event | category | flops | bytes accessed | tf_op | source)
XLA Modules:
  0.0 216.1 jit_solution(12264753047679876290)
XLA Ops:
  6.5 0.7 copy-done
  7.2 0.1 convert_reduce_fusion
  7.3 0.7 subtract_bitcast_fusion
  8.0 0.1 pad_add_fusion.rows_ref
  8.0 1.6 copy-done.1
  9.6 1.0 copy-done.4
  10.7 1.0 prep.1
  11.7 28.9 %all_to_all.25.pieces_ref = f32[16,64,384]{2,1,0:T(8,128)S(1)} all-to-all(f32[16,64,384]{2,1,0:T(8,128)S(1)} %get-tuple-element.33), channel_id=1, replica_groups=mesh['half'=2,'row'=16,'col'=8] {'col','half'}, dimensions={0} | all-to-all | bytes 3145728 | tf_op jit(solution)/shard_map/all_to_all | solution.py:491
  40.6 5.6 %all-to-all-start.2 = ((f32[16,128,256]{2,1,0:T(8,128)}), f32[16,128,256]{2,1,0:T(8,128)}, u32[]{:S(2)}, u32[]{:S(2)}) async-start(f32[16,128,256]{2,1,0:T(8,128)} %copy-done.3), calls=%async_computation.2 | async-start | bytes 4194304 | tf_op jit(solution)/shard_map/all_to_all | solution.py:504
  46.2 0.0 all-gather.2.cloned.1.call-start
  46.3 0.1 pad_add_fusion.1.place_ref
  46.4 0.7 slice.3
  47.1 0.1 copy.7
  47.2 1.5 strip.1
  48.7 1.5 collective-permute-done.got_ref
  50.2 0.6 share.1
  50.8 3.8 %collective-permute-start.1 = (f32[32,1024]{1,0:T(8,128)S(1)}, f32[32,1024]{1,0:T(8,128)S(1)}, u32[]{:S(2)}, u32[]{:S(2)}) collective-permute-start(f32[32,1024]{1,0:T(8,128)S(1)} %get-tuple-element.37.refs_1_), channel_id=1, source_target_pairs={{0,16},{8,24},{1,17},{9,25},{2,18},{10,26},{3,19},{11,27},{4,20},{... | collective-permute-start | bytes 393224 | tf_op jit(solution)/shard_map/ppermute | solution.py:500
  54.6 2.0 collective-permute-start.2
  56.7 2.0 collective-permute-start.3
  58.7 3.2 %collective-permute-start.4 = (f32[32,1024]{1,0:T(8,128)S(1)}, f32[32,1024]{1,0:T(8,128)S(1)}, u32[]{:S(2)}, u32[]{:S(2)}) collective-permute-start(f32[32,1024]{1,0:T(8,128)S(1)} %get-tuple-element.37.refs_1_), channel_id=1, source_target_pairs={{0,64},{8,72},{1,65},{9,73},{2,66},{10,74},{3,67},{11,75},{4,68},{... | collective-permute-start | bytes 393224 | tf_op jit(solution)/shard_map/ppermute | solution.py:500
  61.9 1.3 collective-permute-start.5
  63.3 1.3 collective-permute-start.6
  64.6 1.3 collective-permute-start.7
  65.9 0.2 collective-permute-done.4.refs_5_
  66.1 1.0 collective-permute-done.5.refs_6_
  67.1 2.8 %collective-permute-done.6.refs_7_ = f32[32,1024]{1,0:T(8,128)S(1)} collective-permute-done((f32[32,1024]{1,0:T(8,128)S(1)}, f32[32,1024]{1,0:T(8,128)S(1)}, u32[]{:S(2)}, u32[]{:S(2)}) %collective-permute-start.6) | collective-permute-done | bytes 131104 | tf_op jit(solution)/shard_map/ppermute | solution.py:500
  69.9 2.0 collective-permute-done.7.refs_8_
  71.9 1.5 pick.1
  73.4 16.8 %all_to_all.26 = f32[16,32,256]{2,1,0:T(8,128)S(1)} all-to-all(f32[16,32,256]{2,1,0:T(8,128)S(1)} %get-tuple-element.39), channel_id=1, replica_groups=mesh['half'=2,'row'=16,'col'=8] {'col','half'}, dimensions={0} | all-to-all | bytes 1048576 | tf_op jit(solution)/shard_map/all_to_all | solution.py:503
  90.3 5.7 %all-to-all-start.3 = ((f32[16,32,1024]{2,1,0:T(8,128)}), f32[16,32,1024]{2,1,0:T(8,128)}, u32[]{:S(2)}, u32[]{:S(2)}) async-start(f32[16,32,1024]{2,1,0:T(8,128)} %pick.1), calls=%async_computation.3 | async-start | bytes 4194304 | tf_op jit(solution)/shard_map/all_to_all | solution.py:508
  96.0 5.5 %collective-permute-start.8 = (f32[16,32,256]{2,1,0:T(8,128)S(1)}, f32[16,32,256]{2,1,0:T(8,128)S(1)}, u32[]{:S(2)}, u32[]{:S(2)}) collective-permute-start(f32[16,32,256]{2,1,0:T(8,128)S(1)} %all_to_all.26), channel_id=1, source_target_pairs={{0,48},{8,56},{1,49},{9,57},{2,50},{10,58},{3,51},{11,59},{4,52},{... | collective-permute-start | bytes 1572872 | tf_op jit(solution)/shard_map/ppermute | solution.py:514
  101.5 3.6 %collective-permute-start.9 = (f32[16,32,256]{2,1,0:T(8,128)S(1)}, f32[16,32,256]{2,1,0:T(8,128)}, u32[]{:S(2)}, u32[]{:S(2)}) collective-permute-start(f32[16,32,256]{2,1,0:T(8,128)S(1)} %all_to_all.26), channel_id=1, source_target_pairs={{0,96},{8,104},{1,97},{9,105},{2,98},{10,106},{3,99},{11,107},{4,1... | collective-permute-start | bytes 1572872 | tf_op jit(solution)/shard_map/ppermute | solution.py:514
  105.1 19.3 %all-to-all-done.3.own_ref = f32[16,32,1024]{2,1,0:T(8,128)} async-done(((f32[16,32,1024]{2,1,0:T(8,128)}), f32[16,32,1024]{2,1,0:T(8,128)}, u32[]{:S(2)}, u32[]{:S(2)}) %all-to-all-start.3) | async-done | bytes 2097184 | tf_op jit(solution)/shard_map/all_to_all | solution.py:508
  124.5 1.5 turn.1
  125.9 1.1 add_add_fusion.1
  127.1 2.9 %collective-permute-start.11 = (f32[16,32,256]{2,1,0:T(8,128)S(1)}, f32[16,32,256]{2,1,0:T(8,128)S(1)}, u32[]{:S(2)}, u32[]{:S(2)}) collective-permute-start(f32[16,32,256]{2,1,0:T(8,128)S(1)} %add_add_fusion.1), channel_id=1, source_target_pairs={{0,16},{8,24},{48,64},{56,72},{96,112},{104,120},{1,17},{9,25},{49... | collective-permute-start | bytes 1572872 | tf_op jit(solution)/shard_map/ppermute | solution.py:514
  130.0 0.9 collective-permute-start.12
  130.9 25.1 %first_half.1 = (f32[1024,1024]{1,0:T(8,128)}, bf16[512,512]{1,0:T(8,128)(2,1)}, bf16[512,512]{1,0:T(8,128)(2,1)}, f32[512,512]{1,0:T(8,128)}, f32[512,512]{1,0:T(8,128)}) custom-call(s32[2]{0:T(128)} %copy-done.5, f32[16,32,1024]{2,1,0:T(8,128)} %all-to-all-done.3.own_ref, f32[16,32,1024]{2,1,0:T(8,128)} %collective-permute-done.10.other_ref), custom_call_target="tpu_custom_call" | custom-call | flops 30000001024 | bytes 12582912 | tf_op jit(solution)/shard_map/first_half/pallas_call | solution.py:400
  156.0 0.1 add_add_fusion.c_in
  156.1 0.3 collective-permute-start.13
  156.4 0.6 add_convert_fusion.flags_ref
  157.1 0.7 select_reduce_fusion.inv_ref
  157.8 8.4 %all-to-all-start.4 = ((f32[8,256,256]{2,1,0:T(8,128)}), f32[8,256,256]{2,1,0:T(8,128)S(1)}, u32[]{:S(2)}, u32[]{:S(2)}) async-start(f32[8,256,256]{2,1,0:T(8,128)} %turn.1), calls=%async_computation.4 | async-start | bytes 4194304 | tf_op jit(solution)/shard_map/all_to_all | solution.py:521
  166.1 0.8 copy-done.8
  166.9 24.5 %second_half.1.wt_ref = f32[256,1024]{1,0:T(8,128)} custom-call(s32[2]{0:T(128)} %copy-done.5, f32[512,512]{1,0:T(8,128)} %get-tuple-element.50.rest_in, f32[512,512]{1,0:T(8,128)} %get-tuple-element.51.cross_in, bf16[512,512]{1,0:T(8,128)(2,1)} %get-tuple-element.52.mh_in, bf16[512,512]{1,0:T(8,128)(2,1)} %get-tuple-element.53.ml_in, ...), custom_call_target="tpu_custom_call" | custom-call | flops 30000001024 | bytes 6291456 | tf_op jit(solution)/shard_map/second_half/pallas_call | solution.py:415
  191.4 3.5 %all-to-all-done.4.front_ref = f32[8,256,256]{2,1,0:T(8,128)S(1)} async-done(((f32[8,256,256]{2,1,0:T(8,128)}), f32[8,256,256]{2,1,0:T(8,128)S(1)}, u32[]{:S(2)}, u32[]{:S(2)}) %all-to-all-start.4) | async-done | bytes 2097184 | tf_op jit(solution)/shard_map/all_to_all | solution.py:521
  194.9 1.3 copy-done.6
  196.2 13.0 %product.1 = f32[2048,256]{1,0:T(8,128)} custom-call(s32[2,16]{1,0:T(2,128)} %select_reduce_fusion.inv_ref, s32[2]{0:T(128)} %add_convert_fusion.flags_ref, f32[256,1024]{1,0:T(8,128)} %second_half.1.wt_ref, f32[1024,2048]{1,0:T(8,128)} %all-gather.2.cloned.1.call-done.rows_ref, f32[1024,1024]{1,0:T(8,128)} %get-tuple-element.58.sym_ref, ...), custom_call_target="tpu_custom_call" | custom-call | flops 3221225472 | bytes 16777216 | tf_op jit(solution)/shard_map/product/pallas_call | solution.py:456
  (29 shorter events, 0.1 us)
Async XLA Ops:
  6.5 0.7 copy-start
  8.0 1.6 copy-start.1
  9.6 1.0 copy-start.4
  11.7 28.9 %copy-start.3 = (f32[16,128,256]{2,1,0:T(8,128)}, f32[16,128,256]{2,1,0:T(8,128)S(1)}, u32[]{:S(2)}) copy-start(f32[16,128,256]{2,1,0:T(8,128)S(1)} %get-tuple-element.40) | copy-start | bytes 6291460
  40.6 32.9 %all-to-all-start.2 = ((f32[16,128,256]{2,1,0:T(8,128)}), f32[16,128,256]{2,1,0:T(8,128)}, u32[]{:S(2)}, u32[]{:S(2)}) async-start(f32[16,128,256]{2,1,0:T(8,128)} %copy-done.3), calls=%async_computation.2 | async-start | bytes 4194304 | tf_op jit(solution)/shard_map/all_to_all | solution.py:504
  46.2 148.7 %all-gather.2.cloned.1.call-start = ((), (), s32[]{:S(2)}) async-start(), calls=%async_computation.5 | async-start | bytes 8912896 | tf_op jit(solution)/shard_map/all_gather | solution.py:506
  46.3 27.1 %copy-start.5 = (s32[2]{0:T(128)}, s32[2]{0:T(128)S(1)}, u32[]{:S(2)}) copy-start(s32[2]{0:T(128)S(1)} %pad_add_fusion.1.place_ref) | copy-start | bytes 28
  48.7 1.5 collective-permute-start
  50.8 12.4 %collective-permute-start.1 = (f32[32,1024]{1,0:T(8,128)S(1)}, f32[32,1024]{1,0:T(8,128)S(1)}, u32[]{:S(2)}, u32[]{:S(2)}) collective-permute-start(f32[32,1024]{1,0:T(8,128)S(1)} %get-tuple-element.37.refs_1_), channel_id=1, source_target_pairs={{0,16},{8,24},{1,17},{9,25},{2,18},{10,26},{3,19},{11,27},{4,20},{... | collective-permute-start | bytes 393224 | tf_op jit(solution)/shard_map/ppermute | solution.py:500
  54.6 9.9 %collective-permute-start.2 = (f32[32,1024]{1,0:T(8,128)S(1)}, f32[32,1024]{1,0:T(8,128)S(1)}, u32[]{:S(2)}, u32[]{:S(2)}) collective-permute-start(f32[32,1024]{1,0:T(8,128)S(1)} %get-tuple-element.37.refs_1_), channel_id=1, source_target_pairs={{0,32},{8,40},{1,33},{9,41},{2,34},{10,42},{3,35},{11,43},{4,36},{... | collective-permute-start | bytes 393224 | tf_op jit(solution)/shard_map/ppermute | solution.py:500
  56.7 9.2 %collective-permute-start.3 = (f32[32,1024]{1,0:T(8,128)S(1)}, f32[32,1024]{1,0:T(8,128)S(1)}, u32[]{:S(2)}, u32[]{:S(2)}) collective-permute-start(f32[32,1024]{1,0:T(8,128)S(1)} %get-tuple-element.37.refs_1_), channel_id=1, source_target_pairs={{0,48},{8,56},{1,49},{9,57},{2,50},{10,58},{3,51},{11,59},{4,52},{... | collective-permute-start | bytes 393224 | tf_op jit(solution)/shard_map/ppermute | solution.py:500
  58.7 7.4 %collective-permute-start.4 = (f32[32,1024]{1,0:T(8,128)S(1)}, f32[32,1024]{1,0:T(8,128)S(1)}, u32[]{:S(2)}, u32[]{:S(2)}) collective-permute-start(f32[32,1024]{1,0:T(8,128)S(1)} %get-tuple-element.37.refs_1_), channel_id=1, source_target_pairs={{0,64},{8,72},{1,65},{9,73},{2,66},{10,74},{3,67},{11,75},{4,68},{... | collective-permute-start | bytes 393224 | tf_op jit(solution)/shard_map/ppermute | solution.py:500
  61.9 5.1 %collective-permute-start.5 = (f32[32,1024]{1,0:T(8,128)S(1)}, f32[32,1024]{1,0:T(8,128)S(1)}, u32[]{:S(2)}, u32[]{:S(2)}) collective-permute-start(f32[32,1024]{1,0:T(8,128)S(1)} %get-tuple-element.37.refs_1_), channel_id=1, source_target_pairs={{0,80},{8,88},{1,81},{9,89},{2,82},{10,90},{3,83},{11,91},{4,84},{... | collective-permute-start | bytes 393224 | tf_op jit(solution)/shard_map/ppermute | solution.py:500
  63.3 6.6 %collective-permute-start.6 = (f32[32,1024]{1,0:T(8,128)S(1)}, f32[32,1024]{1,0:T(8,128)S(1)}, u32[]{:S(2)}, u32[]{:S(2)}) collective-permute-start(f32[32,1024]{1,0:T(8,128)S(1)} %get-tuple-element.37.refs_1_), channel_id=1, source_target_pairs={{0,96},{8,104},{1,97},{9,105},{2,98},{10,106},{3,99},{11,107},{4,1... | collective-permute-start | bytes 393224 | tf_op jit(solution)/shard_map/ppermute | solution.py:500
  64.6 7.3 %collective-permute-start.7 = (f32[32,1024]{1,0:T(8,128)S(1)}, f32[32,1024]{1,0:T(8,128)S(1)}, u32[]{:S(2)}, u32[]{:S(2)}) collective-permute-start(f32[32,1024]{1,0:T(8,128)S(1)} %get-tuple-element.37.refs_1_), channel_id=1, source_target_pairs={{0,112},{8,120},{1,113},{9,121},{2,114},{10,122},{3,115},{11,123},... | collective-permute-start | bytes 393224 | tf_op jit(solution)/shard_map/ppermute | solution.py:500
  90.3 34.2 %copy-start.2 = (f32[256,2048]{1,0:T(8,128)S(1)}, f32[256,2048]{1,0:T(8,128)}, u32[]{:S(2)}) copy-start(f32[256,2048]{1,0:T(8,128)} %parent_ref.2) | copy-start | bytes 6291460
  90.3 34.2 %all-to-all-start.3 = ((f32[16,32,1024]{2,1,0:T(8,128)}), f32[16,32,1024]{2,1,0:T(8,128)}, u32[]{:S(2)}, u32[]{:S(2)}) async-start(f32[16,32,1024]{2,1,0:T(8,128)} %pick.1), calls=%async_computation.3 | async-start | bytes 4194304 | tf_op jit(solution)/shard_map/all_to_all | solution.py:508
  96.0 29.9 %collective-permute-start.8 = (f32[16,32,256]{2,1,0:T(8,128)S(1)}, f32[16,32,256]{2,1,0:T(8,128)S(1)}, u32[]{:S(2)}, u32[]{:S(2)}) collective-permute-start(f32[16,32,256]{2,1,0:T(8,128)S(1)} %all_to_all.26), channel_id=1, source_target_pairs={{0,48},{8,56},{1,49},{9,57},{2,50},{10,58},{3,51},{11,59},{4,52},{... | collective-permute-start | bytes 1572872 | tf_op jit(solution)/shard_map/ppermute | solution.py:514
  101.5 24.5 %collective-permute-start.9 = (f32[16,32,256]{2,1,0:T(8,128)S(1)}, f32[16,32,256]{2,1,0:T(8,128)}, u32[]{:S(2)}, u32[]{:S(2)}) collective-permute-start(f32[16,32,256]{2,1,0:T(8,128)S(1)} %all_to_all.26), channel_id=1, source_target_pairs={{0,96},{8,104},{1,97},{9,105},{2,98},{10,106},{3,99},{11,107},{4,1... | collective-permute-start | bytes 1572872 | tf_op jit(solution)/shard_map/ppermute | solution.py:514
  124.5 6.5 %collective-permute-start.10 = (f32[16,32,1024]{2,1,0:T(8,128)}, f32[16,32,1024]{2,1,0:T(8,128)}, u32[]{:S(2)}, u32[]{:S(2)}) collective-permute-start(f32[16,32,1024]{2,1,0:T(8,128)} %all-to-all-done.3.own_ref), channel_id=1, source_target_pairs={{0,8},{8,0},{16,24},{24,16},{32,40},{40,32},{48,56},{56,48},{64,72... | collective-permute-start | bytes 6291464 | tf_op jit(solution)/shard_map/ppermute | solution.py:509
  127.1 28.9 %collective-permute-start.11 = (f32[16,32,256]{2,1,0:T(8,128)S(1)}, f32[16,32,256]{2,1,0:T(8,128)S(1)}, u32[]{:S(2)}, u32[]{:S(2)}) collective-permute-start(f32[16,32,256]{2,1,0:T(8,128)S(1)} %add_add_fusion.1), channel_id=1, source_target_pairs={{0,16},{8,24},{48,64},{56,72},{96,112},{104,120},{1,17},{9,25},{49... | collective-permute-start | bytes 1572872 | tf_op jit(solution)/shard_map/ppermute | solution.py:514
  130.0 26.0 %collective-permute-start.12 = (f32[16,32,256]{2,1,0:T(8,128)S(1)}, f32[16,32,256]{2,1,0:T(8,128)S(1)}, u32[]{:S(2)}, u32[]{:S(2)}) collective-permute-start(f32[16,32,256]{2,1,0:T(8,128)S(1)} %add_add_fusion.1), channel_id=1, source_target_pairs={{48,32},{56,40},{96,80},{104,88},{49,33},{57,41},{97,81},{105,89},... | collective-permute-start | bytes 1572872 | tf_op jit(solution)/shard_map/ppermute | solution.py:514
  156.1 1.6 copy-start.7
  156.1 10.0 %collective-permute-start.13 = (f32[16,32,256]{2,1,0:T(8,128)S(1)}, f32[16,32,256]{2,1,0:T(8,128)S(1)}, u32[]{:S(2)}, u32[]{:S(2)}) collective-permute-start(f32[16,32,256]{2,1,0:T(8,128)S(1)} %add_add_fusion.c_in), channel_id=1, source_target_pairs={{0,8},{8,0},{16,24},{24,16},{32,40},{40,32},{48,56},{56,48},{64,72... | collective-permute-start | bytes 1572872 | tf_op jit(solution)/shard_map/ppermute | solution.py:527
  157.8 37.2 %all-to-all-start.4 = ((f32[8,256,256]{2,1,0:T(8,128)}), f32[8,256,256]{2,1,0:T(8,128)S(1)}, u32[]{:S(2)}, u32[]{:S(2)}) async-start(f32[8,256,256]{2,1,0:T(8,128)} %turn.1), calls=%async_computation.4 | async-start | bytes 4194304 | tf_op jit(solution)/shard_map/all_to_all | solution.py:521
  166.1 0.8 copy-start.8
  194.9 1.3 copy-start.6
Sparse Core Ops, SparseCore 0:
  73.6 92.2 all-gather.1

commit v5 on v3

--- a/solution.py
+++ b/solution.py
@@ -11,7 +11,7 @@
 STRIP = 64
 RUN = 32
 HALF = NB // 2
-TILE = 256
+TILE = 512
 PLANE = ("col", "half")
 VMEM_LIMIT = 24 * 1024 * 1024
 
@@ -441,7 +441,7 @@
     term = dot3(wh[...], wl[...], ah, al).T
     keep = flags_ref[1] == 0
     for b in range(TILE // BLK):
-        part = front_ref[0, b * BLK : (b + 1) * BLK, :]
+        part = front_ref[b // 2, (b % 2) * BLK : (b % 2 + 1) * BLK, :]
         for s in range(2):
             n = inv_ref[s, (TILE // BLK) * t + b]
             part = part + jnp.where(n >= 0, child_ref[jnp.maximum(n, 0) * 2 + s], 0.0)
@@ -462,7 +462,7 @@
                 pl.BlockSpec((256, NB), lambda t, i, f: (0, 0)),
                 pl.BlockSpec((NB, TILE), lambda t, i, f: (0, t)),
                 pl.BlockSpec((NB, TILE), lambda t, i, f: (0, sym_tile(t, f))),
-                pl.BlockSpec((1, TILE, 256), lambda t, i, f: (t, 0, 0)),
+                pl.BlockSpec((TILE // 256, 256, 256), lambda t, i, f: (t, 0, 0)),
                 pl.BlockSpec((16, BLK, 256), lambda t, i, f: (0, 0, 0)),
             ],
             out_specs=pl.BlockSpec((TILE, 256), lambda t, i, f: (t, 0)),
@@ -498,15 +498,15 @@
 
     start, wanted = share(place, keep, lax.ppermute(give, "row", swap))
     halves = [lax.ppermute(start, "row", [(0, 2 * z), (1, 2 * z + 1)]) for z in range(1, 8)]
+    child = lax.all_to_all(wide, PLANE, 0, 0, tiled=True)
+    start, child, *halves = lax.optimization_barrier((start, child, *halves))
     spread = pick(chip, [start] + halves, copies=16)
 
     matching = lax.all_to_all(wanted, PLANE, 0, 0, tiled=True)
-    child = lax.all_to_all(wide, PLANE, 0, 0, tiled=True)
     late_strip, spread = lax.optimization_barrier((a_strip, spread))
     a_turned = lax.all_gather(late_strip, PLANE, axis=0, tiled=True)
-    spread, matching, child = lax.optimization_barrier((spread, matching, child))
+    spread, matching = lax.optimization_barrier((spread, matching))
     gathered = lax.all_to_all(spread, PLANE, 0, 0, tiled=True)
-    other = lax.ppermute(gathered, "row", swap)
     parent_then, _ = lax.optimization_barrier((parent_front, spread))
     turned_parent = turn(parent_then)
 
@@ -518,6 +518,7 @@
     to_3, to_6, turned_parent = lax.optimization_barrier((to_3, to_6, turned_parent))
     relay = mine + (to_3 + to_6)
     gathered, relay, turned_parent = lax.optimization_barrier((gathered, relay, turned_parent))
+    other = lax.ppermute(gathered, "row", swap)
     front = lax.all_to_all(turned_parent, "col", 0, 0, tiled=True)
     last = [along(relay, [(0, 1), (3, 4), (6, 7)]), along(relay, [(3, 2), (6, 5)])]
     sym, mh, ml, rest, cross = first_half(place, gathered, other)

time: 269 us -> 217 us (0.81)
  waiting for transfers between devices: 73 us -> 40.8 us
  blocking collectives: 57.3 us -> 28.9 us
  starting transfers between devices: 39.9 us -> 51.2 us
    all_to_all x2 -> x1, blocking collectives: 57.3 us -> 28.9 us  [body(): pieces = lax.all_to_all(strips, PLANE, 0, 0, tiled=True)]
    all_to_all x1, waiting for transfers between devices: 44.4 us -> 21.3 us  [body(): gathered = lax.all_to_all(spread, PLANE, 0, 0, tiled=True)]
    all_to_all x1 -> x2, waiting for transfers between devices: 21.4 us -> 9.63 us  [the longest x1 9.63 us: body(): matching = lax.all_to_all(wanted, PLANE, 0, 0, tiled=True)]
    ppermute x4, starting transfers between devices: 6.23 us -> 12 us  [along(): lax.ppermute(x, 'row', [(2 * i + n, 2 * j + n) for i, j in pairs for n in...]
    all_to_all x1 -> x2, starting transfers between devices: 7.71 us -> 12.9 us  [the longest x1 7.31 us: body(): matching = lax.all_to_all(wanted, PLANE, 0, 0, tiled=True)]
    unnamed x24 -> x20, local copies, waits for them, and re-layouts: 7.57 us -> 6.19 us
  transfers between devices with their start and end apart: 18 -> 19, of which waited for: 7 -> 9; matrix products, arithmetic and copies ran while one was open for 2% -> 2% of each run, Pallas kernels for 19% -> 25%
where the time goes in v5:
time: 217 us; the launch traced here: 214 us
  Pallas kernels  67.9 us (31%)
  starting transfers between devices  51.2 us (24%)
  waiting for transfers between devices  40.8 us (19%)
  blocking collectives  28.9 us (13%)
  between operations  13.7 us (6%)
  local copies, waits for them, and re-layouts  6.99 us (3%)
  other arithmetic  4.74 us (2%)
    all_to_all x1, blocking collectives, body(): pieces = lax.all_to_all(strips, PLANE, 0, 0, tiled=True)  28.9 us
    pallas_call x1, Pallas kernels, first_half(): pl.pallas_call(first_kernel, in_specs=[pl.BlockSpec(memory_space=pltpu.SM...  25.1 us
    pallas_call x1, Pallas kernels, second_half(): pl.pallas_call(second_kernel, in_specs=[pl.BlockSpec(memory_space=pltpu.S...  24.5 us
    all_to_all x1, waiting for transfers between devices, body(): gathered = lax.all_to_all(spread, PLANE, 0, 0, tiled=True)  21.3 us
    ppermute x7, starting transfers between devices, body(): lax.ppermute(start, 'row', [(0, 2 * z), (1, 2 * z + 1)])  15 us
    ppermute x4, starting transfers between devices, along(): lax.ppermute(x, 'row', [(2 * i + n, 2 * j + n) for i, j in pairs for n in...  12 us
    pallas_call x1, Pallas kernels, product(): pl.pallas_call(product_kernel, grid_spec=pltpu.PrefetchScalarGridSpec(num...  11.4 us
    all_to_all x1, waiting for transfers between devices, body(): matching = lax.all_to_all(wanted, PLANE, 0, 0, tiled=True)  9.63 us
  transfers between devices with their start and end apart: 19, of which 9 were waited for; matrix products, arithmetic and copies ran while one was open for 2% of the time, Pallas kernels for 25%

profile of v5, /device:TPU:2, one launch (start us, length us, event | category | flops | bytes accessed | tf_op | source)
XLA Modules:
  0.0 214.2 jit_solution(1467009513833652302)
XLA Ops:
  6.5 0.7 copy-done
  7.2 0.1 convert_reduce_fusion
  7.3 0.7 subtract_bitcast_fusion
  8.0 1.6 copy-done.1
  9.6 1.0 copy-done.4
  10.7 1.0 prep.1
  11.7 28.9 %all_to_all.25.pieces_ref = f32[16,64,384]{2,1,0:T(8,128)S(1)} all-to-all(f32[16,64,384]{2,1,0:T(8,128)S(1)} %get-tuple-element.41), channel_id=1, replica_groups=mesh['half'=2,'row'=16,'col'=8] {'col','half'}, dimensions={0} | all-to-all | bytes 3145728 | tf_op jit(solution)/shard_map/all_to_all | solution.py:491
  40.6 5.6 %all-to-all-start.1 = ((f32[16,128,256]{2,1,0:T(8,128)}), f32[16,128,256]{2,1,0:T(8,128)}, u32[]{:S(2)}, u32[]{:S(2)}) async-start(f32[16,128,256]{2,1,0:T(8,128)} %copy-done.3), calls=%async_computation.1 | async-start | bytes 4194304 | tf_op jit(solution)/shard_map/all_to_all | solution.py:501
  46.3 0.7 slice.3
  47.1 0.1 copy.7
  47.1 1.5 strip.1
  48.7 1.5 collective-permute-done.got_ref
  50.2 1.5 share.1
  51.7 3.8 %collective-permute-start.1 = (f32[32,1024]{1,0:T(8,128)S(1)}, f32[32,1024]{1,0:T(8,128)S(1)}, u32[]{:S(2)}, u32[]{:S(2)}) collective-permute-start(f32[32,1024]{1,0:T(8,128)S(1)} %get-tuple-element.47.refs_1_), channel_id=1, source_target_pairs={{0,16},{8,24},{1,17},{9,25},{2,18},{10,26},{3,19},{11,27},{4,20},{... | collective-permute-start | bytes 393224 | tf_op jit(solution)/shard_map/ppermute | solution.py:500
  55.5 2.0 collective-permute-start.2
  57.5 2.0 collective-permute-start.3
  59.6 3.2 %collective-permute-start.4 = (f32[32,1024]{1,0:T(8,128)S(1)}, f32[32,1024]{1,0:T(8,128)S(1)}, u32[]{:S(2)}, u32[]{:S(2)}) collective-permute-start(f32[32,1024]{1,0:T(8,128)S(1)} %get-tuple-element.47.refs_1_), channel_id=1, source_target_pairs={{0,64},{8,72},{1,65},{9,73},{2,66},{10,74},{3,67},{11,75},{4,68},{... | collective-permute-start | bytes 393224 | tf_op jit(solution)/shard_map/ppermute | solution.py:500
  62.8 1.3 collective-permute-start.5
  64.1 1.3 collective-permute-start.6
  65.4 1.3 collective-permute-start.7
  66.8 0.2 collective-permute-done.4.refs_5_
  67.0 1.0 collective-permute-done.5.refs_6_
  67.9 2.8 %collective-permute-done.6.refs_7_ = f32[32,1024]{1,0:T(8,128)S(1)} collective-permute-done((f32[32,1024]{1,0:T(8,128)S(1)}, f32[32,1024]{1,0:T(8,128)S(1)}, u32[]{:S(2)}, u32[]{:S(2)}) %collective-permute-start.6) | collective-permute-done | bytes 131104 | tf_op jit(solution)/shard_map/ppermute | solution.py:500
  70.7 2.0 collective-permute-done.7.refs_8_
  72.8 1.5 pick.1
  74.3 7.3 %all-to-all-start.2 = ((f32[16,32,256]{2,1,0:T(8,128)}), f32[16,32,256]{2,1,0:T(8,128)S(1)}, u32[]{:S(2)}, u32[]{:S(2)}) async-start(f32[16,32,256]{2,1,0:T(8,128)} %get-tuple-element.56), calls=%async_computation.2 | async-start | bytes 1048576 | tf_op jit(solution)/shard_map/all_to_all | solution.py:505
  81.6 9.6 %all-to-all-done.2 = f32[16,32,256]{2,1,0:T(8,128)S(1)} async-done(((f32[16,32,256]{2,1,0:T(8,128)}), f32[16,32,256]{2,1,0:T(8,128)S(1)}, u32[]{:S(2)}, u32[]{:S(2)}) %all-to-all-start.2) | async-done | bytes 524320 | tf_op jit(solution)/shard_map/all_to_all | solution.py:505
  91.2 6.1 %collective-permute-start.8 = (f32[16,32,256]{2,1,0:T(8,128)S(1)}, f32[16,32,256]{2,1,0:T(8,128)S(1)}, u32[]{:S(2)}, u32[]{:S(2)}) collective-permute-start(f32[16,32,256]{2,1,0:T(8,128)S(1)} %all-to-all-done.2), channel_id=1, source_target_pairs={{0,48},{8,56},{1,49},{9,57},{2,50},{10,58},{3,51},{11,59},{4,52},{... | collective-permute-start | bytes 1572872 | tf_op jit(solution)/shard_map/ppermute | solution.py:514
  97.3 3.1 %collective-permute-start.9 = (f32[16,32,256]{2,1,0:T(8,128)S(1)}, f32[16,32,256]{2,1,0:T(8,128)}, u32[]{:S(2)}, u32[]{:S(2)}) collective-permute-start(f32[16,32,256]{2,1,0:T(8,128)S(1)} %all-to-all-done.2), channel_id=1, source_target_pairs={{0,96},{8,104},{1,97},{9,105},{2,98},{10,106},{3,99},{11,107},{4,1... | collective-permute-start | bytes 1572872 | tf_op jit(solution)/shard_map/ppermute | solution.py:514
  100.5 5.7 %all-to-all-start.3 = ((f32[16,32,1024]{2,1,0:T(8,128)}), f32[16,32,1024]{2,1,0:T(8,128)}, u32[]{:S(2)}, u32[]{:S(2)}) async-start(f32[16,32,1024]{2,1,0:T(8,128)} %pick.1), calls=%async_computation.3 | async-start | bytes 4194304 | tf_op jit(solution)/shard_map/all_to_all | solution.py:509
  106.2 1.5 turn.1
  107.6 1.7 collective-permute-done.9
  109.4 1.2 add_add_fusion.1
  110.6 21.3 %all-to-all-done.3.own_ref = f32[16,32,1024]{2,1,0:T(8,128)} async-done(((f32[16,32,1024]{2,1,0:T(8,128)}), f32[16,32,1024]{2,1,0:T(8,128)}, u32[]{:S(2)}, u32[]{:S(2)}) %all-to-all-start.3) | async-done | bytes 2097184 | tf_op jit(solution)/shard_map/all_to_all | solution.py:509
  131.8 1.3 collective-permute-start.11
  133.2 1.5 collective-permute-start.12
  134.6 5.5 %all-to-all-start.4 = ((f32[8,256,256]{2,1,0:T(8,128)}), f32[8,256,256]{2,1,0:T(8,128)S(1)}, u32[]{:S(2)}, u32[]{:S(2)}) async-start(f32[8,256,256]{2,1,0:T(8,128)} %turn.1), calls=%async_computation.4 | async-start | bytes 4194304 | tf_op jit(solution)/shard_map/all_to_all | solution.py:522
  140.1 25.1 %first_half.1 = (f32[1024,1024]{1,0:T(8,128)}, bf16[512,512]{1,0:T(8,128)(2,1)}, bf16[512,512]{1,0:T(8,128)(2,1)}, f32[512,512]{1,0:T(8,128)}, f32[512,512]{1,0:T(8,128)}) custom-call(s32[2]{0:T(128)} %copy-done.5, f32[16,32,1024]{2,1,0:T(8,128)} %all-to-all-done.3.own_ref, f32[16,32,1024]{2,1,0:T(8,128)} %collective-permute-done.10.other_ref), custom_call_target="tpu_custom_call" | custom-call | flops 30000001024 | bytes 12582912 | tf_op jit(solution)/shard_map/first_half/pallas_call | solution.py:400
  165.2 0.8 copy-done.8
  166.0 1.4 add_add_fusion.c_in
  167.4 0.1 collective-permute-start.13
  167.5 0.6 add_convert_fusion.flags_ref
  168.1 0.7 select_reduce_fusion.inv_ref
  168.8 0.6 collective-permute-done.13.d_in
  169.4 0.8 copy-done.9
  170.2 24.5 %second_half.1.wt_ref = f32[256,1024]{1,0:T(8,128)} custom-call(s32[2]{0:T(128)} %copy-done.5, f32[512,512]{1,0:T(8,128)} %get-tuple-element.66.rest_in, f32[512,512]{1,0:T(8,128)} %get-tuple-element.67.cross_in, bf16[512,512]{1,0:T(8,128)(2,1)} %get-tuple-element.68.mh_in, bf16[512,512]{1,0:T(8,128)(2,1)} %get-tuple-element.69.ml_in, ...), custom_call_target="tpu_custom_call" | custom-call | flops 1000000000 | bytes 6291456 | tf_op jit(solution)/shard_map/second_half/pallas_call | solution.py:415
  194.8 1.3 copy-done.6
  196.0 11.4 %product.1 = f32[2048,256]{1,0:T(8,128)} custom-call(s32[2,16]{1,0:T(2,128)} %select_reduce_fusion.inv_ref, s32[2]{0:T(128)} %add_convert_fusion.flags_ref, f32[256,1024]{1,0:T(8,128)} %second_half.1.wt_ref, f32[1024,2048]{1,0:T(8,128)} %all-gather.2.cloned.1.call-done.rows_ref, f32[1024,1024]{1,0:T(8,128)} %get-tuple-element.74.sym_ref, ...), custom_call_target="tpu_custom_call" | custom-call | flops 3221225472 | bytes 16777216 | tf_op jit(solution)/shard_map/product/pallas_call | solution.py:456
  (32 shorter events, 0.3 us)
Async XLA Ops:
  6.5 0.7 copy-start
  8.0 1.6 copy-start.1
  9.6 1.0 copy-start.4
  11.7 28.9 %copy-start.3 = (f32[16,128,256]{2,1,0:T(8,128)}, f32[16,128,256]{2,1,0:T(8,128)S(1)}, u32[]{:S(2)}) copy-start(f32[16,128,256]{2,1,0:T(8,128)S(1)} %get-tuple-element.46) | copy-start | bytes 6291460
  40.6 32.2 %all-to-all-start.1 = ((f32[16,128,256]{2,1,0:T(8,128)}), f32[16,128,256]{2,1,0:T(8,128)}, u32[]{:S(2)}, u32[]{:S(2)}) async-start(f32[16,128,256]{2,1,0:T(8,128)} %copy-done.3), calls=%async_computation.1 | async-start | bytes 4194304 | tf_op jit(solution)/shard_map/all_to_all | solution.py:501
  46.2 148.5 %all-gather.2.cloned.1.call-start = ((), (), s32[]{:S(2)}) async-start(), calls=%async_computation.5 | async-start | bytes 8912896 | tf_op jit(solution)/shard_map/all_gather | solution.py:507
  46.3 27.9 %copy-start.5 = (s32[2]{0:T(128)}, s32[2]{0:T(128)S(1)}, u32[]{:S(2)}) copy-start(s32[2]{0:T(128)S(1)} %pad_add_fusion.1.place_ref) | copy-start | bytes 28
  48.7 1.5 collective-permute-start
  51.7 12.4 %collective-permute-start.1 = (f32[32,1024]{1,0:T(8,128)S(1)}, f32[32,1024]{1,0:T(8,128)S(1)}, u32[]{:S(2)}, u32[]{:S(2)}) collective-permute-start(f32[32,1024]{1,0:T(8,128)S(1)} %get-tuple-element.47.refs_1_), channel_id=1, source_target_pairs={{0,16},{8,24},{1,17},{9,25},{2,18},{10,26},{3,19},{11,27},{4,20},{... | collective-permute-start | bytes 393224 | tf_op jit(solution)/shard_map/ppermute | solution.py:500
  55.5 9.9 %collective-permute-start.2 = (f32[32,1024]{1,0:T(8,128)S(1)}, f32[32,1024]{1,0:T(8,128)S(1)}, u32[]{:S(2)}, u32[]{:S(2)}) collective-permute-start(f32[32,1024]{1,0:T(8,128)S(1)} %get-tuple-element.47.refs_1_), channel_id=1, source_target_pairs={{0,32},{8,40},{1,33},{9,41},{2,34},{10,42},{3,35},{11,43},{4,36},{... | collective-permute-start | bytes 393224 | tf_op jit(solution)/shard_map/ppermute | solution.py:500
  57.5 9.2 %collective-permute-start.3 = (f32[32,1024]{1,0:T(8,128)S(1)}, f32[32,1024]{1,0:T(8,128)S(1)}, u32[]{:S(2)}, u32[]{:S(2)}) collective-permute-start(f32[32,1024]{1,0:T(8,128)S(1)} %get-tuple-element.47.refs_1_), channel_id=1, source_target_pairs={{0,48},{8,56},{1,49},{9,57},{2,50},{10,58},{3,51},{11,59},{4,52},{... | collective-permute-start | bytes 393224 | tf_op jit(solution)/shard_map/ppermute | solution.py:500
  59.6 7.4 %collective-permute-start.4 = (f32[32,1024]{1,0:T(8,128)S(1)}, f32[32,1024]{1,0:T(8,128)S(1)}, u32[]{:S(2)}, u32[]{:S(2)}) collective-permute-start(f32[32,1024]{1,0:T(8,128)S(1)} %get-tuple-element.47.refs_1_), channel_id=1, source_target_pairs={{0,64},{8,72},{1,65},{9,73},{2,66},{10,74},{3,67},{11,75},{4,68},{... | collective-permute-start | bytes 393224 | tf_op jit(solution)/shard_map/ppermute | solution.py:500
  62.8 5.1 %collective-permute-start.5 = (f32[32,1024]{1,0:T(8,128)S(1)}, f32[32,1024]{1,0:T(8,128)S(1)}, u32[]{:S(2)}, u32[]{:S(2)}) collective-permute-start(f32[32,1024]{1,0:T(8,128)S(1)} %get-tuple-element.47.refs_1_), channel_id=1, source_target_pairs={{0,80},{8,88},{1,81},{9,89},{2,82},{10,90},{3,83},{11,91},{4,84},{... | collective-permute-start | bytes 393224 | tf_op jit(solution)/shard_map/ppermute | solution.py:500
  64.1 6.6 %collective-permute-start.6 = (f32[32,1024]{1,0:T(8,128)S(1)}, f32[32,1024]{1,0:T(8,128)S(1)}, u32[]{:S(2)}, u32[]{:S(2)}) collective-permute-start(f32[32,1024]{1,0:T(8,128)S(1)} %get-tuple-element.47.refs_1_), channel_id=1, source_target_pairs={{0,96},{8,104},{1,97},{9,105},{2,98},{10,106},{3,99},{11,107},{4,1... | collective-permute-start | bytes 393224 | tf_op jit(solution)/shard_map/ppermute | solution.py:500
  65.4 7.3 %collective-permute-start.7 = (f32[32,1024]{1,0:T(8,128)S(1)}, f32[32,1024]{1,0:T(8,128)S(1)}, u32[]{:S(2)}, u32[]{:S(2)}) collective-permute-start(f32[32,1024]{1,0:T(8,128)S(1)} %get-tuple-element.47.refs_1_), channel_id=1, source_target_pairs={{0,112},{8,120},{1,113},{9,121},{2,114},{10,122},{3,115},{11,123},... | collective-permute-start | bytes 393224 | tf_op jit(solution)/shard_map/ppermute | solution.py:500
  74.3 16.9 %all-to-all-start.2 = ((f32[16,32,256]{2,1,0:T(8,128)}), f32[16,32,256]{2,1,0:T(8,128)S(1)}, u32[]{:S(2)}, u32[]{:S(2)}) async-start(f32[16,32,256]{2,1,0:T(8,128)} %get-tuple-element.56), calls=%async_computation.2 | async-start | bytes 1048576 | tf_op jit(solution)/shard_map/all_to_all | solution.py:505
  81.6 24.5 %copy-start.2 = (f32[256,2048]{1,0:T(8,128)S(1)}, f32[256,2048]{1,0:T(8,128)}, u32[]{:S(2)}) copy-start(f32[256,2048]{1,0:T(8,128)} %parent_ref.2) | copy-start | bytes 6291460
  91.2 16.4 %collective-permute-start.8 = (f32[16,32,256]{2,1,0:T(8,128)S(1)}, f32[16,32,256]{2,1,0:T(8,128)S(1)}, u32[]{:S(2)}, u32[]{:S(2)}) collective-permute-start(f32[16,32,256]{2,1,0:T(8,128)S(1)} %all-to-all-done.2), channel_id=1, source_target_pairs={{0,48},{8,56},{1,49},{9,57},{2,50},{10,58},{3,51},{11,59},{4,52},{... | collective-permute-start | bytes 1572872 | tf_op jit(solution)/shard_map/ppermute | solution.py:514
  97.3 12.0 %collective-permute-start.9 = (f32[16,32,256]{2,1,0:T(8,128)S(1)}, f32[16,32,256]{2,1,0:T(8,128)}, u32[]{:S(2)}, u32[]{:S(2)}) collective-permute-start(f32[16,32,256]{2,1,0:T(8,128)S(1)} %all-to-all-done.2), channel_id=1, source_target_pairs={{0,96},{8,104},{1,97},{9,105},{2,98},{10,106},{3,99},{11,107},{4,1... | collective-permute-start | bytes 1572872 | tf_op jit(solution)/shard_map/ppermute | solution.py:514
  100.5 31.4 %all-to-all-start.3 = ((f32[16,32,1024]{2,1,0:T(8,128)}), f32[16,32,1024]{2,1,0:T(8,128)}, u32[]{:S(2)}, u32[]{:S(2)}) async-start(f32[16,32,1024]{2,1,0:T(8,128)} %pick.1), calls=%async_computation.3 | async-start | bytes 4194304 | tf_op jit(solution)/shard_map/all_to_all | solution.py:509
  131.8 8.3 %collective-permute-start.10 = (f32[16,32,1024]{2,1,0:T(8,128)}, f32[16,32,1024]{2,1,0:T(8,128)}, u32[]{:S(2)}, u32[]{:S(2)}) collective-permute-start(f32[16,32,1024]{2,1,0:T(8,128)} %all-to-all-done.3.own_ref), channel_id=1, source_target_pairs={{0,8},{8,0},{16,24},{24,16},{32,40},{40,32},{48,56},{56,48},{64,72... | collective-permute-start | bytes 6291464 | tf_op jit(solution)/shard_map/ppermute | solution.py:521
  131.8 33.4 %collective-permute-start.11 = (f32[16,32,256]{2,1,0:T(8,128)S(1)}, f32[16,32,256]{2,1,0:T(8,128)S(1)}, u32[]{:S(2)}, u32[]{:S(2)}) collective-permute-start(f32[16,32,256]{2,1,0:T(8,128)S(1)} %add_add_fusion.1), channel_id=1, source_target_pairs={{0,16},{8,24},{48,64},{56,72},{96,112},{104,120},{1,17},{9,25},{49... | collective-permute-start | bytes 1572872 | tf_op jit(solution)/shard_map/ppermute | solution.py:514
  133.2 32.1 %collective-permute-start.12 = (f32[16,32,256]{2,1,0:T(8,128)S(1)}, f32[16,32,256]{2,1,0:T(8,128)}, u32[]{:S(2)}, u32[]{:S(2)}) collective-permute-start(f32[16,32,256]{2,1,0:T(8,128)S(1)} %add_add_fusion.1), channel_id=1, source_target_pairs={{48,32},{56,40},{96,80},{104,88},{49,33},{57,41},{97,81},{105,89},... | collective-permute-start | bytes 1572872 | tf_op jit(solution)/shard_map/ppermute | solution.py:514
  134.6 60.1 %all-to-all-start.4 = ((f32[8,256,256]{2,1,0:T(8,128)}), f32[8,256,256]{2,1,0:T(8,128)S(1)}, u32[]{:S(2)}, u32[]{:S(2)}) async-start(f32[8,256,256]{2,1,0:T(8,128)} %turn.1), calls=%async_computation.4 | async-start | bytes 4194304 | tf_op jit(solution)/shard_map/all_to_all | solution.py:522
  165.2 0.8 copy-start.8
  167.4 2.0 copy-start.7
  167.4 2.0 collective-permute-start.13
  169.4 0.8 copy-start.9
  194.7 1.3 copy-start.6
Sparse Core Ops, SparseCore 0:
  74.4 116.5 all-gather.1

commit v6 on v5

--- a/solution.py
+++ b/solution.py
@@ -334,8 +334,8 @@
 
 
 def second_kernel(
-    place_ref, rest_in, cross_in, mh_in, ml_in, c_in, d_in, wt_ref,
-    lh, ll, uh, ul, nh, nl, zh, zl, de, row, rest_ref, cross_ref, mh_ref, ml_ref, c_ref, d_ref, c_all, sem
+    place_ref, rest_in, cross_in, mh_in, ml_in, c_in, d_in, wt_out,
+    lh, ll, uh, ul, nh, nl, zh, zl, de, row, rest_ref, cross_ref, mh_ref, ml_ref, c_ref, d_ref, c_all, wt_ref, sem
 ):
     strip = place_ref[1]
     pairs = [(rest_in, rest_ref), (cross_in, cross_ref), (mh_in, mh_ref), (ml_in, ml_ref), (c_in, c_ref), (d_in, d_ref)]
@@ -382,6 +382,10 @@
         wt_ref[:, 0:HALF] = dot3(sh, sl, mh_ref[...], ml_ref[...]) + dot3(th, tl, zh[...], zl[...])
         wt_ref[:, HALF:] = dot3(th, tl, nh[...], nl[...])
 
+    move = pltpu.make_async_copy(wt_ref, wt_out, sem.at[6])
+    move.start()
+    move.wait()
+
 
 SQUARE = (HALF, HALF)
 
@@ -415,22 +419,27 @@
     return pl.pallas_call(
         second_kernel,
         in_specs=[pl.BlockSpec(memory_space=pltpu.SMEM)] + [hbm] * 6,
-        out_specs=pl.BlockSpec(memory_space=pltpu.VMEM),
+        out_specs=hbm,
         out_shape=jax.ShapeDtypeStruct((256, NB), jnp.float32),
         scratch_shapes=factor_scratch(8)
         + [pltpu.VMEM(x.shape, x.dtype) for x in arrays]
-        + [pltpu.VMEM((NB, 256), jnp.float32), pltpu.SemaphoreType.DMA((6,))],
+        + [
+            pltpu.VMEM((NB, 256), jnp.float32),
+            pltpu.VMEM((256, NB), jnp.float32),
+            pltpu.SemaphoreType.DMA((7,)),
+        ],
         compiler_params=pltpu.CompilerParams(vmem_limit_bytes=60 * 1024 * 1024),
         cost_estimate=pl.CostEstimate(flops=1_000_000_000, bytes_accessed=6 << 20, transcendentals=0),
         name="second_half",
     )(place, *arrays)
 
 
-def product_kernel(inv_ref, flags_ref, wt_ref, rows_ref, sym_ref, front_ref, child_ref, out_ref, wh, wl):
+def product_kernel(inv_ref, flags_ref, wt_ref, rows_ref, sym_ref, front_ref, child_in, out_ref, wh, wl, child_ref, sem):
     t = pl.program_id(0)
 
     @pl.when(t == 0)
     def _():
+        pltpu.make_async_copy(child_in, child_ref, sem).start()
         high, low = split_bf16(wt_ref[...])
         wh[...] = high
         wl[...] = low
@@ -439,6 +448,11 @@
     a = jnp.where(use_sym, sym_ref[...], rows_ref[...])
     ah, al = split_bf16(a)
     term = dot3(wh[...], wl[...], ah, al).T
+
+    @pl.when(t == 0)
+    def _():
+        pltpu.make_async_copy(child_in, child_ref, sem).wait()
+
     keep = flags_ref[1] == 0
     for b in range(TILE // BLK):
         part = front_ref[b // 2, (b % 2) * BLK : (b % 2 + 1) * BLK, :]
@@ -463,10 +477,15 @@
                 pl.BlockSpec((NB, TILE), lambda t, i, f: (0, t)),
                 pl.BlockSpec((NB, TILE), lambda t, i, f: (0, sym_tile(t, f))),
                 pl.BlockSpec((TILE // 256, 256, 256), lambda t, i, f: (t, 0, 0)),
-                pl.BlockSpec((16, BLK, 256), lambda t, i, f: (0, 0, 0)),
+                pl.BlockSpec(memory_space=pltpu.HBM),
             ],
             out_specs=pl.BlockSpec((TILE, 256), lambda t, i, f: (t, 0)),
-            scratch_shapes=[pltpu.VMEM((256, NB), jnp.bfloat16), pltpu.VMEM((256, NB), jnp.bfloat16)],
+            scratch_shapes=[
+                pltpu.VMEM((256, NB), jnp.bfloat16),
+                pltpu.VMEM((256, NB), jnp.bfloat16),
+                pltpu.VMEM((16, BLK, 256), jnp.float32),
+                pltpu.SemaphoreType.DMA,
+            ],
         ),
         out_shape=jax.ShapeDtypeStruct((2048, 256), jnp.float32),
         compiler_params=pltpu.CompilerParams(vmem_limit_bytes=60 * 1024 * 1024),

time: 217 us -> 217 us (level)
  no operation moved by 1% of the time
where the time goes in v6:
time: 217 us; the launch traced here: 214 us
  Pallas kernels  68 us (31%)
  starting transfers between devices  51.2 us (24%)
  waiting for transfers between devices  40.8 us (19%)
  blocking collectives  28.9 us (13%)
  between operations  13.7 us (6%)
  local copies, waits for them, and re-layouts  6.99 us (3%)
  other arithmetic  4.74 us (2%)
    all_to_all x1, blocking collectives, body(): pieces = lax.all_to_all(strips, PLANE, 0, 0, tiled=True)  28.9 us
    pallas_call x1, Pallas kernels, first_half(): pl.pallas_call(first_kernel, in_specs=[pl.BlockSpec(memory_space=pltpu.SM...  25.1 us
    pallas_call x1, Pallas kernels, second_half(): pl.pallas_call(second_kernel, in_specs=[pl.BlockSpec(memory_space=pltpu.S...  24.5 us
    all_to_all x1, waiting for transfers between devices, body(): gathered = lax.all_to_all(spread, PLANE, 0, 0, tiled=True)  21.3 us
    ppermute x7, starting transfers between devices, body(): lax.ppermute(start, 'row', [(0, 2 * z), (1, 2 * z + 1)])  15 us
    ppermute x4, starting transfers between devices, along(): lax.ppermute(x, 'row', [(2 * i + n, 2 * j + n) for i, j in pairs for n in...  12 us
    pallas_call x1, Pallas kernels, product(): pl.pallas_call(product_kernel, grid_spec=pltpu.PrefetchScalarGridSpec(num...  11.4 us
    all_to_all x1, waiting for transfers between devices, body(): matching = lax.all_to_all(wanted, PLANE, 0, 0, tiled=True)  9.63 us
  transfers between devices with their start and end apart: 19, of which 9 were waited for; matrix products, arithmetic and copies ran while one was open for 2% of the time, Pallas kernels for 25%

profile of v6, /device:TPU:2, one launch (start us, length us, event | category | flops | bytes accessed | tf_op | source)
XLA Modules:
  0.0 214.3 jit_solution(11191741975009635561)
XLA Ops:
  6.5 0.7 copy-done
  7.2 0.1 convert_reduce_fusion
  7.3 0.7 subtract_bitcast_fusion
  8.0 1.6 copy-done.1
  9.6 1.0 copy-done.4
  10.7 1.0 prep.1
  11.7 28.9 %all_to_all.25.pieces_ref = f32[16,64,384]{2,1,0:T(8,128)S(1)} all-to-all(f32[16,64,384]{2,1,0:T(8,128)S(1)} %get-tuple-element.41), channel_id=1, replica_groups=mesh['half'=2,'row'=16,'col'=8] {'col','half'}, dimensions={0} | all-to-all | bytes 3145728 | tf_op jit(solution)/shard_map/all_to_all | solution.py:510
  40.6 5.6 %all-to-all-start.1 = ((f32[16,128,256]{2,1,0:T(8,128)}), f32[16,128,256]{2,1,0:T(8,128)}, u32[]{:S(2)}, u32[]{:S(2)}) async-start(f32[16,128,256]{2,1,0:T(8,128)} %copy-done.3), calls=%async_computation.1 | async-start | bytes 4194304 | tf_op jit(solution)/shard_map/all_to_all | solution.py:520
  46.3 0.7 slice.3
  47.1 0.1 copy.7
  47.1 1.5 strip.1
  48.7 1.5 collective-permute-done.got_ref
  50.2 1.5 share.1
  51.7 3.8 %collective-permute-start.1 = (f32[32,1024]{1,0:T(8,128)S(1)}, f32[32,1024]{1,0:T(8,128)S(1)}, u32[]{:S(2)}, u32[]{:S(2)}) collective-permute-start(f32[32,1024]{1,0:T(8,128)S(1)} %get-tuple-element.47.refs_1_), channel_id=1, source_target_pairs={{0,16},{8,24},{1,17},{9,25},{2,18},{10,26},{3,19},{11,27},{4,20},{... | collective-permute-start | bytes 393224 | tf_op jit(solution)/shard_map/ppermute | solution.py:519
  55.5 2.0 collective-permute-start.2
  57.5 2.0 collective-permute-start.3
  59.6 3.2 %collective-permute-start.4 = (f32[32,1024]{1,0:T(8,128)S(1)}, f32[32,1024]{1,0:T(8,128)S(1)}, u32[]{:S(2)}, u32[]{:S(2)}) collective-permute-start(f32[32,1024]{1,0:T(8,128)S(1)} %get-tuple-element.47.refs_1_), channel_id=1, source_target_pairs={{0,64},{8,72},{1,65},{9,73},{2,66},{10,74},{3,67},{11,75},{4,68},{... | collective-permute-start | bytes 393224 | tf_op jit(solution)/shard_map/ppermute | solution.py:519
  62.8 1.3 collective-permute-start.5
  64.1 1.3 collective-permute-start.6
  65.4 1.3 collective-permute-start.7
  66.8 0.2 collective-permute-done.4.refs_5_
  67.0 1.0 collective-permute-done.5.refs_6_
  67.9 2.8 %collective-permute-done.6.refs_7_ = f32[32,1024]{1,0:T(8,128)S(1)} collective-permute-done((f32[32,1024]{1,0:T(8,128)S(1)}, f32[32,1024]{1,0:T(8,128)S(1)}, u32[]{:S(2)}, u32[]{:S(2)}) %collective-permute-start.6) | collective-permute-done | bytes 131104 | tf_op jit(solution)/shard_map/ppermute | solution.py:519
  70.8 2.0 collective-permute-done.7.refs_8_
  72.8 1.5 pick.1
  74.3 7.3 %all-to-all-start.2 = ((f32[16,32,256]{2,1,0:T(8,128)}), f32[16,32,256]{2,1,0:T(8,128)S(1)}, u32[]{:S(2)}, u32[]{:S(2)}) async-start(f32[16,32,256]{2,1,0:T(8,128)} %get-tuple-element.56), calls=%async_computation.2 | async-start | bytes 1048576 | tf_op jit(solution)/shard_map/all_to_all | solution.py:524
  81.6 9.6 %all-to-all-done.2 = f32[16,32,256]{2,1,0:T(8,128)S(1)} async-done(((f32[16,32,256]{2,1,0:T(8,128)}), f32[16,32,256]{2,1,0:T(8,128)S(1)}, u32[]{:S(2)}, u32[]{:S(2)}) %all-to-all-start.2) | async-done | bytes 524320 | tf_op jit(solution)/shard_map/all_to_all | solution.py:524
  91.2 6.1 %collective-permute-start.8 = (f32[16,32,256]{2,1,0:T(8,128)S(1)}, f32[16,32,256]{2,1,0:T(8,128)S(1)}, u32[]{:S(2)}, u32[]{:S(2)}) collective-permute-start(f32[16,32,256]{2,1,0:T(8,128)S(1)} %all-to-all-done.2), channel_id=1, source_target_pairs={{0,48},{8,56},{1,49},{9,57},{2,50},{10,58},{3,51},{11,59},{4,52},{... | collective-permute-start | bytes 1572872 | tf_op jit(solution)/shard_map/ppermute | solution.py:533
  97.3 3.1 %collective-permute-start.9 = (f32[16,32,256]{2,1,0:T(8,128)S(1)}, f32[16,32,256]{2,1,0:T(8,128)}, u32[]{:S(2)}, u32[]{:S(2)}) collective-permute-start(f32[16,32,256]{2,1,0:T(8,128)S(1)} %all-to-all-done.2), channel_id=1, source_target_pairs={{0,96},{8,104},{1,97},{9,105},{2,98},{10,106},{3,99},{11,107},{4,1... | collective-permute-start | bytes 1572872 | tf_op jit(solution)/shard_map/ppermute | solution.py:533
  100.5 5.7 %all-to-all-start.3 = ((f32[16,32,1024]{2,1,0:T(8,128)}), f32[16,32,1024]{2,1,0:T(8,128)}, u32[]{:S(2)}, u32[]{:S(2)}) async-start(f32[16,32,1024]{2,1,0:T(8,128)} %pick.1), calls=%async_computation.3 | async-start | bytes 4194304 | tf_op jit(solution)/shard_map/all_to_all | solution.py:528
  106.2 1.5 turn.1
  107.6 1.7 collective-permute-done.9
  109.4 1.2 add_add_fusion.1
  110.6 21.3 %all-to-all-done.3.own_ref = f32[16,32,1024]{2,1,0:T(8,128)} async-done(((f32[16,32,1024]{2,1,0:T(8,128)}), f32[16,32,1024]{2,1,0:T(8,128)}, u32[]{:S(2)}, u32[]{:S(2)}) %all-to-all-start.3) | async-done | bytes 2097184 | tf_op jit(solution)/shard_map/all_to_all | solution.py:528
  131.8 1.3 collective-permute-start.11
  133.2 1.5 collective-permute-start.12
  134.6 5.5 %all-to-all-start.4 = ((f32[8,256,256]{2,1,0:T(8,128)}), f32[8,256,256]{2,1,0:T(8,128)S(1)}, u32[]{:S(2)}, u32[]{:S(2)}) async-start(f32[8,256,256]{2,1,0:T(8,128)} %turn.1), calls=%async_computation.4 | async-start | bytes 4194304 | tf_op jit(solution)/shard_map/all_to_all | solution.py:541
  140.1 25.1 %first_half.1 = (f32[1024,1024]{1,0:T(8,128)}, bf16[512,512]{1,0:T(8,128)(2,1)}, bf16[512,512]{1,0:T(8,128)(2,1)}, f32[512,512]{1,0:T(8,128)}, f32[512,512]{1,0:T(8,128)}) custom-call(s32[2]{0:T(128)} %copy-done.5, f32[16,32,1024]{2,1,0:T(8,128)} %all-to-all-done.3.own_ref, f32[16,32,1024]{2,1,0:T(8,128)} %collective-permute-done.10.other_ref), custom_call_target="tpu_custom_call" | custom-call | flops 30000001024 | bytes 12582912 | tf_op jit(solution)/shard_map/first_half/pallas_call | solution.py:404
  165.2 0.8 copy-done.8
  166.0 1.4 add_add_fusion.c_in
  167.4 0.1 collective-permute-start.13
  167.5 0.6 add_convert_fusion.flags_ref
  168.1 0.7 select_reduce_fusion.inv_ref
  168.8 0.6 collective-permute-done.13.d_in
  169.4 0.8 copy-done.9
  170.2 24.5 %second_half.1.wt_ref = f32[256,1024]{1,0:T(8,128)} custom-call(s32[2]{0:T(128)} %copy-done.5, f32[512,512]{1,0:T(8,128)} %get-tuple-element.66.rest_in, f32[512,512]{1,0:T(8,128)} %get-tuple-element.67.cross_in, bf16[512,512]{1,0:T(8,128)(2,1)} %get-tuple-element.68.mh_in, bf16[512,512]{1,0:T(8,128)(2,1)} %get-tuple-element.69.ml_in, ...), custom_call_target="tpu_custom_call" | custom-call | flops 1000000000 | bytes 6291456 | tf_op jit(solution)/shard_map/second_half/pallas_call | solution.py:419
  194.8 1.3 copy-done.6
  196.1 11.4 %product.1 = f32[2048,256]{1,0:T(8,128)} custom-call(s32[2,16]{1,0:T(2,128)} %select_reduce_fusion.inv_ref, s32[2]{0:T(128)} %add_convert_fusion.flags_ref, f32[256,1024]{1,0:T(8,128)} %second_half.1.wt_ref, f32[1024,2048]{1,0:T(8,128)} %all-gather.2.cloned.1.call-done.rows_ref, f32[1024,1024]{1,0:T(8,128)} %get-tuple-element.74.sym_ref, ...), custom_call_target="tpu_custom_call" | custom-call | flops 3221225472 | bytes 16777216 | tf_op jit(solution)/shard_map/product/pallas_call | solution.py:470
  (32 shorter events, 0.3 us)
Async XLA Ops:
  6.5 0.7 copy-start
  8.0 1.6 copy-start.1
  9.6 1.0 copy-start.4
  11.7 28.9 %copy-start.3 = (f32[16,128,256]{2,1,0:T(8,128)}, f32[16,128,256]{2,1,0:T(8,128)S(1)}, u32[]{:S(2)}) copy-start(f32[16,128,256]{2,1,0:T(8,128)S(1)} %get-tuple-element.46) | copy-start | bytes 6291460
  40.6 32.2 %all-to-all-start.1 = ((f32[16,128,256]{2,1,0:T(8,128)}), f32[16,128,256]{2,1,0:T(8,128)}, u32[]{:S(2)}, u32[]{:S(2)}) async-start(f32[16,128,256]{2,1,0:T(8,128)} %copy-done.3), calls=%async_computation.1 | async-start | bytes 4194304 | tf_op jit(solution)/shard_map/all_to_all | solution.py:520
  46.2 148.6 %all-gather.2.cloned.1.call-start = ((), (), s32[]{:S(2)}) async-start(), calls=%async_computation.5 | async-start | bytes 8912896 | tf_op jit(solution)/shard_map/all_gather | solution.py:526
  46.3 27.9 %copy-start.5 = (s32[2]{0:T(128)}, s32[2]{0:T(128)S(1)}, u32[]{:S(2)}) copy-start(s32[2]{0:T(128)S(1)} %pad_add_fusion.1.place_ref) | copy-start | bytes 28
  48.7 1.5 collective-permute-start
  51.7 12.4 %collective-permute-start.1 = (f32[32,1024]{1,0:T(8,128)S(1)}, f32[32,1024]{1,0:T(8,128)S(1)}, u32[]{:S(2)}, u32[]{:S(2)}) collective-permute-start(f32[32,1024]{1,0:T(8,128)S(1)} %get-tuple-element.47.refs_1_), channel_id=1, source_target_pairs={{0,16},{8,24},{1,17},{9,25},{2,18},{10,26},{3,19},{11,27},{4,20},{... | collective-permute-start | bytes 393224 | tf_op jit(solution)/shard_map/ppermute | solution.py:519
  55.5 9.9 %collective-permute-start.2 = (f32[32,1024]{1,0:T(8,128)S(1)}, f32[32,1024]{1,0:T(8,128)S(1)}, u32[]{:S(2)}, u32[]{:S(2)}) collective-permute-start(f32[32,1024]{1,0:T(8,128)S(1)} %get-tuple-element.47.refs_1_), channel_id=1, source_target_pairs={{0,32},{8,40},{1,33},{9,41},{2,34},{10,42},{3,35},{11,43},{4,36},{... | collective-permute-start | bytes 393224 | tf_op jit(solution)/shard_map/ppermute | solution.py:519
  57.5 9.2 %collective-permute-start.3 = (f32[32,1024]{1,0:T(8,128)S(1)}, f32[32,1024]{1,0:T(8,128)S(1)}, u32[]{:S(2)}, u32[]{:S(2)}) collective-permute-start(f32[32,1024]{1,0:T(8,128)S(1)} %get-tuple-element.47.refs_1_), channel_id=1, source_target_pairs={{0,48},{8,56},{1,49},{9,57},{2,50},{10,58},{3,51},{11,59},{4,52},{... | collective-permute-start | bytes 393224 | tf_op jit(solution)/shard_map/ppermute | solution.py:519
  59.6 7.4 %collective-permute-start.4 = (f32[32,1024]{1,0:T(8,128)S(1)}, f32[32,1024]{1,0:T(8,128)S(1)}, u32[]{:S(2)}, u32[]{:S(2)}) collective-permute-start(f32[32,1024]{1,0:T(8,128)S(1)} %get-tuple-element.47.refs_1_), channel_id=1, source_target_pairs={{0,64},{8,72},{1,65},{9,73},{2,66},{10,74},{3,67},{11,75},{4,68},{... | collective-permute-start | bytes 393224 | tf_op jit(solution)/shard_map/ppermute | solution.py:519
  62.8 5.1 %collective-permute-start.5 = (f32[32,1024]{1,0:T(8,128)S(1)}, f32[32,1024]{1,0:T(8,128)S(1)}, u32[]{:S(2)}, u32[]{:S(2)}) collective-permute-start(f32[32,1024]{1,0:T(8,128)S(1)} %get-tuple-element.47.refs_1_), channel_id=1, source_target_pairs={{0,80},{8,88},{1,81},{9,89},{2,82},{10,90},{3,83},{11,91},{4,84},{... | collective-permute-start | bytes 393224 | tf_op jit(solution)/shard_map/ppermute | solution.py:519
  64.1 6.6 %collective-permute-start.6 = (f32[32,1024]{1,0:T(8,128)S(1)}, f32[32,1024]{1,0:T(8,128)S(1)}, u32[]{:S(2)}, u32[]{:S(2)}) collective-permute-start(f32[32,1024]{1,0:T(8,128)S(1)} %get-tuple-element.47.refs_1_), channel_id=1, source_target_pairs={{0,96},{8,104},{1,97},{9,105},{2,98},{10,106},{3,99},{11,107},{4,1... | collective-permute-start | bytes 393224 | tf_op jit(solution)/shard_map/ppermute | solution.py:519
  65.4 7.3 %collective-permute-start.7 = (f32[32,1024]{1,0:T(8,128)S(1)}, f32[32,1024]{1,0:T(8,128)S(1)}, u32[]{:S(2)}, u32[]{:S(2)}) collective-permute-start(f32[32,1024]{1,0:T(8,128)S(1)} %get-tuple-element.47.refs_1_), channel_id=1, source_target_pairs={{0,112},{8,120},{1,113},{9,121},{2,114},{10,122},{3,115},{11,123},... | collective-permute-start | bytes 393224 | tf_op jit(solution)/shard_map/ppermute | solution.py:519
  74.3 16.9 %all-to-all-start.2 = ((f32[16,32,256]{2,1,0:T(8,128)}), f32[16,32,256]{2,1,0:T(8,128)S(1)}, u32[]{:S(2)}, u32[]{:S(2)}) async-start(f32[16,32,256]{2,1,0:T(8,128)} %get-tuple-element.56), calls=%async_computation.2 | async-start | bytes 1048576 | tf_op jit(solution)/shard_map/all_to_all | solution.py:524
  81.6 24.5 %copy-start.2 = (f32[256,2048]{1,0:T(8,128)S(1)}, f32[256,2048]{1,0:T(8,128)}, u32[]{:S(2)}) copy-start(f32[256,2048]{1,0:T(8,128)} %parent_ref.2) | copy-start | bytes 6291460
  91.2 16.4 %collective-permute-start.8 = (f32[16,32,256]{2,1,0:T(8,128)S(1)}, f32[16,32,256]{2,1,0:T(8,128)S(1)}, u32[]{:S(2)}, u32[]{:S(2)}) collective-permute-start(f32[16,32,256]{2,1,0:T(8,128)S(1)} %all-to-all-done.2), channel_id=1, source_target_pairs={{0,48},{8,56},{1,49},{9,57},{2,50},{10,58},{3,51},{11,59},{4,52},{... | collective-permute-start | bytes 1572872 | tf_op jit(solution)/shard_map/ppermute | solution.py:533
  97.3 12.0 %collective-permute-start.9 = (f32[16,32,256]{2,1,0:T(8,128)S(1)}, f32[16,32,256]{2,1,0:T(8,128)}, u32[]{:S(2)}, u32[]{:S(2)}) collective-permute-start(f32[16,32,256]{2,1,0:T(8,128)S(1)} %all-to-all-done.2), channel_id=1, source_target_pairs={{0,96},{8,104},{1,97},{9,105},{2,98},{10,106},{3,99},{11,107},{4,1... | collective-permute-start | bytes 1572872 | tf_op jit(solution)/shard_map/ppermute | solution.py:533
  100.5 31.4 %all-to-all-start.3 = ((f32[16,32,1024]{2,1,0:T(8,128)}), f32[16,32,1024]{2,1,0:T(8,128)}, u32[]{:S(2)}, u32[]{:S(2)}) async-start(f32[16,32,1024]{2,1,0:T(8,128)} %pick.1), calls=%async_computation.3 | async-start | bytes 4194304 | tf_op jit(solution)/shard_map/all_to_all | solution.py:528
  131.8 8.3 %collective-permute-start.10 = (f32[16,32,1024]{2,1,0:T(8,128)}, f32[16,32,1024]{2,1,0:T(8,128)}, u32[]{:S(2)}, u32[]{:S(2)}) collective-permute-start(f32[16,32,1024]{2,1,0:T(8,128)} %all-to-all-done.3.own_ref), channel_id=1, source_target_pairs={{0,8},{8,0},{16,24},{24,16},{32,40},{40,32},{48,56},{56,48},{64,72... | collective-permute-start | bytes 6291464 | tf_op jit(solution)/shard_map/ppermute | solution.py:540
  131.8 33.4 %collective-permute-start.11 = (f32[16,32,256]{2,1,0:T(8,128)S(1)}, f32[16,32,256]{2,1,0:T(8,128)S(1)}, u32[]{:S(2)}, u32[]{:S(2)}) collective-permute-start(f32[16,32,256]{2,1,0:T(8,128)S(1)} %add_add_fusion.1), channel_id=1, source_target_pairs={{0,16},{8,24},{48,64},{56,72},{96,112},{104,120},{1,17},{9,25},{49... | collective-permute-start | bytes 1572872 | tf_op jit(solution)/shard_map/ppermute | solution.py:533
  133.2 32.1 %collective-permute-start.12 = (f32[16,32,256]{2,1,0:T(8,128)S(1)}, f32[16,32,256]{2,1,0:T(8,128)}, u32[]{:S(2)}, u32[]{:S(2)}) collective-permute-start(f32[16,32,256]{2,1,0:T(8,128)S(1)} %add_add_fusion.1), channel_id=1, source_target_pairs={{48,32},{56,40},{96,80},{104,88},{49,33},{57,41},{97,81},{105,89},... | collective-permute-start | bytes 1572872 | tf_op jit(solution)/shard_map/ppermute | solution.py:533
  134.6 60.1 %all-to-all-start.4 = ((f32[8,256,256]{2,1,0:T(8,128)}), f32[8,256,256]{2,1,0:T(8,128)S(1)}, u32[]{:S(2)}, u32[]{:S(2)}) async-start(f32[8,256,256]{2,1,0:T(8,128)} %turn.1), calls=%async_computation.4 | async-start | bytes 4194304 | tf_op jit(solution)/shard_map/all_to_all | solution.py:541
  165.2 0.8 copy-start.8
  167.4 2.0 copy-start.7
  167.4 2.0 collective-permute-start.13
  169.4 0.8 copy-start.9
  194.7 1.3 copy-start.6
Sparse Core Ops, SparseCore 0:
  74.4 116.5 all-gather.1
